TPU v7x, 32 devices: a whole 2x2x4 slice. The times are simulated.
32 devices in a mesh: seg: 4 (over y, x), blk: 8 (over z, core).
Axes of the slice: x: 2, y: 2, z: 4, core: 2. Of those that a mesh axis runs over, the one named last changes fastest.
Arguments:
- guess_a: bfloat16 [4, 8, 2, 256, 256], P('seg', 'blk'), may hold values from -6 to 6
- guess_b: bfloat16 [4, 8, 2, 256, 256], P('seg', 'blk'), may hold values from -6 to 6
- left_env_a: bfloat16 [4, 12, 8, 2, 256, 256], P('seg', None, 'blk')
- right_env_a: bfloat16 [4, 12, 8, 2, 256, 256], P('seg', None, 'blk')
- left_env_b: bfloat16 [4, 12, 8, 2, 256, 256], P('seg', None, 'blk')
- right_env_b: bfloat16 [4, 12, 8, 2, 256, 256], P('seg', None, 'blk')
- channel_mix: float32 [12, 12], replicated, may hold values from -1.75 to 1.75
- term_shift: int32 [12], replicated, may hold values from 0 to 4, as said below
- sector_sizes: int32 [4, 4, 8, 2], P('seg', None, 'blk'), may hold values from 32 to 256, as said below
- edge_state: bfloat16 [8, 2, 256, 256], P('blk'), may hold values from -6 to 6
Outputs:
- ground_a: float32 [4, 8, 2, 256, 256], P('seg', 'blk')
- ground_b: float32 [4, 8, 2, 256, 256], P('seg', 'blk')
- energies: float32 [4, 2], P('seg')
- boundary_env: bfloat16 [4, 12, 8, 2, 256, 256], P('seg', None, 'blk')
Inputs may be any that keep to these rules, and one draw needn't show every extreme that they name: `sector_sizes`: each of the four tables of every segment reaches 256 and 32. `term_shift`: every code 0 to 4 appears at least once.
All inputs are finite; a program needn't handle non-finite values.
Results may differ from a plain program's by a relative error of at most 0.0088.
Values may be sent and summed in bfloat16 or wider, within the bound.
No kernel may reach another device: no remote copies, remote signals or barrier semaphores. Data moves between devices by JAX's collectives and lax.ppermute only.
A program may use at most 128 MiB of HBM per device.

v0:
```python
import jax
import jax.numpy as jnp
from jax import lax
from jax.sharding import PartitionSpec as P


def padded_2(block, sides, width):
    for axis, dim in sides:
        count = lax.axis_size(axis)
        forward = [(i, i + 1) for i in range(count - 1)]
        backward = [(target, source) for source, target in forward]
        low = lax.ppermute(
            lax.slice_in_dim(block, block.shape[dim] - width, None, axis=dim), axis, forward
        )
        high = lax.ppermute(lax.slice_in_dim(block, 0, width, axis=dim), axis, backward)
        block = jnp.concatenate([low, block, high], axis=dim)
    return block


def passed_along(block, axis, distance):
    devices = range(lax.axis_size(axis))
    route = [(i - distance, i) for i in devices if i - distance in devices]
    return lax.ppermute(block, axis, route)


def block_mask(row_sizes, col_sizes, block):
    places = jnp.arange(block, dtype=jnp.int32)
    rows_live = places[None, None, :] < row_sizes[:, :, None]
    cols_live = places[None, None, :] < col_sizes[:, :, None]
    return (rows_live[:, :, :, None] & cols_live[:, :, None, :]).astype(jnp.float32)


def apply_local(vectors, lefts, rights, term_shift, masks):
    up_count = vectors[0].shape[0]
    down_count = vectors[0].shape[1]
    stacked = jnp.stack(vectors)
    rims = padded_2(stacked, (("blk", 1),), 1)
    padded = jnp.pad(rims, ((0, 0), (0, 0), (1, 1), (0, 0), (0, 0)))
    starts = ((1, 1), (0, 1), (2, 1), (1, 0), (1, 2))
    shifted = jnp.stack(
        [
            padded[:, up_start : up_start + up_count, down_start : down_start + down_count]
            for up_start, down_start in starts
        ]
    )
    sources = jnp.take(shifted[:, 0], term_shift, axis=0)
    half_step = jnp.einsum(
        "wudij,wudjk->wudik", lefts[0], sources, preferred_element_type=jnp.float32
    ).astype(jnp.bfloat16)
    summed = jnp.einsum(
        "wudik,wudlk->udil", half_step, rights[0], preferred_element_type=jnp.float32
    )
    outputs = [summed * masks[0]]
    return outputs


def lanczos_bonds(guesses, lefts, rights, term_shift, masks):
    starts = [guesses[0].astype(jnp.float32) * masks[0]]
    norm_sq = lax.psum(jnp.stack([jnp.sum(vector * vector) for vector in starts]), "blk")
    norms = jnp.sqrt(norm_sq)
    basis_zero = [starts[0] / norms[0]]
    image_zero = apply_local(
        [vector.astype(jnp.bfloat16) for vector in basis_zero], lefts, rights, term_shift, masks
    )
    correlations = jnp.stack([jnp.sum(basis_zero[0] * image_zero[0])])
    alpha_zero = lax.psum(correlations, "blk")
    residuals = [image_zero[0] - alpha_zero[0] * basis_zero[0]]
    beta_sq = lax.psum(jnp.stack([jnp.sum(vector * vector) for vector in residuals]), "blk")
    beta_value = jnp.sqrt(beta_sq)
    basis_one = [residuals[0] / beta_value[0]]
    image_one = apply_local(
        [vector.astype(jnp.bfloat16) for vector in basis_one], lefts, rights, term_shift, masks
    )
    alpha_one = lax.psum(jnp.stack([jnp.sum(basis_one[0] * image_one[0])]), "blk")
    spread = 0.5 * (alpha_zero - alpha_one)
    energies = 0.5 * (alpha_zero + alpha_one) - jnp.sqrt(spread * spread + beta_value * beta_value)
    weight_one = energies - alpha_zero
    length = jnp.sqrt(beta_value * beta_value + weight_one * weight_one)
    grounds = [
        norms[0] * (beta_value[0] * basis_zero[0] + weight_one[0] * basis_one[0]) / length[0]
    ]
    return (grounds, energies)


def grow_env(state, env, channel_mix, factor):
    channels = env.shape[0]

    def one_channel(channel):
        env_w = lax.dynamic_index_in_dim(env, channel, 0, keepdims=False)
        half_step = jnp.einsum(
            "udij,udjk->udik", env_w, state, preferred_element_type=jnp.float32
        ).astype(jnp.bfloat16)
        return jnp.einsum("udji,udjk->udik", state, half_step, preferred_element_type=jnp.float32)

    blocks = lax.map(one_channel, jnp.arange(channels, dtype=jnp.int32))
    return (
        jnp.einsum("vw,wudik->vudik", channel_mix, blocks, precision=lax.Precision.HIGHEST) * factor
    )


def local(
    guess_a,
    guess_b,
    left_env_a,
    right_env_a,
    left_env_b,
    right_env_b,
    channel_mix,
    term_shift,
    sector_sizes,
    edge_state,
):
    block = guess_a.shape[-1]
    local_sizes = sector_sizes[0]
    mask_a = block_mask(local_sizes[0], local_sizes[1], block)
    mask_b = block_mask(local_sizes[2], local_sizes[3], block)
    grounds_a, energy_a = lanczos_bonds(
        [guess_a[0]], [left_env_a[0]], [right_env_a[0]], term_shift, [mask_a]
    )
    grounds_b, energy_b = lanczos_bonds(
        [guess_b[0]], [left_env_b[0]], [right_env_b[0]], term_shift, [mask_b]
    )
    ground_a = grounds_a[0]
    ground_b = grounds_b[0]
    energies = jnp.concatenate([energy_a, energy_b])
    env_a = grow_env(ground_a.astype(jnp.bfloat16), left_env_a[0], channel_mix, 1.0 / block).astype(
        jnp.bfloat16
    )
    state_b = ground_b.astype(jnp.bfloat16)
    seg_place = lax.axis_index("seg")
    last_seg = lax.axis_size("seg") - 1
    from_left = passed_along(env_a, "seg", 1)
    made = grow_env(state_b, from_left, channel_mix, 1.0 / block).astype(jnp.bfloat16)
    returned = passed_along(made, "seg", -1)
    own_edge = lax.cond(
        seg_place == last_seg,
        lambda: grow_env(edge_state, env_a, channel_mix, 1.0 / block).astype(jnp.bfloat16),
        lambda: jnp.zeros(env_a.shape, jnp.bfloat16),
    )
    boundary = jnp.where(seg_place == last_seg, own_edge, returned)
    return (ground_a[None], ground_b[None], energies[None], boundary[None])


def solution(mesh):
    placed = (
        P("seg", "blk", None, None, None),
        P("seg", "blk", None, None, None),
        P("seg", None, "blk", None, None, None),
        P("seg", None, "blk", None, None, None),
        P("seg", None, "blk", None, None, None),
        P("seg", None, "blk", None, None, None),
        P(),
        P(),
        P("seg", None, "blk", None),
        P("blk", None, None, None),
    )
    return jax.shard_map(
        local,
        mesh=mesh,
        in_specs=placed,
        out_specs=(
            P("seg", "blk", None, None, None),
            P("seg", "blk", None, None, None),
            P("seg", None),
            P("seg", None, "blk", None, None, None),
        ),
        check_vma=False,
    )
```

profile of v0, /device:TPU:6, one launch (start us, length us, event | category | flops | bytes accessed | tf_op | source)
XLA Modules:
  0.0 514.0 jit_solution(12715492648210931925)
XLA Ops:
  5.5 17.2 %all-reduce.7 = (f32[1]{0:T(128)}, f32[1]{0:T(128)}) all-reduce(f32[1]{0:T(128)} %bitcast.21, f32[1]{0:T(128)} %bitcast.60), channel_id=1, replica_groups=mesh['seg'=4,'blk'=8] {'blk'}, use_global_device_ids=true, to_apply=%region_1.0 | all-reduce | flops 2 | bytes 16 | tf_op jit(solution)/shard_map/psum | solution.py:59
  31.2 3.0 collective-permute-start
  47.9 3.8 gather_fusion.2
  51.7 3.8 gather_fusion
  55.5 6.2 %fusion.36 = (bf16[12,2,256,256]{3,2,1,0:T(8,128)(2,1)}, bf16[12,2,256,256]{3,2,1,0:T(8,128)(2,1)}) fusion(bf16[12,2,256,256]{3,2,1,0:T(8,128)(2,1)} %gather_fusion.2, pred[12]{0:T(512)(128)(4,1)S(1)} %compare_and_fusion, bf16[12,2,256,256]{3,2,1,0:T(8,128)(2,1)} %gather_fusion), kind=kLoop, calls=%fused_computation.41 | loop fusion | flops 3145728 | bytes 12582924 | tf_op jit(solution)/shard_map/reshape.60
  61.7 6.1 %multiply_reduce_fusion.3 = (f32[]{:T(128)}, f32[2,256,256]{2,1,0:T(8,128)}) fusion(f32[]{:T(128)} %bitcast.22, bf16[1,1,2,256,256]{4,3,2,1,0:T(8,128)(2,1)S(1)} %copy-done.4, pred[2,256]{1,0:T(4,128)(4,1)S(1)} %get-tuple-element.186, pred[2,256]{1,0:T(4,128)(4,1)S(1)} %get-tuple-element.187, bf16[12,2,256,256]{3,2,1,0:T(8,128)(2,1)} %get-tuple-element.179, ...), kind=kOutput, calls=%fused_computation.119 | convolution fusion | flops 1613103104 | bytes 10224648 | tf_op jit(solution)/shard_map/wudik,wudlk->udil/dot_general | solution.py:50
  67.8 7.0 %multiply_reduce_fusion.1 = (f32[]{:T(128)}, f32[2,256,256]{2,1,0:T(8,128)}) fusion(f32[]{:T(128)} %bitcast.61, bf16[1,1,2,256,256]{4,3,2,1,0:T(8,128)(2,1)} %param.21, pred[2,256]{1,0:T(4,128)(4,1)S(1)} %get-tuple-element.184, pred[2,256]{1,0:T(4,128)(4,1)S(1)} %get-tuple-element.185, bf16[12,2,256,256]{3,2,1,0:T(8,128)(2,1)} %get-tuple-element.178, ...), kind=kOutput, calls=%fused_computation.115 | convolution fusion | flops 1613103104 | bytes 10224648 | tf_op jit(solution)/shard_map/wudik,wudlk->udil/dot_general | solution.py:50
  74.8 16.2 %all-reduce.6 = (f32[1]{0:T(128)}, f32[1]{0:T(128)}) all-reduce(f32[1]{0:T(128)} %bitcast.38, f32[1]{0:T(128)} %bitcast.77), channel_id=1, replica_groups=mesh['seg'=4,'blk'=8] {'blk'}, use_global_device_ids=true, to_apply=%region_3.5 | all-reduce | flops 2 | bytes 16 | tf_op jit(solution)/shard_map/psum | solution.py:66
  96.2 14.3 %all-reduce.5 = (f32[1]{0:T(128)}, f32[1]{0:T(128)}) all-reduce(f32[1]{0:T(128)} %bitcast.40, f32[1]{0:T(128)} %bitcast.79), channel_id=1, replica_groups=mesh['seg'=4,'blk'=8] {'blk'}, use_global_device_ids=true, to_apply=%region_5.7 | all-reduce | flops 2 | bytes 16 | tf_op jit(solution)/shard_map/psum | solution.py:68
  119.6 3.7 collective-permute-start.2
  129.3 3.8 gather_fusion.3
  139.1 3.8 gather_fusion.1
  143.0 6.2 %fusion.33 = (bf16[12,2,256,256]{3,2,1,0:T(8,128)(2,1)}, bf16[12,2,256,256]{3,2,1,0:T(8,128)(2,1)}) fusion(bf16[12,2,256,256]{3,2,1,0:T(8,128)(2,1)} %gather_fusion.3, pred[12]{0:T(512)(128)(4,1)S(1)} %compare_and_fusion, bf16[12,2,256,256]{3,2,1,0:T(8,128)(2,1)} %gather_fusion.1), kind=kLoop, calls=%fused_computation.37 | loop fusion | flops 3145728 | bytes 12582924 | tf_op jit(solution)/shard_map/reshape.67
  149.1 5.4 %fusion.186 = f32[]{:T(128)} fusion(f32[2,256,256]{2,1,0:T(8,128)} %copy-done.8, bf16[12,2,256,256]{3,2,1,0:T(8,128)(2,1)} %get-tuple-element.177, pred[2,256]{1,0:T(4,128)(4,1)S(1)} %get-tuple-element.186, pred[2,256]{1,0:T(4,128)(4,1)S(1)} %get-tuple-element.187, bf16[1,12,1,2,256,256]{5,4,3,2,1,0:T(8,128)(2,1)S(1)} %copy-done, ...), kind=kOutput, calls=%fused_computation.98 | convolution fusion | flops 1612709888 | bytes 9962500 | tf_op jit(solution)/shard_map/wudik,wudlk->udil/dot_general | solution.py:50
  154.5 6.4 %fusion.195 = f32[]{:T(128)} fusion(f32[2,256,256]{2,1,0:T(8,128)} %copy-done.6, bf16[12,2,256,256]{3,2,1,0:T(8,128)(2,1)} %get-tuple-element.176, pred[2,256]{1,0:T(4,128)(4,1)S(1)} %get-tuple-element.184, pred[2,256]{1,0:T(4,128)(4,1)S(1)} %get-tuple-element.185, bf16[1,12,1,2,256,256]{5,4,3,2,1,0:T(8,128)(2,1)} %param.25, ...), kind=kOutput, calls=%fused_computation.99 | convolution fusion | flops 1612709888 | bytes 9962500 | tf_op jit(solution)/shard_map/wudik,wudlk->udil/dot_general | solution.py:50
  160.9 15.7 %all-reduce.4 = (f32[1]{0:T(128)}, f32[1]{0:T(128)}) all-reduce(f32[1]{0:T(128)} %bitcast.55, f32[1]{0:T(128)} %bitcast.94), channel_id=1, replica_groups=mesh['seg'=4,'blk'=8] {'blk'}, use_global_device_ids=true, to_apply=%region_7.9 | all-reduce | flops 2 | bytes 16 | tf_op jit(solution)/shard_map/psum | solution.py:74
  181.1 3.4 broadcast.244.clone
  184.5 56.4 %while.30 = (s32[]{:T(128)}, f32[12,1,2,256,256]{3,4,2,1,0:T(8,128)}, s32[12]{0:T(128)S(1)}, bf16[12,1,2,256,256]{4,3,2,1,0:T(8,128)(2,1)}, bf16[1,2,256,256]{3,...) while((s32[]{:T(128)}, f32[12,1,2,256,256]{3,4,2,1,0:T(8,128)}, s32[12]{0:T(128)S(1)}, ...), condition=%wide.region_17.19_spmd, body=%wide.region_16.18_spmd.sunk | while | flops 134348800 | bytes 1310867 | solution.py:95
  240.9 9.6 %copy.30 = f32[12,2,256,256]{3,0,2,1:T(8,128)} copy(f32[12,2,256,256]{2,3,1,0:T(8,128)} %bitcast.385) | data formatting | bytes 12582912 | tf_op jit(solution)/shard_map/reshape.72
  250.5 10.4 %fusion.29 = bf16[12,1,2,256,256]{4,0,3,2,1:T(8,128)(2,1)S(1)} fusion(f32[12,2,256,256]{3,0,2,1:T(8,128)} %copy.30, f32[12,12]{1,0:T(8,128)S(1)} %copy-done.10), kind=kOutput, calls=%fused_computation.32 | convolution fusion | flops 229638144 | bytes 9437760 | tf_op jit(solution)/shard_map/vw,wudik->vudik/dot_general | solution.py:97
  269.7 65.2 %collective-permute-done.8 = bf16[12,1,2,256,256]{4,3,2,1,0:T(8,128)(2,1)} collective-permute-done((bf16[12,1,2,256,256]{4,3,2,1,0:T(8,128)(2,1)}, bf16[12,1,2,256,256]{4,3,2,1,0:T(8,128)(2,1)}, u32[]{:S(2)}, u32[]{:S(2)}) %collective-permute-start.8) | collective-permute-done | bytes 3145760 | tf_op jit(solution)/shard_map/ppermute | solution.py:23
  334.8 3.4 broadcast.244
  338.3 56.4 %while.31 = (s32[]{:T(128)}, f32[12,1,2,256,256]{3,4,2,1,0:T(8,128)}, s32[12]{0:T(128)S(1)}, bf16[12,1,2,256,256]{4,3,2,1,0:T(8,128)(2,1)}, bf16[1,2,256,256]{3,...) while((s32[]{:T(128)}, f32[12,1,2,256,256]{3,4,2,1,0:T(8,128)}, s32[12]{0:T(128)S(1)}, ...), condition=%wide.region_23.25_spmd, body=%wide.region_22.24_spmd.sunk | while | flops 134348800 | bytes 1310867 | solution.py:95
  394.6 9.6 %copy.33 = f32[12,2,256,256]{3,0,2,1:T(8,128)} copy(f32[12,2,256,256]{2,3,1,0:T(8,128)} %bitcast.384) | data formatting | bytes 12582912 | tf_op jit(solution)/shard_map/reshape.74
  404.3 10.4 %fusion.30 = bf16[12,1,2,256,256]{4,0,3,2,1:T(8,128)(2,1)S(1)} fusion(f32[12,2,256,256]{3,0,2,1:T(8,128)} %copy.33, f32[12,12]{1,0:T(8,128)S(1)} %copy-done.10), kind=kOutput, calls=%fused_computation.33 | convolution fusion | flops 229638144 | bytes 9437760 | tf_op jit(solution)/shard_map/vw,wudik->vudik/dot_general | solution.py:97
  417.6 5.0 collective-permute-start.9
  422.6 86.8 %conditional.1 = (bf16[12,1,2,256,256]{4,3,2,1,0:T(8,128)(2,1)}) conditional(s32[]{:T(128)} %convert_element_type.177, () %tuple.27, (bf16[12,1,2,256,256]{4,0,3,2,1:T(8,128)(2,1)}, bf16[1,2,256,256]{3,2,1,0:T(8,128)(2,1)S(1)}, f32[12,12]{1,0:T(8,128)S(1)}) %tuple.92), branch_computations={%region_18.20_spmd, %region_19.23_spmd} | conditional | flops 363986944 | bytes 35914580 | solution.py:135
  422.6 4.9 copy.31
  427.5 58.9 %while.29 = (s32[]{:T(128)}, f32[12,1,2,256,256]{3,4,2,1,0:T(8,128)}, s32[12]{0:T(128)S(1)}, bf16[12,1,2,256,256]{4,3,2,1,0:T(8,128)(2,1)}, bf16[1,2,256,256]{3,...) while((s32[]{:T(128)}, f32[12,1,2,256,256]{3,4,2,1,0:T(8,128)}, s32[12]{0:T(128)S(1)}, ...), condition=%wide.region_21.22_spmd, body=%wide.region_20.21_spmd.sunk | while | flops 134348800 | bytes 1310867 | solution.py:95
  486.4 9.6 %copy.25 = f32[12,2,256,256]{3,0,2,1:T(8,128)} copy(f32[12,2,256,256]{2,3,1,0:T(8,128)} %bitcast.388) | data formatting | bytes 12582912 | tf_op jit(solution)/shard_map/reshape.26
  496.1 10.4 %fusion.18 = bf16[12,1,2,256,256]{4,0,3,2,1:T(8,128)(2,1)S(1)} fusion(f32[12,2,256,256]{3,0,2,1:T(8,128)} %copy.25, f32[12,12]{1,0:T(8,128)S(1)} %get-tuple-element.85), kind=kOutput, calls=%fused_computation.19 | convolution fusion | flops 229638144 | bytes 9437760 | tf_op jit(solution)/shard_map/cond/branch_1_fun/vw,wudik->vudik/dot_general | solution.py:97
  509.9 4.0 select_bitcast_fusion
  (156 shorter events, 163.3 us)
Async XLA Ops:
  0.6 61.1 %copy-start = (bf16[1,12,1,2,256,256]{5,4,3,2,1,0:T(8,128)(2,1)S(1)}, bf16[1,12,1,2,256,256]{5,4,3,2,1,0:T(8,128)(2,1)}, u32[]{:S(2)}) copy-start(bf16[1,12,1,2,256,256]{5,4,3,2,1,0:T(8,128)(2,1)} %param.23) | copy-start | bytes 9437188
  25.3 11.6 %collective-permute-start.4 = (bf16[1,1,2,256,256]{4,3,2,1,0:T(8,128)(2,1)}, bf16[1,1,2,256,256]{4,3,2,1,0:T(8,128)(2,1)}, u32[]{:S(2)}, u32[]{:S(2)}) collective-permute-start(bf16[1,1,2,256,256]{4,3,2,1,0:T(8,128)(2,1)} %get-tuple-element.169), channel_id=1, source_target_pairs={{0,1},{1,2},{2,3},{3,4},{4,5},{5,6},{6,7},{8,9},{9,10},{10,11},{11... | collective-permute-start | bytes 786440 | tf_op jit(solution)/shard_map/ppermute | solution.py:12
  27.3 11.3 %collective-permute-start.5 = (bf16[1,1,2,256,256]{4,3,2,1,0:T(8,128)(2,1)}, bf16[1,1,2,256,256]{4,3,2,1,0:T(8,128)(2,1)}, u32[]{:S(2)}, u32[]{:S(2)}) collective-permute-start(bf16[1,1,2,256,256]{4,3,2,1,0:T(8,128)(2,1)} %get-tuple-element.169), channel_id=1, source_target_pairs={{1,0},{2,1},{3,2},{4,3},{5,4},{6,5},{7,6},{9,8},{10,9},{11,10},{12... | collective-permute-start | bytes 786440 | tf_op jit(solution)/shard_map/ppermute | solution.py:15
  31.2 11.7 %collective-permute-start = (bf16[1,1,2,256,256]{4,3,2,1,0:T(8,128)(2,1)}, bf16[1,1,2,256,256]{4,3,2,1,0:T(8,128)(2,1)S(1)}, u32[]{:S(2)}, u32[]{:S(2)}) collective-permute-start(bf16[1,1,2,256,256]{4,3,2,1,0:T(8,128)(2,1)} %get-tuple-element.171), channel_id=1, source_target_pairs={{0,1},{1,2},{2,3},{3,4},{4,5},{5,6},{6,7},{8,9},{9,10},{10,11},{11... | collective-permute-start | bytes 786440 | tf_op jit(solution)/shard_map/ppermute | solution.py:12
  34.2 9.4 %collective-permute-start.1 = (bf16[1,1,2,256,256]{4,3,2,1,0:T(8,128)(2,1)}, bf16[1,1,2,256,256]{4,3,2,1,0:T(8,128)(2,1)}, u32[]{:S(2)}, u32[]{:S(2)}) collective-permute-start(bf16[1,1,2,256,256]{4,3,2,1,0:T(8,128)(2,1)} %get-tuple-element.171), channel_id=1, source_target_pairs={{1,0},{2,1},{3,2},{4,3},{5,4},{6,5},{7,6},{9,8},{10,9},{11,10},{12... | collective-permute-start | bytes 786440 | tf_op jit(solution)/shard_map/ppermute | solution.py:15
  55.5 6.2 %copy-start.4 = (bf16[1,1,2,256,256]{4,3,2,1,0:T(8,128)(2,1)S(1)}, bf16[1,1,2,256,256]{4,3,2,1,0:T(8,128)(2,1)}, u32[]{:S(2)}) copy-start(bf16[1,1,2,256,256]{4,3,2,1,0:T(8,128)(2,1)} %param.20) | copy-start | bytes 786436
  113.1 11.7 %copy-start.6 = (f32[2,256,256]{2,1,0:T(8,128)}, f32[2,256,256]{2,1,0:T(8,128)S(1)}, u32[]{:S(2)}) copy-start(f32[2,256,256]{2,1,0:T(8,128)S(1)} %get-tuple-element.165) | copy-start | bytes 1572868
  113.1 13.1 %collective-permute-start.6 = (bf16[1,1,2,256,256]{4,3,2,1,0:T(8,128)(2,1)S(1)}, bf16[1,1,2,256,256]{4,3,2,1,0:T(8,128)(2,1)S(1)}, u32[]{:S(2)}, u32[]{:S(2)}) collective-permute-start(bf16[1,1,2,256,256]{4,3,2,1,0:T(8,128)(2,1)S(1)} %get-tuple-element.164), channel_id=1, source_target_pairs={{0,1},{1,2},{2,3},{3,4},{4,5},{5,6},{6,7},{8,9},{9,10},{10,11},{11... | collective-permute-start | bytes 786440 | tf_op jit(solution)/shard_map/ppermute | solution.py:12
  115.0 12.0 %collective-permute-start.7 = (bf16[1,1,2,256,256]{4,3,2,1,0:T(8,128)(2,1)S(1)}, bf16[1,1,2,256,256]{4,3,2,1,0:T(8,128)(2,1)S(1)}, u32[]{:S(2)}, u32[]{:S(2)}) collective-permute-start(bf16[1,1,2,256,256]{4,3,2,1,0:T(8,128)(2,1)S(1)} %get-tuple-element.164), channel_id=1, source_target_pairs={{1,0},{2,1},{3,2},{4,3},{5,4},{6,5},{7,6},{9,8},{10,9},{11,10},{12... | collective-permute-start | bytes 786440 | tf_op jit(solution)/shard_map/ppermute | solution.py:15
  119.6 5.9 %copy-start.8 = (f32[2,256,256]{2,1,0:T(8,128)}, f32[2,256,256]{2,1,0:T(8,128)S(1)}, u32[]{:S(2)}) copy-start(f32[2,256,256]{2,1,0:T(8,128)S(1)} %get-tuple-element.167) | copy-start | bytes 1572868
  119.6 13.5 %collective-permute-start.2 = (bf16[1,1,2,256,256]{4,3,2,1,0:T(8,128)(2,1)}, bf16[1,1,2,256,256]{4,3,2,1,0:T(8,128)(2,1)}, u32[]{:S(2)}, u32[]{:S(2)}) collective-permute-start(bf16[1,1,2,256,256]{4,3,2,1,0:T(8,128)(2,1)} %get-tuple-element.166), channel_id=1, source_target_pairs={{0,1},{1,2},{2,3},{3,4},{4,5},{5,6},{6,7},{8,9},{9,10},{10,11},{11... | collective-permute-start | bytes 786440 | tf_op jit(solution)/shard_map/ppermute | solution.py:12
  123.3 11.5 %collective-permute-start.3 = (bf16[1,1,2,256,256]{4,3,2,1,0:T(8,128)(2,1)}, bf16[1,1,2,256,256]{4,3,2,1,0:T(8,128)(2,1)}, u32[]{:S(2)}, u32[]{:S(2)}) collective-permute-start(bf16[1,1,2,256,256]{4,3,2,1,0:T(8,128)(2,1)} %get-tuple-element.166), channel_id=1, source_target_pairs={{1,0},{2,1},{3,2},{4,3},{5,4},{6,5},{7,6},{9,8},{10,9},{11,10},{12... | collective-permute-start | bytes 786440 | tf_op jit(solution)/shard_map/ppermute | solution.py:15
  154.5 25.5 %copy-start.9 = (f32[2,256,256]{2,1,0:T(8,128)S(1)}, f32[2,256,256]{2,1,0:T(8,128)}, u32[]{:S(2)}) copy-start(f32[2,256,256]{2,1,0:T(8,128)} %copy-done.8) | copy-start | bytes 1572868
  240.9 9.6 %copy-start.10 = (f32[12,12]{1,0:T(8,128)S(1)}, f32[12,12]{1,0:T(8,128)}, u32[]{:S(2)}) copy-start(f32[12,12]{1,0:T(8,128)} %param.26) | copy-start | bytes 1732
  261.0 3.0 copy-start.2
  261.0 7.6 %copy-start.5 = (bf16[1,1,2,256,256]{4,3,2,1,0:T(8,128)(2,1)S(1)}, bf16[1,1,2,256,256]{4,3,2,1,0:T(8,128)(2,1)}, u32[]{:S(2)}) copy-start(bf16[1,1,2,256,256]{4,3,2,1,0:T(8,128)(2,1)} %param.21) | copy-start | bytes 786436
  261.0 7.6 %copy-start.7 = (f32[2,256,256]{2,1,0:T(8,128)S(1)}, f32[2,256,256]{2,1,0:T(8,128)}, u32[]{:S(2)}) copy-start(f32[2,256,256]{2,1,0:T(8,128)} %copy-done.6) | copy-start | bytes 1572868
  264.0 70.8 %collective-permute-start.8 = (bf16[12,1,2,256,256]{4,3,2,1,0:T(8,128)(2,1)}, bf16[12,1,2,256,256]{4,3,2,1,0:T(8,128)(2,1)}, u32[]{:S(2)}, u32[]{:S(2)}) collective-permute-start(bf16[12,1,2,256,256]{4,3,2,1,0:T(8,128)(2,1)} %copy.32), channel_id=1, source_target_pairs={{0,8},{8,16},{16,24},{1,9},{9,17},{17,25},{2,10},{10,18},{18,26},{... | collective-permute-start | bytes 9437192 | tf_op jit(solution)/shard_map/ppermute | solution.py:23
  414.7 7.9 %copy-start.3 = (bf16[1,2,256,256]{3,2,1,0:T(8,128)(2,1)S(1)}, bf16[1,2,256,256]{3,2,1,0:T(8,128)(2,1)}, u32[]{:S(2)}) copy-start(bf16[1,2,256,256]{3,2,1,0:T(8,128)(2,1)} %param.29) | copy-start | bytes 786436
  417.6 92.4 %collective-permute-start.9 = (bf16[12,1,2,256,256]{4,3,2,1,0:T(8,128)(2,1)}, bf16[12,1,2,256,256]{4,3,2,1,0:T(8,128)(2,1)}, u32[]{:S(2)}, u32[]{:S(2)}) collective-permute-start(bf16[12,1,2,256,256]{4,3,2,1,0:T(8,128)(2,1)} %copy.34), channel_id=1, source_target_pairs={{8,0},{16,8},{24,16},{9,1},{17,9},{25,17},{10,2},{18,10},{26,18},{... | collective-permute-start | bytes 9437192 | tf_op jit(solution)/shard_map/ppermute | solution.py:23
  509.9 4.0 copy-start.1
where the time goes:
time: 518 us; the launch traced here: 514 us
  matrix products  134 us (26%)
  local copies, waits for them, and re-layouts  104 us (20%)
  loops' own time  71.6 us (14%)
  waiting for transfers between devices  65.2 us (13%)
  blocking collectives  63.4 us (12%)
  other arithmetic  42.8 us (8%)
  starting transfers between devices  22.4 us (4%)
  between operations  10.2 us (2%)
    dot_general x36, matrix products, one_channel(): jnp.einsum('udji,udjk->udik', state, half_step, preferred_element_type=jn...  78.1 us
    another operation x3, loops' own time, grow_env(): blocks = lax.map(one_channel, jnp.arange(channels, dtype=jnp.int32))  71.6 us
    ppermute x2, waiting for transfers between devices, passed_along(): return lax.ppermute(block, axis, route)  65.2 us
    another operation x6, local copies, waits for them, and re-layouts  40.7 us
    dot_general x3, matrix products, grow_env(): jnp.einsum('vw,wudik->vudik', channel_mix, blocks, precision=lax.Precisio...  31.3 us
    dot_general x4, matrix products, apply_local(): jnp.einsum('wudik,wudlk->udil', half_step, rights[0], preferred_element_t...  24.9 us
    dynamic_slice x36, local copies, waits for them, and re-layouts, grow_env(): blocks = lax.map(one_channel, jnp.arange(channels, dtype=jnp.int32))  21.9 us
    psum x1, blocking collectives, lanczos_bonds(): lax.psum(jnp.stack([jnp.sum(vector * vector) for vector in starts]), 'blk')  17.2 us
  transfers between devices with their start and end apart: 10, of which 1 were waited for; matrix products, arithmetic and copies ran while one was open for 17% of the time, Pallas kernels for 0%

commit v1 on v0

v1 whole, which is shorter than its diff:
```python
import functools

import jax
import jax.numpy as jnp
from jax import lax
from jax.experimental import pallas as pl
from jax.experimental.pallas import tpu as pltpu
from jax.sharding import PartitionSpec as P

F32 = jnp.float32
BF16 = jnp.bfloat16
VMEM = pl.BlockSpec(memory_space=pltpu.VMEM)
SMEM = pl.BlockSpec(memory_space=pltpu.SMEM)
ANY = pl.BlockSpec(memory_space=pl.ANY)
MIB = 1 << 20
GROUP = 16

(
    SIZE,
    QUOTIENT,
    REST,
    REST_IMAGE,
    START_IMAGE,
    REST_OWN,
    REST_LOW,
    REST_HIGH,
    START_OWN,
    START_LOW,
    START_HIGH,
) = range(11)
BOND_LANES = 64


def call(body, name, ins, outs, scratch, flops, moved, limit=24 * MIB):
    return pl.pallas_call(
        body,
        name=name,
        in_specs=ins,
        out_specs=outs[0],
        out_shape=outs[1],
        scratch_shapes=scratch,
        cost_estimate=pl.CostEstimate(flops=flops, bytes_accessed=moved, transcendentals=0),
        compiler_params=pltpu.CompilerParams(vmem_limit_bytes=limit),
    )


def live(rows, cols, block):
    row = lax.broadcasted_iota(jnp.int32, (block, block), 0)
    col = lax.broadcasted_iota(jnp.int32, (block, block), 1)
    return (row < rows) & (col < cols)


def dot(left, right):
    return jnp.dot(left, right, preferred_element_type=F32)


def dot_by_rows(left, right):
    return lax.dot_general(left, right, (((1,), (1,)), ((), ())), preferred_element_type=F32)


def dot_by_cols(left, right):
    return lax.dot_general(left, right, (((0,), (0,)), ((), ())), preferred_element_type=F32)


def total(array):
    return jnp.sum(jnp.sum(array, axis=0, keepdims=True), axis=1, keepdims=True)


def in_lanes(shape, pairs):
    lane = lax.broadcasted_iota(jnp.int32, shape, 1)
    row = jnp.zeros(shape, F32)
    for place, value in pairs:
        row = jnp.where(lane == place, value, row)
    return row


def masked_starts(sizes, guess_a, guess_b, start_a, start_b):
    downs, block = guess_a.shape[0], guess_a.shape[-1]
    for bond, (guess, start) in enumerate(((guess_a, start_a), (guess_b, start_b))):
        for down in range(downs):
            place = 2 * bond * downs + down
            mask = live(sizes[place], sizes[place + downs], block)
            start[down] = jnp.where(mask, guess[down], jnp.zeros_like(guess[down]))


def mixed_env(mix_high, mix_low, env, mixed):
    channels, downs, block = env.shape[0], env.shape[1], env.shape[-1]
    for down in range(downs):
        for group in range(block // GROUP):
            rows = slice(group * GROUP, (group + 1) * GROUP)
            part = env[:, down, rows, :].reshape(channels * GROUP, block)
            made = dot(mix_high[...], part) + dot(mix_low[...], part)
            mixed[:, down, rows, :] = made.astype(BF16).reshape(channels, GROUP, block)


def fill_sources(sources, own, low, high):
    downs = own.shape[0]
    for down in range(downs):
        sources[0, down] = own[down]
        sources[1, down] = low[down]
        sources[2, down] = high[down]
        zero = jnp.zeros(own.shape[1:], own.dtype)
        sources[3, down] = own[down - 1] if down > 0 else zero
        sources[4, down] = own[down + 1] if down + 1 < downs else zero


def first_image(bond, shift, sizes, left, right, own, low, high, rest, rest_sent, row, parts, sources):
    channels, downs, block = left.shape[0], left.shape[1], left.shape[-1]
    fill_sources(sources, own, low, high)
    parts[...] = jnp.zeros_like(parts)
    for channel in range(channels):
        code = shift[channel]
        kind = jnp.where(code <= 2, code, 0)
        for down in range(downs):
            half = dot(left[channel, down], sources[code, down]).astype(BF16)
            parts[kind, down] += dot_by_rows(half, right[channel, down])
    size = jnp.zeros((1, 1), F32)
    cross = jnp.zeros((1, 1), F32)
    for down in range(downs):
        place = 2 * bond * downs + down
        mask = live(sizes[place], sizes[place + downs], block)
        for kind in range(3):
            parts[kind, down] = jnp.where(mask, parts[kind, down], 0.0)
        image = parts[0, down] + parts[1, down] + parts[2, down]
        start = own[down].astype(F32)
        size += total(start * start)
        cross += total(start * image)
    quotient = jnp.where(size > 0.0, cross / jnp.where(size > 0.0, size, 1.0), 0.0)
    found = {place: jnp.zeros((1, 1), F32) for place in range(REST_OWN, START_HIGH + 1)}
    rest_sq = jnp.zeros((1, 1), F32)
    for down in range(downs):
        start = own[down].astype(F32)
        image = parts[0, down] + parts[1, down] + parts[2, down]
        left_over = image - quotient * start
        rest[down] = left_over
        rest_sent[down] = left_over.astype(BF16)
        rest_sq += total(left_over * left_over)
        for kind in range(3):
            found[REST_OWN + kind] += total(left_over * parts[kind, down])
            found[START_OWN + kind] += total(start * parts[kind, down])
    found[SIZE] = size
    found[QUOTIENT] = quotient
    found[REST] = rest_sq
    offset = bond * BOND_LANES
    row[...] = in_lanes(row.shape, [(offset + place, found[place]) for place in sorted(found)])


def second_image(bond, shift, left, right, own, low, high, start, rest, *refs):
    rows, out, sources = refs[:-2], refs[-2], refs[-1]
    channels, downs = left.shape[0], left.shape[1]
    fill_sources(sources, own, low, high)
    rest_image = jnp.zeros((1, 1), F32)
    start_image = jnp.zeros((1, 1), F32)
    for down in range(downs):
        image = jnp.zeros(left.shape[2:], F32)
        for channel in range(channels):
            half = dot(left[channel, down], sources[shift[channel], down]).astype(BF16)
            image = image + dot_by_rows(half, right[channel, down])
        rest_image += total(rest[down] * image)
        start_image += total(start[down].astype(F32) * image)
    offset = bond * BOND_LANES
    shape = (1, out.shape[1])
    row = in_lanes(
        shape, [(offset + REST_IMAGE, rest_image), (offset + START_IMAGE, start_image)]
    )
    for other in rows:
        row = row + other[0:1, :]
    out[...] = jnp.broadcast_to(row, out.shape)


def ritz(rows, bond):
    ups = rows.shape[0]

    def column(array, place):
        at = bond * BOND_LANES + place
        return array[:, at : at + 1]

    size = column(rows, SIZE)
    quotient = column(rows, QUOTIENT)
    norm_sq = total(size)
    alpha_zero = total(size * quotient) / norm_sq
    off = quotient - alpha_zero
    off_low = column(pltpu.roll(rows, 1, 0), QUOTIENT) - alpha_zero
    off_high = column(pltpu.roll(rows, ups - 1, 0), QUOTIENT) - alpha_zero
    residual_sq = total(column(rows, REST) + size * off * off)
    crossed = column(rows, REST_IMAGE) + off * column(rows, START_IMAGE)
    for kind, factor in enumerate((off, off_low, off_high)):
        crossed += factor * (column(rows, REST_OWN + kind) + off * column(rows, START_OWN + kind))
    alpha_one = total(crossed) / residual_sq
    beta_sq = residual_sq / norm_sq
    beta = jnp.sqrt(beta_sq)
    spread = 0.5 * (alpha_zero - alpha_one)
    energy = 0.5 * (alpha_zero + alpha_one) - jnp.sqrt(spread * spread + beta_sq)
    weight_one = energy - alpha_zero
    length = jnp.sqrt(beta_sq + weight_one * weight_one)
    of_rest = weight_one / (beta * length)
    of_start = beta / length + of_rest * off
    return energy, of_start, of_rest


def own_row(column, place):
    rows = lax.broadcasted_iota(jnp.int32, column.shape, 0)
    return total(jnp.where(rows == place, column, 0.0))


def finish(
    factor,
    ups,
    place,
    numbers,
    start_a,
    rest_a,
    start_b,
    rest_b,
    start_next,
    rest_next,
    edge,
    env,
    ground_a,
    ground_b,
    energies,
    boundary,
    made,
    sems,
):
    channels, downs = env.shape[0], env.shape[1]
    segments = numbers.shape[0] // ups
    seg, blk = place[0], place[1]
    here = numbers[pl.ds(pl.multiple_of(seg * ups, ups), ups), :]
    after = jnp.minimum(seg + 1, segments - 1)
    there = numbers[pl.ds(pl.multiple_of(after * ups, ups), ups), :]
    energy_a, a_start, a_rest = ritz(here, 0)
    energy_b, b_start, b_rest = ritz(here, 1)
    energy_next, next_start, next_rest = ritz(there, 1)
    del energy_next
    a_start, b_start, next_start = (own_row(x, blk) for x in (a_start, b_start, next_start))
    lane = lax.broadcasted_iota(jnp.int32, energies.shape, 1)
    energies[...] = jnp.where(lane == 0, energy_a, energy_b)
    last = seg == segments - 1
    products = []
    for down in range(downs):
        found_a = a_start * start_a[down].astype(F32) + a_rest * rest_a[down]
        ground_a[down] = found_a
        ground_b[down] = b_start * start_b[down].astype(F32) + b_rest * rest_b[down]
        found_next = next_start * start_next[down].astype(F32) + next_rest * rest_next[down].astype(F32)
        state = jnp.where(last, edge[down], found_next.astype(BF16))
        products.append((dot(found_a.astype(BF16), state) * factor).astype(BF16))
    copies = []
    for channel in range(channels):
        for down in range(downs):
            half = dot(env[channel, down], products[down]).astype(BF16)
            made[channel, down] = dot_by_cols(products[down], half).astype(BF16)
        copy = pltpu.make_async_copy(made.at[channel], boundary.at[channel], sems.at[channel])
        copy.start()
        copies.append(copy)
    for copy in copies:
        copy.wait()


def passed_along(block, axis, distance):
    devices = range(lax.axis_size(axis))
    route = [(i - distance, i) for i in devices if i - distance in devices]
    return lax.ppermute(block, axis, route)


def local(
    guess_a,
    guess_b,
    left_env_a,
    right_env_a,
    left_env_b,
    right_env_b,
    channel_mix,
    term_shift,
    sector_sizes,
    edge_state,
):
    block = guess_a.shape[-1]
    downs = guess_a.shape[2]
    channels = left_env_a.shape[1]
    ups = lax.axis_size("blk")
    segments = lax.axis_size("seg")
    devices = ups * segments
    pair = (downs, block, block)
    env_shape = (channels, downs, block, block)
    lefts = [left_env_a.reshape(env_shape), left_env_b.reshape(env_shape)]
    rights = [right_env_a.reshape(env_shape), right_env_b.reshape(env_shape)]
    sizes = sector_sizes.reshape(-1)
    bits = 2 * downs * block * block
    env_bytes = channels * bits
    apply_flops = 4 * channels * downs * block**3
    state16 = jax.ShapeDtypeStruct(pair, BF16)
    state32 = jax.ShapeDtypeStruct(pair, F32)

    starts = call(
        masked_starts,
        "masked_starts",
        [SMEM, VMEM, VMEM],
        ((VMEM, VMEM), (state16, state16)),
        [],
        4 * downs * block * block,
        4 * bits,
    )(sizes, guess_a.reshape(pair), guess_b.reshape(pair))
    lows = [passed_along(start, "blk", 1) for start in starts]
    highs = [passed_along(start, "blk", -1) for start in starts]
    start_next = passed_along(starts[1], "seg", -1)

    squared = jnp.dot(channel_mix, channel_mix, precision=lax.Precision.HIGHEST)
    spread = (squared[:, None, :, None] * jnp.eye(GROUP, dtype=F32)[None, :, None, :]).reshape(
        channels * GROUP, channels * GROUP
    )
    mix_high = spread.astype(BF16)
    mix_low = (spread - mix_high.astype(F32)).astype(BF16)
    env = call(
        mixed_env,
        "mixed_env",
        [VMEM] * 3,
        (VMEM, jax.ShapeDtypeStruct(env_shape, BF16)),
        [],
        4 * channels * channels * GROUP * downs * block * block,
        2 * env_bytes,
    )(mix_high, mix_low, lefts[0])

    rests, rests_sent, rows = [], [], []
    for bond in range(2):
        rest, rest_sent, row = call(
            functools.partial(first_image, bond),
            f"first_image_{bond}",
            [SMEM, SMEM] + [VMEM] * 5,
            ((VMEM,) * 3, (state32, state16, jax.ShapeDtypeStruct((8, 128), F32))),
            [pltpu.VMEM((3,) + pair, F32), pltpu.VMEM((5,) + pair, BF16)],
            apply_flops,
            2 * env_bytes,
        )(term_shift, sizes, lefts[bond], rights[bond], starts[bond], lows[bond], highs[bond])
        rests.append(rest)
        rests_sent.append(rest_sent)
        rows.append(row)
    rest_lows = [passed_along(rest, "blk", 1) for rest in rests_sent]
    rest_highs = [passed_along(rest, "blk", -1) for rest in rests_sent]
    rest_next = passed_along(rests_sent[1], "seg", -1)
    for bond in range(2):
        rows_in = rows if bond == 1 else []
        height = devices if bond == 1 else 8
        row = call(
            functools.partial(second_image, bond),
            f"second_image_{bond}",
            [SMEM] + [VMEM] * (7 + len(rows_in)),
            (VMEM, jax.ShapeDtypeStruct((height, 128), F32)),
            [pltpu.VMEM((5,) + pair, BF16)],
            apply_flops,
            2 * env_bytes,
        )(
            term_shift,
            lefts[bond],
            rights[bond],
            rests_sent[bond],
            rest_lows[bond],
            rest_highs[bond],
            starts[bond],
            rests[bond],
            *rows_in,
        )
        rows.append(row)
    numbers = lax.all_to_all(rows[-1], ("seg", "blk"), 0, 0, tiled=True)
    place = jnp.stack([lax.axis_index("seg"), lax.axis_index("blk")]).astype(jnp.int32)
    ground_a, ground_b, energies, boundary = call(
        functools.partial(finish, 1.0 / block, ups),
        "finish",
        [SMEM] + [VMEM] * 9,
        (
            (VMEM, VMEM, VMEM, ANY),
            (
                state32,
                state32,
                jax.ShapeDtypeStruct((1, 2), F32),
                jax.ShapeDtypeStruct(env_shape, BF16),
            ),
        ),
        [pltpu.VMEM(env_shape, BF16), pltpu.SemaphoreType.DMA((channels,))],
        apply_flops,
        2 * env_bytes,
    )(
        place,
        numbers,
        starts[0],
        rests[0],
        starts[1],
        rests[1],
        start_next,
        rest_next,
        edge_state.reshape(pair),
        env,
    )
    return (
        ground_a.reshape(guess_a.shape),
        ground_b.reshape(guess_b.shape),
        energies,
        boundary.reshape(left_env_a.shape),
    )


def solution(mesh):
    placed = (
        P("seg", "blk", None, None, None),
        P("seg", "blk", None, None, None),
        P("seg", None, "blk", None, None, None),
        P("seg", None, "blk", None, None, None),
        P("seg", None, "blk", None, None, None),
        P("seg", None, "blk", None, None, None),
        P(),
        P(),
        P("seg", None, "blk", None),
        P("blk", None, None, None),
    )
    return jax.shard_map(
        local,
        mesh=mesh,
        in_specs=placed,
        out_specs=(
            P("seg", "blk", None, None, None),
            P("seg", "blk", None, None, None),
            P("seg", None),
            P("seg", None, "blk", None, None, None),
        ),
        check_vma=False,
    )
```

time: 518 us -> 82.7 us (0.16)
  the two profiles are of different devices: /device:TPU:6 before, /device:TPU:0 now
where the time goes in v1:
time: 82.7 us; the launch traced here: 82 us
  starting transfers between devices  34 us (41%)
  Pallas kernels  24.6 us (30%)
  local copies, waits for them, and re-layouts  12.1 us (15%)
  waiting for transfers between devices  7.08 us (9%)
  other arithmetic  3.09 us (4%)
  between operations  1.03 us (1%)
    ppermute x10, starting transfers between devices, passed_along(): return lax.ppermute(block, axis, route)  24.7 us
    unnamed x35, local copies, waits for them, and re-layouts  9.44 us
    all_to_all x1, starting transfers between devices, local(): numbers = lax.all_to_all(rows[-1], ('seg', 'blk'), 0, 0, tiled=True)  9.33 us
    pallas_call x2, Pallas kernels, local(): call(functools.partial(first_image, bond), f'first_image_{bond}', [SMEM,...  8.56 us
    all_to_all x1, waiting for transfers between devices, local(): numbers = lax.all_to_all(rows[-1], ('seg', 'blk'), 0, 0, tiled=True)  7.05 us
    pallas_call x2, Pallas kernels, local(): call(functools.partial(second_image, bond), f'second_image_{bond}', [SMEM...  6.85 us
    pallas_call x1, Pallas kernels, local(): call(functools.partial(finish, 1.0 / block, ups), 'finish', [SMEM] + [VME...  6.03 us
    mul x1, local copies, waits for them, and re-layouts, local(): squared[:, None, :, None] * jnp.eye(GROUP, dtype=F32)[None, :, None, :]  2.55 us
  transfers between devices with their start and end apart: 11, of which 1 were waited for; matrix products, arithmetic and copies ran while one was open for 7% of the time, Pallas kernels for 21%

profile of v1, /device:TPU:0, one launch (start us, length us, event | category | flops | bytes accessed | tf_op | source)
XLA Modules:
  0.0 82.0 jit_solution(9733078245088310892)
XLA Ops:
  0.7 0.9 %copy.18 = s32[1,4,1,2]{3,1,2,0:T(4,128)S(1)} copy(s32[1,4,1,2]{1,3,2,0:T(2,128)} %param.18) | data formatting | bytes 64 | tf_op args[8]
  1.6 0.1 reshape.58.sizes
  1.7 0.9 %copy-done.13 = bf16[1,1,2,256,256]{4,3,2,1,0:T(8,128)(2,1)S(1)} copy-done((bf16[1,1,2,256,256]{4,3,2,1,0:T(8,128)(2,1)S(1)}, bf16[1,1,2,256,256]{4,3,2,1,0:T(8,128)(2,1)}, u32[]{:S(2)}) %copy-start.13) | copy-done | bytes 262168
  2.6 0.9 %copy-done.14 = bf16[1,1,2,256,256]{4,3,2,1,0:T(8,128)(2,1)S(1)} copy-done((bf16[1,1,2,256,256]{4,3,2,1,0:T(8,128)(2,1)S(1)}, bf16[1,1,2,256,256]{4,3,2,1,0:T(8,128)(2,1)}, u32[]{:S(2)}) %copy-start.14) | copy-done | bytes 262168
  3.6 1.3 %masked_starts.1 = (bf16[2,256,256]{2,1,0:T(8,128)(2,1)S(1)}, bf16[2,256,256]{2,1,0:T(8,128)(2,1)}) custom-call(s32[8]{0:T(128)S(1)} %reshape.58.sizes, bf16[2,256,256]{2,1,0:T(8,128)(2,1)S(1)} %bitcast.31, bf16[2,256,256]{2,1,0:T(8,128)(2,1)S(1)} %bitcast.32), custom_call_target="tpu_custom_call" | custom-call | flops 524288 | bytes 1048576 | tf_op jit(solution)/shard_map/masked_starts/pallas_call | solution.py:295
  4.9 1.3 %collective-permute-start.5 = (bf16[2,256,256]{2,1,0:T(8,128)(2,1)S(1)}, bf16[2,256,256]{2,1,0:T(8,128)(2,1)}, u32[]{:S(2)}, u32[]{:S(2)}) collective-permute-start(bf16[2,256,256]{2,1,0:T(8,128)(2,1)S(1)} %get-tuple-element.19.own.start.start_a), channel_id=1, source_target_pairs={{1,0},{2,1},{3,2},{4,3},{5,4},{6,5},{7,6},{9,8},{10,9},{11,10},{12... | collective-permute-start | bytes 786440 | tf_op jit(solution)/shard_map/ppermute | solution.py:263
  6.2 3.7 %collective-permute-start.4 = (bf16[2,256,256]{2,1,0:T(8,128)(2,1)S(1)}, bf16[2,256,256]{2,1,0:T(8,128)(2,1)}, u32[]{:S(2)}, u32[]{:S(2)}) collective-permute-start(bf16[2,256,256]{2,1,0:T(8,128)(2,1)S(1)} %get-tuple-element.19.own.start.start_a), channel_id=1, source_target_pairs={{0,1},{1,2},{2,3},{3,4},{4,5},{5,6},{6,7},{8,9},{9,10},{10,11},{11... | collective-permute-start | bytes 786440 | tf_op jit(solution)/shard_map/ppermute | solution.py:263
  9.9 1.3 %collective-permute-start.8 = (bf16[2,256,256]{2,1,0:T(8,128)(2,1)}, bf16[2,256,256]{2,1,0:T(8,128)(2,1)}, u32[]{:S(2)}, u32[]{:S(2)}) collective-permute-start(bf16[2,256,256]{2,1,0:T(8,128)(2,1)} %get-tuple-element.16.own.start.start_b), channel_id=1, source_target_pairs={{8,0},{16,8},{24,16},{9,1},{17,9},{25,17},{10,2},{18,10},{26,18},{... | collective-permute-start | bytes 786440 | tf_op jit(solution)/shard_map/ppermute | solution.py:263
  11.2 1.3 %collective-permute-start.1 = (bf16[2,256,256]{2,1,0:T(8,128)(2,1)}, bf16[2,256,256]{2,1,0:T(8,128)(2,1)}, u32[]{:S(2)}, u32[]{:S(2)}) collective-permute-start(bf16[2,256,256]{2,1,0:T(8,128)(2,1)} %get-tuple-element.16.own.start.start_b), channel_id=1, source_target_pairs={{1,0},{2,1},{3,2},{4,3},{5,4},{6,5},{7,6},{9,8},{10,9},{11,10},{12... | collective-permute-start | bytes 786440 | tf_op jit(solution)/shard_map/ppermute | solution.py:263
  12.5 5.2 %collective-permute-start = (bf16[2,256,256]{2,1,0:T(8,128)(2,1)}, bf16[2,256,256]{2,1,0:T(8,128)(2,1)}, u32[]{:S(2)}, u32[]{:S(2)}) collective-permute-start(bf16[2,256,256]{2,1,0:T(8,128)(2,1)} %get-tuple-element.16.own.start.start_b), channel_id=1, source_target_pairs={{0,1},{1,2},{2,3},{3,4},{4,5},{5,6},{6,7},{8,9},{9,10},{10,11},{11... | collective-permute-start | bytes 786440 | tf_op jit(solution)/shard_map/ppermute | solution.py:263
  17.7 0.1 fusion.1
  17.9 1.3 %broadcast_multiply_fusion = f32[12,16,12,16]{3,2,1,0:T(8,128)} fusion(f32[16,16]{1,0:T(8,128)S(1)} %fusion, f32[12,12]{1,0:T(8,128)S(1)} %fusion.1), kind=kLoop, calls=%fused_computation | loop fusion | flops 36864 | bytes 149056 | tf_op jit(solution)/shard_map/mul | solution.py:309
  19.2 2.6 %mul.20 = f32[192,192]{1,0:T(8,128)} reshape(f32[12,16,12,16]{3,2,1,0:T(8,128)} %broadcast_multiply_fusion) | data formatting | bytes 294912 | tf_op jit(solution)/shard_map/mul | solution.py:309
  21.7 1.7 %subtract_convert_fusion = (bf16[192,192]{1,0:T(8,128)(2,1)S(1)}, bf16[192,192]{1,0:T(8,128)(2,1)}) fusion(f32[192,192]{1,0:T(8,128)} %mul.20), kind=kLoop, calls=%fused_computation.1 | loop fusion | flops 147456 | bytes 294912 | tf_op jit(solution)/shard_map/convert_element_type | solution.py:313
  23.5 1.9 %copy-done.2 = bf16[1,12,1,2,256,256]{5,4,3,2,1,0:T(8,128)(2,1)S(1)} copy-done((bf16[1,12,1,2,256,256]{5,4,3,2,1,0:T(8,128)(2,1)S(1)}, bf16[1,12,1,2,256,256]{5,4,3,2,1,0:T(8,128)(2,1)}, u32[]{:S(2)}) %copy-start.2) | copy-done | bytes 3145752
  25.4 4.1 %first_image_0.1 = (f32[2,256,256]{2,1,0:T(8,128)S(1)}, bf16[2,256,256]{2,1,0:T(8,128)(2,1)S(1)}, f32[8,128]{1,0:T(8,128)S(1)}) custom-call(s32[12]{0:T(128)S(1)} %copy-done.15, s32[8]{0:T(128)S(1)} %reshape.58.sizes, bf16[12,2,256,256]{3,2,1,0:T(8,128)(2,1)S(1)} %bitcast.22, bf16[12,2,256,256]{3,2,1,0:T(8,128)(2,1)S(1)} %bitcast.25, ...), custom_call_target="tpu_custom_call" | custom-call | flops 1610612736 | bytes 6291456 | tf_op jit(solution)/shard_map/first_image_0/pallas_call | solution.py:326
  29.4 1.3 %collective-permute-start.7 = (bf16[2,256,256]{2,1,0:T(8,128)(2,1)S(1)}, bf16[2,256,256]{2,1,0:T(8,128)(2,1)S(1)}, u32[]{:S(2)}, u32[]{:S(2)}) collective-permute-start(bf16[2,256,256]{2,1,0:T(8,128)(2,1)S(1)} %get-tuple-element.22.own), channel_id=1, source_target_pairs={{1,0},{2,1},{3,2},{4,3},{5,4},{6,5},{7,6},{9,8},{10,9},{11,10},{12... | collective-permute-start | bytes 786440 | tf_op jit(solution)/shard_map/ppermute | solution.py:263
  30.7 3.6 %collective-permute-start.6 = (bf16[2,256,256]{2,1,0:T(8,128)(2,1)S(1)}, bf16[2,256,256]{2,1,0:T(8,128)(2,1)S(1)}, u32[]{:S(2)}, u32[]{:S(2)}) collective-permute-start(bf16[2,256,256]{2,1,0:T(8,128)(2,1)S(1)} %get-tuple-element.22.own), channel_id=1, source_target_pairs={{0,1},{1,2},{2,3},{3,4},{4,5},{5,6},{6,7},{8,9},{9,10},{10,11},{11... | collective-permute-start | bytes 786440 | tf_op jit(solution)/shard_map/ppermute | solution.py:263
  34.4 4.5 %first_image_1.1 = (f32[2,256,256]{2,1,0:T(8,128)S(1)}, bf16[2,256,256]{2,1,0:T(8,128)(2,1)}, f32[8,128]{1,0:T(8,128)S(1)}) custom-call(s32[12]{0:T(128)S(1)} %copy-done.15, s32[8]{0:T(128)S(1)} %reshape.58.sizes, bf16[12,2,256,256]{3,2,1,0:T(8,128)(2,1)S(1)} %bitcast.27, bf16[12,2,256,256]{3,2,1,0:T(8,128)(2,1)S(1)} %bitcast.29, ...), custom_call_target="tpu_custom_call" | custom-call | flops 1610612736 | bytes 6291456 | tf_op jit(solution)/shard_map/first_image_1/pallas_call | solution.py:326
  38.9 1.3 %collective-permute-start.3 = (bf16[2,256,256]{2,1,0:T(8,128)(2,1)}, bf16[2,256,256]{2,1,0:T(8,128)(2,1)S(1)}, u32[]{:S(2)}, u32[]{:S(2)}) collective-permute-start(bf16[2,256,256]{2,1,0:T(8,128)(2,1)} %get-tuple-element.17.own), channel_id=1, source_target_pairs={{1,0},{2,1},{3,2},{4,3},{5,4},{6,5},{7,6},{9,8},{10,9},{11,10},{12... | collective-permute-start | bytes 786440 | tf_op jit(solution)/shard_map/ppermute | solution.py:263
  40.2 4.3 %collective-permute-start.2 = (bf16[2,256,256]{2,1,0:T(8,128)(2,1)}, bf16[2,256,256]{2,1,0:T(8,128)(2,1)S(1)}, u32[]{:S(2)}, u32[]{:S(2)}) collective-permute-start(bf16[2,256,256]{2,1,0:T(8,128)(2,1)} %get-tuple-element.17.own), channel_id=1, source_target_pairs={{0,1},{1,2},{2,3},{3,4},{4,5},{5,6},{6,7},{8,9},{9,10},{10,11},{11... | collective-permute-start | bytes 786440 | tf_op jit(solution)/shard_map/ppermute | solution.py:263
  44.5 1.8 %mixed_env.1.env = bf16[12,2,256,256]{3,2,1,0:T(8,128)(2,1)S(1)} custom-call(bf16[192,192]{1,0:T(8,128)(2,1)S(1)} %copy-done.12, bf16[192,192]{1,0:T(8,128)(2,1)S(1)} %get-tuple-element.40.mix_low, bf16[12,2,256,256]{3,2,1,0:T(8,128)(2,1)S(1)} %bitcast.23), custom_call_target="tpu_custom_call" | custom-call | flops 1207959552 | bytes 6291456 | tf_op jit(solution)/shard_map/mixed_env/pallas_call | solution.py:314
  46.3 1.7 %copy-done.6 = bf16[12,2,256,256]{3,2,1,0:T(8,128)(2,1)} copy-done((bf16[12,2,256,256]{3,2,1,0:T(8,128)(2,1)}, bf16[12,2,256,256]{3,2,1,0:T(8,128)(2,1)S(1)}, u32[]{:S(2)}) %copy-start.6) | copy-done | bytes 3145752
  47.9 1.5 %collective-permute-start.9 = (bf16[2,256,256]{2,1,0:T(8,128)(2,1)}, bf16[2,256,256]{2,1,0:T(8,128)(2,1)}, u32[]{:S(2)}, u32[]{:S(2)}) collective-permute-start(bf16[2,256,256]{2,1,0:T(8,128)(2,1)} %get-tuple-element.17.own), channel_id=1, source_target_pairs={{8,0},{16,8},{24,16},{9,1},{17,9},{25,17},{10,2},{18,10},{26,18},{... | collective-permute-start | bytes 786440 | tf_op jit(solution)/shard_map/ppermute | solution.py:263
  49.4 2.8 %second_image_0.1.refs_2_ = f32[8,128]{1,0:T(8,128)S(1)} custom-call(s32[12]{0:T(128)S(1)} %copy-done.15, bf16[12,2,256,256]{3,2,1,0:T(8,128)(2,1)S(1)} %bitcast.24, bf16[12,2,256,256]{3,2,1,0:T(8,128)(2,1)S(1)} %bitcast.26, bf16[2,256,256]{2,1,0:T(8,128)(2,1)S(1)} %get-tuple-element.22.own, bf16[2,256,256]{2,1,0:T(8,128)(2,1)S(1)} %collective-permute-done.6.low, ...), custom_call_target="tpu_custom_call" | custom-call | flops 1610612736 | bytes 6291456 | tf_op jit(solution)/shard_map/second_image_0/pallas_call | solution.py:344
  52.3 4.0 %second_image_1.1 = f32[32,128]{1,0:T(8,128)} custom-call(s32[12]{0:T(128)S(1)} %copy-done.15, bf16[12,2,256,256]{3,2,1,0:T(8,128)(2,1)S(1)} %bitcast.28, bf16[12,2,256,256]{3,2,1,0:T(8,128)(2,1)S(1)} %bitcast.30, bf16[2,256,256]{2,1,0:T(8,128)(2,1)} %get-tuple-element.17.own, bf16[2,256,256]{2,1,0:T(8,128)(2,1)S(1)} %collective-permute-done.2.low, ...), custom_call_target="tpu_custom_call" | custom-call | flops 1610612736 | bytes 6291456 | tf_op jit(solution)/shard_map/second_image_1/pallas_call | solution.py:344
  56.3 9.3 %all-to-all-start = ((f32[32,1,128]{2,1,0:T(1,128)}), f32[32,1,128]{2,1,0:T(1,128)S(1)}, u32[]{:S(2)}, u32[]{:S(2)}) async-start(f32[32,1,128]{2,1,0:T(1,128)} %bitcast.9), calls=%async_computation | async-start | bytes 32768 | tf_op jit(solution)/shard_map/all_to_all | solution.py:364
  65.7 7.0 %all-to-all-done = f32[32,1,128]{2,1,0:T(1,128)S(1)} async-done(((f32[32,1,128]{2,1,0:T(1,128)}), f32[32,1,128]{2,1,0:T(1,128)S(1)}, u32[]{:S(2)}, u32[]{:S(2)}) %all-to-all-start) | async-done | bytes 16416 | tf_op jit(solution)/shard_map/all_to_all | solution.py:364
  72.8 1.0 %copy-done.9 = f32[2,256,256]{2,1,0:T(8,128)S(1)} copy-done((f32[2,256,256]{2,1,0:T(8,128)S(1)}, f32[2,256,256]{2,1,0:T(8,128)}, u32[]{:S(2)}) %copy-start.9) | copy-done | bytes 524312
  73.8 1.0 %copy-done.11 = f32[2,256,256]{2,1,0:T(8,128)S(1)} copy-done((f32[2,256,256]{2,1,0:T(8,128)S(1)}, f32[2,256,256]{2,1,0:T(8,128)}, u32[]{:S(2)}) %copy-start.11) | copy-done | bytes 524312
  74.9 0.9 %copy-done.16 = bf16[1,2,256,256]{3,2,1,0:T(8,128)(2,1)S(1)} copy-done((bf16[1,2,256,256]{3,2,1,0:T(8,128)(2,1)S(1)}, bf16[1,2,256,256]{3,2,1,0:T(8,128)(2,1)}, u32[]{:S(2)}) %copy-start.16) | copy-done | bytes 262168
  75.8 6.0 %finish.1 = (f32[2,256,256]{2,1,0:T(8,128)}, f32[2,256,256]{2,1,0:T(8,128)}, f32[1,2]{1,0:T(1,128)}, bf16[12,2,256,256]{3,2,1,0:T(8,128)(2,1)}) custom-call(s32[2]{0:T(128)S(1)} %pad_add_fusion.place, f32[32,128]{1,0:T(8,128)S(1)} %bitcast.33, bf16[2,256,256]{2,1,0:T(8,128)(2,1)S(1)} %get-tuple-element.19.own.start.start_a, f32[2,256,256]{2,1,0:T(8,128)S(1)} %copy-done.9, ...), custom_call_target="tpu_custom_call" | custom-call | flops 1610612736 | bytes 6291456 | tf_op jit(solution)/shard_map/finish/pallas_call | solution.py:366
  (39 shorter events, 0.2 us)
Async XLA Ops:
  0.6 17.1 %copy-start = (f32[12,12]{1,0:T(8,128)S(1)}, f32[12,12]{1,0:T(8,128)}, u32[]{:S(2)}) copy-start(f32[12,12]{1,0:T(8,128)} %param.16) | copy-start | bytes 1732
  0.6 22.8 %copy-start.1 = (bf16[1,12,1,2,256,256]{5,4,3,2,1,0:T(8,128)(2,1)S(1)}, bf16[1,12,1,2,256,256]{5,4,3,2,1,0:T(8,128)(2,1)}, u32[]{:S(2)}) copy-start(bf16[1,12,1,2,256,256]{5,4,3,2,1,0:T(8,128)(2,1)} %param.12) | copy-start | bytes 9437188
  1.7 1.0 %copy-start.13 = (bf16[1,1,2,256,256]{4,3,2,1,0:T(8,128)(2,1)S(1)}, bf16[1,1,2,256,256]{4,3,2,1,0:T(8,128)(2,1)}, u32[]{:S(2)}) copy-start(bf16[1,1,2,256,256]{4,3,2,1,0:T(8,128)(2,1)} %param.10) | copy-start | bytes 786436
  2.6 0.9 %copy-start.14 = (bf16[1,1,2,256,256]{4,3,2,1,0:T(8,128)(2,1)S(1)}, bf16[1,1,2,256,256]{4,3,2,1,0:T(8,128)(2,1)}, u32[]{:S(2)}) copy-start(bf16[1,1,2,256,256]{4,3,2,1,0:T(8,128)(2,1)} %param.11) | copy-start | bytes 786436
  3.6 19.9 %copy-start.15 = (s32[12]{0:T(128)S(1)}, s32[12]{0:T(128)}, u32[]{:S(2)}) copy-start(s32[12]{0:T(128)} %shift.7) | copy-start | bytes 148
  4.9 18.5 %collective-permute-start.5 = (bf16[2,256,256]{2,1,0:T(8,128)(2,1)S(1)}, bf16[2,256,256]{2,1,0:T(8,128)(2,1)}, u32[]{:S(2)}, u32[]{:S(2)}) collective-permute-start(bf16[2,256,256]{2,1,0:T(8,128)(2,1)S(1)} %get-tuple-element.19.own.start.start_a), channel_id=1, source_target_pairs={{1,0},{2,1},{3,2},{4,3},{5,4},{6,5},{7,6},{9,8},{10,9},{11,10},{12... | collective-permute-start | bytes 786440 | tf_op jit(solution)/shard_map/ppermute | solution.py:263
  6.2 17.3 %collective-permute-start.4 = (bf16[2,256,256]{2,1,0:T(8,128)(2,1)S(1)}, bf16[2,256,256]{2,1,0:T(8,128)(2,1)}, u32[]{:S(2)}, u32[]{:S(2)}) collective-permute-start(bf16[2,256,256]{2,1,0:T(8,128)(2,1)S(1)} %get-tuple-element.19.own.start.start_a), channel_id=1, source_target_pairs={{0,1},{1,2},{2,3},{3,4},{4,5},{5,6},{6,7},{8,9},{9,10},{10,11},{11... | collective-permute-start | bytes 786440 | tf_op jit(solution)/shard_map/ppermute | solution.py:263
  9.9 55.8 %collective-permute-start.8 = (bf16[2,256,256]{2,1,0:T(8,128)(2,1)}, bf16[2,256,256]{2,1,0:T(8,128)(2,1)}, u32[]{:S(2)}, u32[]{:S(2)}) collective-permute-start(bf16[2,256,256]{2,1,0:T(8,128)(2,1)} %get-tuple-element.16.own.start.start_b), channel_id=1, source_target_pairs={{8,0},{16,8},{24,16},{9,1},{17,9},{25,17},{10,2},{18,10},{26,18},{... | collective-permute-start | bytes 786440 | tf_op jit(solution)/shard_map/ppermute | solution.py:263
  11.2 23.1 %collective-permute-start.1 = (bf16[2,256,256]{2,1,0:T(8,128)(2,1)}, bf16[2,256,256]{2,1,0:T(8,128)(2,1)}, u32[]{:S(2)}, u32[]{:S(2)}) collective-permute-start(bf16[2,256,256]{2,1,0:T(8,128)(2,1)} %get-tuple-element.16.own.start.start_b), channel_id=1, source_target_pairs={{1,0},{2,1},{3,2},{4,3},{5,4},{6,5},{7,6},{9,8},{10,9},{11,10},{12... | collective-permute-start | bytes 786440 | tf_op jit(solution)/shard_map/ppermute | solution.py:263
  12.5 21.8 %collective-permute-start = (bf16[2,256,256]{2,1,0:T(8,128)(2,1)}, bf16[2,256,256]{2,1,0:T(8,128)(2,1)}, u32[]{:S(2)}, u32[]{:S(2)}) collective-permute-start(bf16[2,256,256]{2,1,0:T(8,128)(2,1)} %get-tuple-element.16.own.start.start_b), channel_id=1, source_target_pairs={{0,1},{1,2},{2,3},{3,4},{4,5},{5,6},{6,7},{8,9},{9,10},{10,11},{11... | collective-permute-start | bytes 786440 | tf_op jit(solution)/shard_map/ppermute | solution.py:263
  23.5 1.9 %copy-start.2 = (bf16[1,12,1,2,256,256]{5,4,3,2,1,0:T(8,128)(2,1)S(1)}, bf16[1,12,1,2,256,256]{5,4,3,2,1,0:T(8,128)(2,1)}, u32[]{:S(2)}) copy-start(bf16[1,12,1,2,256,256]{5,4,3,2,1,0:T(8,128)(2,1)} %param.13) | copy-start | bytes 9437188
  25.3 9.0 %copy-start.4 = (bf16[1,12,1,2,256,256]{5,4,3,2,1,0:T(8,128)(2,1)S(1)}, bf16[1,12,1,2,256,256]{5,4,3,2,1,0:T(8,128)(2,1)}, u32[]{:S(2)}) copy-start(bf16[1,12,1,2,256,256]{5,4,3,2,1,0:T(8,128)(2,1)} %param.14) | copy-start | bytes 9437188
  25.3 9.0 %copy-start.5 = (bf16[1,12,1,2,256,256]{5,4,3,2,1,0:T(8,128)(2,1)S(1)}, bf16[1,12,1,2,256,256]{5,4,3,2,1,0:T(8,128)(2,1)}, u32[]{:S(2)}) copy-start(bf16[1,12,1,2,256,256]{5,4,3,2,1,0:T(8,128)(2,1)} %param.15) | copy-start | bytes 9437188
  29.4 20.0 %copy-start.8 = (f32[2,256,256]{2,1,0:T(8,128)}, f32[2,256,256]{2,1,0:T(8,128)S(1)}, u32[]{:S(2)}) copy-start(f32[2,256,256]{2,1,0:T(8,128)S(1)} %get-tuple-element.23.rest.rest_a) | copy-start | bytes 1572868
  29.4 18.5 %collective-permute-start.7 = (bf16[2,256,256]{2,1,0:T(8,128)(2,1)S(1)}, bf16[2,256,256]{2,1,0:T(8,128)(2,1)S(1)}, u32[]{:S(2)}, u32[]{:S(2)}) collective-permute-start(bf16[2,256,256]{2,1,0:T(8,128)(2,1)S(1)} %get-tuple-element.22.own), channel_id=1, source_target_pairs={{1,0},{2,1},{3,2},{4,3},{5,4},{6,5},{7,6},{9,8},{10,9},{11,10},{12... | collective-permute-start | bytes 786440 | tf_op jit(solution)/shard_map/ppermute | solution.py:263
  30.7 18.7 %collective-permute-start.6 = (bf16[2,256,256]{2,1,0:T(8,128)(2,1)S(1)}, bf16[2,256,256]{2,1,0:T(8,128)(2,1)S(1)}, u32[]{:S(2)}, u32[]{:S(2)}) collective-permute-start(bf16[2,256,256]{2,1,0:T(8,128)(2,1)S(1)} %get-tuple-element.22.own), channel_id=1, source_target_pairs={{0,1},{1,2},{2,3},{3,4},{4,5},{5,6},{6,7},{8,9},{9,10},{10,11},{11... | collective-permute-start | bytes 786440 | tf_op jit(solution)/shard_map/ppermute | solution.py:263
  34.4 10.1 %copy-start.12 = (bf16[192,192]{1,0:T(8,128)(2,1)S(1)}, bf16[192,192]{1,0:T(8,128)(2,1)}, u32[]{:S(2)}) copy-start(bf16[192,192]{1,0:T(8,128)(2,1)} %get-tuple-element.41.mix_high) | copy-start | bytes 221188
  38.9 13.4 %copy-start.10 = (f32[2,256,256]{2,1,0:T(8,128)}, f32[2,256,256]{2,1,0:T(8,128)S(1)}, u32[]{:S(2)}) copy-start(f32[2,256,256]{2,1,0:T(8,128)S(1)} %get-tuple-element.18.rest.rest_b) | copy-start | bytes 1572868
  38.9 13.4 %collective-permute-start.3 = (bf16[2,256,256]{2,1,0:T(8,128)(2,1)}, bf16[2,256,256]{2,1,0:T(8,128)(2,1)S(1)}, u32[]{:S(2)}, u32[]{:S(2)}) collective-permute-start(bf16[2,256,256]{2,1,0:T(8,128)(2,1)} %get-tuple-element.17.own), channel_id=1, source_target_pairs={{1,0},{2,1},{3,2},{4,3},{5,4},{6,5},{7,6},{9,8},{10,9},{11,10},{12... | collective-permute-start | bytes 786440 | tf_op jit(solution)/shard_map/ppermute | solution.py:263
  40.2 12.1 %collective-permute-start.2 = (bf16[2,256,256]{2,1,0:T(8,128)(2,1)}, bf16[2,256,256]{2,1,0:T(8,128)(2,1)S(1)}, u32[]{:S(2)}, u32[]{:S(2)}) collective-permute-start(bf16[2,256,256]{2,1,0:T(8,128)(2,1)} %get-tuple-element.17.own), channel_id=1, source_target_pairs={{0,1},{1,2},{2,3},{3,4},{4,5},{5,6},{6,7},{8,9},{9,10},{10,11},{11... | collective-permute-start | bytes 786440 | tf_op jit(solution)/shard_map/ppermute | solution.py:263
  44.5 5.0 %copy-start.3 = (bf16[1,12,1,2,256,256]{5,4,3,2,1,0:T(8,128)(2,1)S(1)}, bf16[1,12,1,2,256,256]{5,4,3,2,1,0:T(8,128)(2,1)}, u32[]{:S(2)}) copy-start(bf16[1,12,1,2,256,256]{5,4,3,2,1,0:T(8,128)(2,1)} %param.13) | copy-start | bytes 9437188
  46.3 1.7 %copy-start.6 = (bf16[12,2,256,256]{3,2,1,0:T(8,128)(2,1)}, bf16[12,2,256,256]{3,2,1,0:T(8,128)(2,1)S(1)}, u32[]{:S(2)}) copy-start(bf16[12,2,256,256]{3,2,1,0:T(8,128)(2,1)S(1)} %mixed_env.1.env) | copy-start | bytes 9437188
  47.9 17.8 %collective-permute-start.9 = (bf16[2,256,256]{2,1,0:T(8,128)(2,1)}, bf16[2,256,256]{2,1,0:T(8,128)(2,1)}, u32[]{:S(2)}, u32[]{:S(2)}) collective-permute-start(bf16[2,256,256]{2,1,0:T(8,128)(2,1)} %get-tuple-element.17.own), channel_id=1, source_target_pairs={{8,0},{16,8},{24,16},{9,1},{17,9},{25,17},{10,2},{18,10},{26,18},{... | collective-permute-start | bytes 786440 | tf_op jit(solution)/shard_map/ppermute | solution.py:263
  52.3 20.5 %copy-start.7 = (bf16[12,2,256,256]{3,2,1,0:T(8,128)(2,1)S(1)}, bf16[12,2,256,256]{3,2,1,0:T(8,128)(2,1)}, u32[]{:S(2)}) copy-start(bf16[12,2,256,256]{3,2,1,0:T(8,128)(2,1)} %copy-done.6) | copy-start | bytes 9437188
  56.3 16.5 %all-to-all-start = ((f32[32,1,128]{2,1,0:T(1,128)}), f32[32,1,128]{2,1,0:T(1,128)S(1)}, u32[]{:S(2)}, u32[]{:S(2)}) async-start(f32[32,1,128]{2,1,0:T(1,128)} %bitcast.9), calls=%async_computation | async-start | bytes 32768 | tf_op jit(solution)/shard_map/all_to_all | solution.py:364
  72.8 1.0 %copy-start.9 = (f32[2,256,256]{2,1,0:T(8,128)S(1)}, f32[2,256,256]{2,1,0:T(8,128)}, u32[]{:S(2)}) copy-start(f32[2,256,256]{2,1,0:T(8,128)} %copy-done.8) | copy-start | bytes 1572868
  73.8 1.0 %copy-start.11 = (f32[2,256,256]{2,1,0:T(8,128)S(1)}, f32[2,256,256]{2,1,0:T(8,128)}, u32[]{:S(2)}) copy-start(f32[2,256,256]{2,1,0:T(8,128)} %copy-done.10) | copy-start | bytes 1572868
  74.9 0.9 %copy-start.16 = (bf16[1,2,256,256]{3,2,1,0:T(8,128)(2,1)S(1)}, bf16[1,2,256,256]{3,2,1,0:T(8,128)(2,1)}, u32[]{:S(2)}) copy-start(bf16[1,2,256,256]{3,2,1,0:T(8,128)(2,1)} %param.19) | copy-start | bytes 786436

commit v2 on v0

v2 whole, which is shorter than its diff:
```python
import functools

import jax
import jax.numpy as jnp
from jax import lax
from jax.experimental import pallas as pl
from jax.experimental.pallas import tpu as pltpu
from jax.sharding import PartitionSpec as P

F32 = jnp.float32
BF16 = jnp.bfloat16
VMEM = pl.BlockSpec(memory_space=pltpu.VMEM)
SMEM = pl.BlockSpec(memory_space=pltpu.SMEM)
HBM = pl.BlockSpec(memory_space=pltpu.HBM)
MIB = 1 << 20
GROUP = 16
BATCH = 3
BONDS = 2
CODES = 5

(
    SIZE,
    QUOTIENT,
    REST,
    REST_IMAGE,
    START_IMAGE,
    REST_OWN,
    REST_LOW,
    REST_HIGH,
    START_OWN,
    START_LOW,
    START_HIGH,
) = range(11)
BOND_LANES = 64


def call(body, name, ins, outs, scratch, flops, moved, limit=20 * MIB):
    return pl.pallas_call(
        body,
        name=name,
        in_specs=ins,
        out_specs=tuple(spec for spec, _ in outs),
        out_shape=tuple(shape for _, shape in outs),
        scratch_shapes=scratch,
        cost_estimate=pl.CostEstimate(flops=flops, bytes_accessed=moved, transcendentals=0),
        compiler_params=pltpu.CompilerParams(vmem_limit_bytes=limit),
    )


def in_hbm(array):
    return pltpu.with_memory_space_constraint(array, pltpu.HBM)


def live(rows, cols, block):
    row = lax.broadcasted_iota(jnp.int32, (block, block), 0)
    col = lax.broadcasted_iota(jnp.int32, (block, block), 1)
    return (row < rows) & (col < cols)


def live_of(sizes, bond, down, block):
    return live(sizes[0, 0, down, 2 * bond], sizes[0, 0, down, 2 * bond + 1], block)


def dot(left, right):
    return jnp.dot(left, right, preferred_element_type=F32)


def dot_by_rows(left, right):
    return lax.dot_general(left, right, (((1,), (1,)), ((), ())), preferred_element_type=F32)


def exact_dot(left, right):
    return jnp.dot(left, right, precision=lax.Precision.HIGHEST, preferred_element_type=F32)


def total(array):
    return jnp.sum(jnp.sum(array, axis=0, keepdims=True), axis=1, keepdims=True)


def in_lanes(width, pairs):
    lane = lax.broadcasted_iota(jnp.int32, (1, width), 1)
    row = jnp.zeros((1, width), F32)
    for place, value in pairs:
        row = jnp.where(lane == place, value, row)
    return row


def masked_starts(sizes, guess_a, guess_b, starts, sems):
    copies = [
        pltpu.make_async_copy(guess, starts.at[bond], sems.at[bond])
        for bond, guess in enumerate((guess_a, guess_b))
    ]
    for copy in copies:
        copy.start()
    downs, block = starts.shape[1], starts.shape[-1]
    for bond in range(BONDS):
        copies[bond].wait()
        for down in range(downs):
            start = starts[bond, down]
            starts[bond, down] = jnp.where(
                live_of(sizes, bond, down, block), start, jnp.zeros_like(start)
            )


def list_channels(shift, lists):
    channels = shift.shape[0]
    for code in range(CODES):
        count = jnp.int32(0)
        for channel in range(channels):
            lists[code, count] = jnp.int32(channel)
            count = count + (shift[channel] == code).astype(jnp.int32)
        lists[code, channels] = count


def add_images(lists, code, lefts, rights, sources, sums, arrived=None):
    channels = lefts[0].shape[0]
    downs = lefts[0].shape[1]
    units = [
        (bond, down)
        for bond in range(BONDS)
        for down in range(downs)
        if sources(bond, down) is not None
    ]

    def step(index, carry):
        channel = lists[code, index]
        if arrived is not None:
            arrived(channel)
        halves = [
            dot(lefts[bond][channel, down], sources(bond, down)[...]).astype(BF16)
            for bond, down in units
        ]
        for (bond, down), half in zip(units, halves):
            sums[bond, down] += dot_by_rows(half, rights[bond][channel, down])
        return carry

    lax.fori_loop(0, lists[code, channels], step, 0)


def add_local_images(lists, lefts, rights, states, sums, arrived=None):
    downs = states.shape[1]

    def below(bond, down):
        return states.at[bond, down - 1] if down > 0 else None

    def above(bond, down):
        return states.at[bond, down + 1] if down + 1 < downs else None

    add_images(lists, 0, lefts, rights, lambda bond, down: states.at[bond, down], sums, arrived)
    add_images(lists, 3, lefts, rights, below, sums, arrived)
    add_images(lists, 4, lefts, rights, above, sums, arrived)


def add_halo_images(lists, lefts, rights, swapped, shifted, halo, sums_low, sums_high):
    even = lax.rem(lax.axis_index("blk"), 2) == 0
    downs = swapped.shape[1]
    for bond in range(BONDS):
        for down in range(downs):
            one, other = swapped[bond, down], shifted[bond, down]
            halo[0, bond, down] = jnp.where(even, other, one)
            halo[1, bond, down] = jnp.where(even, one, other)
    add_images(lists, 1, lefts, rights, lambda bond, down: halo.at[0, bond, down], sums_low)
    add_images(lists, 2, lefts, rights, lambda bond, down: halo.at[1, bond, down], sums_high)


def opening(shift, starts, *refs):
    held, loaded, (own_images, lists, sems) = refs[:4], refs[4:8], refs[8:]
    left_a, right_a, left_b, right_b = loaded
    channels = left_a.shape[0]
    list_channels(shift, lists)

    def copies(channel):
        return [
            pltpu.make_async_copy(source.at[channel], target.at[channel], sems.at[channel])
            for source, target in zip(held, loaded)
        ]

    def bring(index, carry, code):
        for copy in copies(lists[code, index]):
            copy.start()
        return carry

    def await_one(channel):
        for copy in copies(channel):
            copy.wait()

    def await_listed(index, carry, code):
        await_one(lists[code, index])
        return carry

    for code in (0, 3, 4, 1, 2):
        lax.fori_loop(0, lists[code, channels], functools.partial(bring, code=code), 0)
    own_images[...] = jnp.zeros_like(own_images)
    add_local_images(lists, (left_a, left_b), (right_a, right_b), starts, own_images, await_one)
    for code in (1, 2):
        lax.fori_loop(0, lists[code, channels], functools.partial(await_listed, code=code), 0)


def mixing(mix, env, after, mixed):
    del after
    channels, downs, block = env.shape[0], env.shape[1], env.shape[-1]
    wide = channels * GROUP
    squared = exact_dot(mix[...], mix[...])
    spread_rows = (
        lax.broadcasted_iota(jnp.int32, (wide, channels), 0) // GROUP
        == lax.broadcasted_iota(jnp.int32, (wide, channels), 1)
    ).astype(F32)
    spread_cols = (
        lax.broadcasted_iota(jnp.int32, (channels, wide), 1) // GROUP
        == lax.broadcasted_iota(jnp.int32, (channels, wide), 0)
    ).astype(F32)
    spread = exact_dot(exact_dot(spread_rows, squared), spread_cols)
    same = lax.rem(lax.broadcasted_iota(jnp.int32, (wide, wide), 0), GROUP) == lax.rem(
        lax.broadcasted_iota(jnp.int32, (wide, wide), 1), GROUP
    )
    spread = jnp.where(same, spread, 0.0)
    mix_high = spread.astype(BF16)
    mix_low = (spread - mix_high.astype(F32)).astype(BF16)
    for down in range(downs):
        for group in range(block // GROUP):
            rows = slice(group * GROUP, (group + 1) * GROUP)
            part = env[:, down, rows, :].reshape(wide, block)
            made = dot(mix_high, part) + dot(mix_low, part)
            mixed[:, down, rows, :] = made.astype(BF16).reshape(channels, GROUP, block)


def first_images(
    lists,
    sizes,
    left_a,
    right_a,
    left_b,
    right_b,
    starts,
    swapped,
    shifted,
    own_images,
    rest,
    sent,
    along,
    halo_images,
    row,
    halo,
):
    downs, block = left_a.shape[1], left_a.shape[-1]
    halo_images[...] = jnp.zeros_like(halo_images)
    add_halo_images(
        lists,
        (left_a, left_b),
        (right_a, right_b),
        swapped,
        shifted,
        halo,
        halo_images.at[0],
        halo_images.at[1],
    )
    found = []
    for bond in range(BONDS):
        size = jnp.zeros((1, 1), F32)
        cross = jnp.zeros((1, 1), F32)
        for down in range(downs):
            image = own_images[bond, down] + halo_images[0, bond, down] + halo_images[1, bond, down]
            rest[bond, down] = image
            start = starts[bond, down].astype(F32)
            size += total(start * start)
            cross += total(start * image)
        quotient = jnp.where(size > 0.0, cross / jnp.where(size > 0.0, size, 1.0), 0.0)
        for down in range(downs):
            image = jnp.where(live_of(sizes, bond, down, block), rest[bond, down], 0.0)
            left_over = image - quotient * starts[bond, down].astype(F32)
            rest[bond, down] = left_over
            sent[bond, down] = left_over.astype(BF16)
        offset = bond * BOND_LANES
        found += [(offset + SIZE, size), (offset + QUOTIENT, quotient)]
    along[0] = starts[BONDS - 1]
    along[1] = sent[BONDS - 1]
    row[...] = jnp.broadcast_to(in_lanes(row.shape[1], found), row.shape)


def local_seconds(
    lists,
    left_a,
    right_a,
    left_b,
    right_b,
    sent,
    starts,
    rest,
    own_images,
    halo_images,
    row_in,
    row,
    sums,
):
    downs = left_a.shape[1]
    sums[...] = jnp.zeros_like(sums)
    add_local_images(lists, (left_a, left_b), (right_a, right_b), sent, sums)
    found = []
    for bond in range(BONDS):
        numbers = {place: jnp.zeros((1, 1), F32) for place in range(REST, START_HIGH + 1)}
        for down in range(downs):
            start = starts[bond, down].astype(F32)
            left_over = rest[bond, down]
            numbers[REST] += total(left_over * left_over)
            numbers[REST_IMAGE] += total(left_over * sums[bond, down])
            numbers[START_IMAGE] += total(start * sums[bond, down])
            parts = (own_images[bond, down], halo_images[0, bond, down], halo_images[1, bond, down])
            for kind, part in enumerate(parts):
                numbers[REST_OWN + kind] += total(left_over * part)
                numbers[START_OWN + kind] += total(start * part)
        offset = bond * BOND_LANES
        found += [(offset + place, numbers[place]) for place in sorted(numbers)]
    row[...] = row_in[...] + jnp.broadcast_to(in_lanes(row.shape[1], found), row.shape)


def halo_seconds(
    lists,
    left_a,
    right_a,
    left_b,
    right_b,
    swapped,
    shifted,
    starts,
    rest,
    row_in,
    row,
    halo,
    sums,
):
    downs = left_a.shape[1]
    sums[...] = jnp.zeros_like(sums)
    add_halo_images(
        lists, (left_a, left_b), (right_a, right_b), swapped, shifted, halo, sums, sums
    )
    found = []
    for bond in range(BONDS):
        of_rest = jnp.zeros((1, 1), F32)
        of_start = jnp.zeros((1, 1), F32)
        for down in range(downs):
            of_rest += total(rest[bond, down] * sums[bond, down])
            of_start += total(starts[bond, down].astype(F32) * sums[bond, down])
        offset = bond * BOND_LANES
        found += [(offset + REST_IMAGE, of_rest), (offset + START_IMAGE, of_start)]
    row[...] = jnp.broadcast_to(row_in[0:1, :] + in_lanes(row.shape[1], found), row.shape)


def ritz(rows):
    ups = rows.shape[1]

    def column(array, place):
        return array[:, :, place : place + 1]

    def over_ups(array):
        return jnp.sum(array, axis=1, keepdims=True)

    size = column(rows, SIZE)
    quotient = column(rows, QUOTIENT)
    norm_sq = over_ups(size)
    alpha_zero = over_ups(size * quotient) / norm_sq
    off = quotient - alpha_zero
    off_low = column(pltpu.roll(rows, 1, 1), QUOTIENT) - alpha_zero
    off_high = column(pltpu.roll(rows, ups - 1, 1), QUOTIENT) - alpha_zero
    residual_sq = over_ups(column(rows, REST) + size * off * off)
    crossed = column(rows, REST_IMAGE) + off * column(rows, START_IMAGE)
    for kind, factor in enumerate((off, off_low, off_high)):
        crossed += factor * (column(rows, REST_OWN + kind) + off * column(rows, START_OWN + kind))
    alpha_one = over_ups(crossed) / residual_sq
    beta_sq = residual_sq / norm_sq
    beta = jnp.sqrt(beta_sq)
    spread = 0.5 * (alpha_zero - alpha_one)
    energy = 0.5 * (alpha_zero + alpha_one) - jnp.sqrt(spread * spread + beta_sq)
    weight_one = energy - alpha_zero
    length = jnp.sqrt(beta_sq + weight_one * weight_one)
    of_rest = weight_one / (beta * length)
    of_start = beta / length + of_rest * off
    return energy, of_start, of_rest


def finish(
    factor,
    ups,
    numbers,
    starts_held,
    rest_held,
    along_held,
    edge_held,
    mixed_held,
    ground_a,
    ground_b,
    energies,
    boundary,
    starts,
    rest,
    along,
    edge,
    mixed,
    made,
    grounds,
    in_sems,
    mixed_sems,
    out_sems,
):
    channels, downs = mixed.shape[0], mixed.shape[1]
    held = ((starts_held, starts), (rest_held, rest), (along_held, along), (edge_held, edge))
    arrivals = [
        pltpu.make_async_copy(source, target, in_sems.at[index])
        for index, (source, target) in enumerate(held)
    ]
    arrivals += [
        pltpu.make_async_copy(mixed_held.at[index], mixed.at[index], mixed_sems.at[index])
        for index in range(channels)
    ]
    for copy in arrivals:
        copy.start()
    segments = numbers.shape[0] // ups
    seg, blk = lax.axis_index("seg"), lax.axis_index("blk")
    here = numbers[pl.ds(pl.multiple_of(seg * ups, ups), ups), :]
    after = jnp.minimum(seg + 1, segments - 1)
    there = numbers[pl.ds(pl.multiple_of(after * ups, ups), ups), :]
    width = numbers.shape[1]
    energy, of_start, of_rest = ritz(
        jnp.stack(
            [
                here,
                pltpu.roll(here, width - BOND_LANES, 1),
                pltpu.roll(there, width - BOND_LANES, 1),
            ]
        )
    )
    place = lax.broadcasted_iota(jnp.int32, of_start.shape, 1)
    of_start = jnp.sum(jnp.where(place == blk, of_start, 0.0), axis=1, keepdims=True)
    lane = lax.broadcasted_iota(jnp.int32, energies.shape, 1)
    energies[...] = jnp.where(lane == 0, energy[0], energy[1])
    last = seg == segments - 1
    for copy in arrivals[:2]:
        copy.wait()
    for bond in range(BONDS):
        for down in range(downs):
            start = starts[bond, down].astype(F32)
            grounds[bond, down] = of_start[bond] * start + of_rest[bond] * rest[bond, down]
    copies = [
        pltpu.make_async_copy(grounds.at[bond], target, out_sems.at[channels + bond])
        for bond, target in enumerate((ground_a, ground_b))
    ]
    for copy in copies:
        copy.start()
    for copy in arrivals[2:4]:
        copy.wait()
    products = []
    for down in range(downs):
        found = of_start[2] * along[0, down].astype(F32) + of_rest[2] * along[1, down].astype(F32)
        state = jnp.where(last, edge[down], found.astype(BF16))
        product = dot(grounds[0, down].astype(BF16), state) * factor
        products.append((product.astype(BF16), product.T.astype(BF16)))
    halves = {}

    def last_product(group):
        for channel in group:
            for down, (_, turned) in enumerate(products):
                made[channel, down] = dot(turned, halves[channel, down]).astype(BF16)
        for channel in group:
            copy = pltpu.make_async_copy(
                made.at[channel], boundary.at[channel], out_sems.at[channel]
            )
            copy.start()
            copies.append(copy)

    groups = [range(i, min(i + BATCH, channels)) for i in range(0, channels, BATCH)]
    for index, group in enumerate(groups):
        for channel in group:
            arrivals[4 + channel].wait()
        for channel in group:
            for down, (product, _) in enumerate(products):
                halves[channel, down] = dot(mixed[channel, down], product).astype(BF16)
        if index > 0:
            last_product(groups[index - 1])
    last_product(groups[-1])
    for copy in copies:
        copy.wait()


def swapped_pairs(block):
    devices = range(lax.axis_size("blk"))
    return lax.ppermute(block, "blk", [(i, i ^ 1) for i in devices if i ^ 1 in devices])


def shifted_pairs(block):
    devices = range(lax.axis_size("blk"))
    pairs = [(i, i + 1) for i in devices if i % 2 == 1 and i + 1 in devices]
    return lax.ppermute(block, "blk", pairs + [(j, i) for i, j in pairs])


def from_right_segment(block):
    segments = lax.axis_size("seg")
    return lax.ppermute(block, "seg", [(i + 1, i) for i in range(segments - 1)])


def local(
    guess_a,
    guess_b,
    left_env_a,
    right_env_a,
    left_env_b,
    right_env_b,
    channel_mix,
    term_shift,
    sector_sizes,
    edge_state,
):
    block = guess_a.shape[-1]
    downs = guess_a.shape[2]
    channels = left_env_a.shape[1]
    ups = lax.axis_size("blk")
    devices = ups * lax.axis_size("seg")
    pair = (downs, block, block)
    both = (BONDS,) + pair
    env_shape = (channels, downs, block, block)
    held = [in_hbm(env.reshape(env_shape)) for env in (left_env_a, right_env_a, left_env_b, right_env_b)]
    bits = 2 * downs * block * block
    env_bytes = channels * bits
    apply_flops = 4 * channels * downs * block**3
    sizes = in_hbm(sector_sizes.transpose(0, 2, 3, 1))
    tile = jax.ShapeDtypeStruct((8, 128), F32)

    (starts,) = call(
        masked_starts,
        "masked_starts",
        [SMEM, HBM, HBM],
        [(VMEM, pltpu.VMEM(both, BF16))],
        [pltpu.SemaphoreType.DMA((2,))],
        4 * downs * block * block,
        4 * bits,
    )(sizes, in_hbm(guess_a.reshape(pair)), in_hbm(guess_b.reshape(pair)))
    shifted, swapped = shifted_pairs(starts), swapped_pairs(starts)

    *loaded, own_images, lists = call(
        opening,
        "opening",
        [SMEM, VMEM] + [HBM] * 4,
        [(VMEM, pltpu.VMEM(env_shape, BF16))] * 4
        + [
            (VMEM, pltpu.VMEM(both, F32)),
            (SMEM, jax.ShapeDtypeStruct((CODES, channels + 1), jnp.int32)),
        ],
        [pltpu.SemaphoreType.DMA((channels,))],
        apply_flops,
        5 * env_bytes,
    )(in_hbm(term_shift), starts, *held)

    halo = pltpu.VMEM((2,) + both, BF16)
    rest, sent, along, halo_images, row = call(
        first_images,
        "first_images",
        [SMEM, SMEM] + [VMEM] * 8,
        [
            (VMEM, pltpu.VMEM(both, F32)),
            (VMEM, pltpu.VMEM(both, BF16)),
            (VMEM, pltpu.VMEM((2,) + pair, BF16)),
            (VMEM, pltpu.VMEM((2,) + both, F32)),
            (VMEM, tile),
        ],
        [halo],
        apply_flops,
        env_bytes,
    )(lists, sizes, *loaded, starts, swapped, shifted, own_images)
    shifted, swapped = shifted_pairs(sent), swapped_pairs(sent)
    from_next = from_right_segment(along)
    (row,) = call(
        local_seconds,
        "local_seconds",
        [SMEM] + [VMEM] * 10,
        [(VMEM, tile)],
        [pltpu.VMEM(both, F32)],
        apply_flops,
        env_bytes,
    )(lists, *loaded, sent, starts, rest, own_images, halo_images, row)
    (row,) = call(
        halo_seconds,
        "halo_seconds",
        [SMEM] + [VMEM] * 9,
        [(VMEM, jax.ShapeDtypeStruct((devices, 128), F32))],
        [halo, pltpu.VMEM(both, F32)],
        apply_flops,
        env_bytes,
    )(lists, *loaded, swapped, shifted, starts, rest, row)
    numbers = lax.all_to_all(row, ("seg", "blk"), 0, 0, tiled=True)
    (mixed,) = call(
        mixing,
        "mixing",
        [VMEM, VMEM, HBM],
        [(VMEM, jax.ShapeDtypeStruct(env_shape, BF16))],
        [],
        4 * channels * channels * GROUP * downs * block * block,
        2 * env_bytes,
    )(channel_mix, loaded[0], row)
    state32 = jax.ShapeDtypeStruct(pair, F32)
    ground_a, ground_b, energies, boundary = call(
        functools.partial(finish, 1.0 / block, ups),
        "finish",
        [VMEM] + [HBM] * 5,
        [
            (HBM, state32),
            (HBM, state32),
            (VMEM, jax.ShapeDtypeStruct((1, 2), F32)),
            (HBM, jax.ShapeDtypeStruct(env_shape, BF16)),
        ],
        [
            pltpu.VMEM(both, BF16),
            pltpu.VMEM(both, F32),
            pltpu.VMEM((2,) + pair, BF16),
            pltpu.VMEM(pair, BF16),
            pltpu.VMEM(env_shape, BF16),
            pltpu.VMEM(env_shape, BF16),
            pltpu.VMEM(both, F32),
            pltpu.SemaphoreType.DMA((4,)),
            pltpu.SemaphoreType.DMA((channels,)),
            pltpu.SemaphoreType.DMA((channels + BONDS,)),
        ],
        apply_flops,
        2 * env_bytes,
    )(
        numbers,
        *(in_hbm(x) for x in (starts, rest, from_next, edge_state.reshape(pair), mixed)),
    )
    return (
        ground_a.reshape(guess_a.shape),
        ground_b.reshape(guess_b.shape),
        energies,
        boundary.reshape(left_env_a.shape),
    )


def solution(mesh):
    placed = (
        P("seg", "blk", None, None, None),
        P("seg", "blk", None, None, None),
        P("seg", None, "blk", None, None, None),
        P("seg", None, "blk", None, None, None),
        P("seg", None, "blk", None, None, None),
        P("seg", None, "blk", None, None, None),
        P(),
        P(),
        P("seg", None, "blk", None),
        P("blk", None, None, None),
    )
    return jax.shard_map(
        local,
        mesh=mesh,
        in_specs=placed,
        out_specs=(
            P("seg", "blk", None, None, None),
            P("seg", "blk", None, None, None),
            P("seg", None),
            P("seg", None, "blk", None, None, None),
        ),
        check_vma=False,
    )
```

time: 518 us -> 53 us (0.10)
  the two profiles are of different devices: /device:TPU:6 before, /device:TPU:0 now
where the time goes in v2:
time: 53 us; the launch traced here: 53.1 us
  Pallas kernels  30.4 us (57%)
  starting transfers between devices  17.4 us (33%)
  waiting for transfers between devices  2.81 us (5%)
  local copies, waits for them, and re-layouts  1.64 us (3%)
  between operations  0.75 us (1%)
    ppermute x2, starting transfers between devices, swapped_pairs(): lax.ppermute(block, 'blk', [(i, i ^ 1) for i in devices if i ^ 1 in devic...  8.01 us
    pallas_call x1, Pallas kernels, local(): call(functools.partial(finish, 1.0 / block, ups), 'finish', [VMEM] + [HBM...  7.35 us
    all_to_all x1, starting transfers between devices, local(): numbers = lax.all_to_all(row, ('seg', 'blk'), 0, 0, tiled=True)  6.78 us
    pallas_call x1, Pallas kernels, local(): call(opening, 'opening', [SMEM, VMEM] + [HBM] * 4, [(VMEM, pltpu.VMEM(env...  6.18 us
    pallas_call x1, Pallas kernels, local(): call(local_seconds, 'local_seconds', [SMEM] + [VMEM] * 10, [(VMEM, tile)]...  4.8 us
    pallas_call x1, Pallas kernels, local(): call(first_images, 'first_images', [SMEM, SMEM] + [VMEM] * 8, [(VMEM, plt...  4.16 us
    pallas_call x1, Pallas kernels, local(): call(halo_seconds, 'halo_seconds', [SMEM] + [VMEM] * 9, [(VMEM, jax.Shape...  3.41 us
    all_to_all x1, waiting for transfers between devices, local(): numbers = lax.all_to_all(row, ('seg', 'blk'), 0, 0, tiled=True)  2.78 us
  transfers between devices with their start and end apart: 6, of which 1 were waited for; matrix products, arithmetic and copies ran while one was open for 0% of the time, Pallas kernels for 32%

profile of v2, /device:TPU:0, one launch (start us, length us, event | category | flops | bytes accessed | tf_op | source)
XLA Modules:
  0.0 53.1 jit_solution(12028369509470574791)
XLA Ops:
  0.6 1.9 %masked_starts.1.starts.starts_held = bf16[2,2,256,256]{3,2,1,0:T(8,128)(2,1)S(1)} custom-call(s32[1,1,2,4]{3,2,1,0:T(2,128)} %bitcast.24, bf16[2,256,256]{2,1,0:T(8,128)(2,1)} %bitcast.22, bf16[2,256,256]{2,1,0:T(8,128)(2,1)} %bitcast.23), custom_call_target="tpu_custom_call" | custom-call | flops 524288 | bytes 1048576 | tf_op jit(solution)/shard_map/masked_starts/pallas_call | solution.py:526
  2.5 0.0 copy-start
  2.5 0.7 %collective-permute-start.1 = (bf16[2,2,256,256]{3,2,1,0:T(8,128)(2,1)S(1)}, bf16[2,2,256,256]{3,2,1,0:T(8,128)(2,1)S(1)}, u32[]{:S(2)}, u32[]{:S(2)}) collective-permute-start(bf16[2,2,256,256]{3,2,1,0:T(8,128)(2,1)S(1)} %masked_starts.1.starts.starts_held), channel_id=1, source_target_pairs={{1,2},{3,4},{5,6},{2,1},{4,3},{6,5},{9,10},{11,12},{13,14},{10,9},... | collective-permute-start | bytes 1572872 | tf_op jit(solution)/shard_map/ppermute | solution.py:491
  3.2 4.4 %collective-permute-start = (bf16[2,2,256,256]{3,2,1,0:T(8,128)(2,1)S(1)}, bf16[2,2,256,256]{3,2,1,0:T(8,128)(2,1)S(1)}, u32[]{:S(2)}, u32[]{:S(2)}) collective-permute-start(bf16[2,2,256,256]{3,2,1,0:T(8,128)(2,1)S(1)} %masked_starts.1.starts.starts_held), channel_id=1, source_target_pairs={{0,1},{1,0},{2,3},{3,2},{4,5},{5,4},{6,7},{7,6},{8,9},{9,8},{10,11... | collective-permute-start | bytes 1572872 | tf_op jit(solution)/shard_map/ppermute | solution.py:485
  7.6 6.2 %opening.1 = (bf16[12,2,256,256]{3,2,1,0:T(8,128)(2,1)S(1)}, bf16[12,2,256,256]{3,2,1,0:T(8,128)(2,1)S(1)}, bf16[12,2,256,256]{3,2,1,0:T(8,128)(2,1)S(1)}, bf16[...) custom-call(s32[12]{0:T(128)} %shift.1, ...), custom_call_target="tpu_custom_call" | custom-call | flops 1610612736 | bytes 15728640 | tf_op jit(solution)/shard_map/opening/pallas_call | solution.py:537
  13.8 0.0 collective-permute-done.1.shifted
  13.8 0.0 collective-permute-done.swapped
  13.8 4.2 %first_images.1 = (f32[2,2,256,256]{3,2,1,0:T(8,128)S(1)}, bf16[2,2,256,256]{3,2,1,0:T(8,128)(2,1)S(1)}, bf16[2,2,256,256]{3,2,1,0:T(8,128)(2,1)}, f32[2,2,2,256,256]{4,3,2,1,0:T(8,128)S(1)}, f32[8,128]{1,0:T(8,128)S(1)}) custom-call(s32[5,13]{1,0:T(8,128)S(1)} %get-tuple-element.19.lists, s32[1,1,2,4]{3,2,1,0:T(2,128)} %bitcast.25, ...), custom_call_target="tpu_custom_call" | custom-call | flops 1610612736 | bytes 3145728 | tf_op jit(solution)/shard_map/first_images/pallas_call | solution.py:552
  18.0 0.0 copy-start.1
  18.0 0.7 %collective-permute-start.3 = (bf16[2,2,256,256]{3,2,1,0:T(8,128)(2,1)S(1)}, bf16[2,2,256,256]{3,2,1,0:T(8,128)(2,1)S(1)}, u32[]{:S(2)}, u32[]{:S(2)}) collective-permute-start(bf16[2,2,256,256]{3,2,1,0:T(8,128)(2,1)S(1)} %get-tuple-element.25.sent), channel_id=1, source_target_pairs={{1,2},{3,4},{5,6},{2,1},{4,3},{6,5},{9,10},{11,12},{13,14},{10,9},... | collective-permute-start | bytes 1572872 | tf_op jit(solution)/shard_map/ppermute | solution.py:491
  18.7 3.6 %collective-permute-start.2 = (bf16[2,2,256,256]{3,2,1,0:T(8,128)(2,1)S(1)}, bf16[2,2,256,256]{3,2,1,0:T(8,128)(2,1)S(1)}, u32[]{:S(2)}, u32[]{:S(2)}) collective-permute-start(bf16[2,2,256,256]{3,2,1,0:T(8,128)(2,1)S(1)} %get-tuple-element.25.sent), channel_id=1, source_target_pairs={{0,1},{1,0},{2,3},{3,2},{4,5},{5,4},{6,7},{7,6},{8,9},{9,8},{10,11... | collective-permute-start | bytes 1572872 | tf_op jit(solution)/shard_map/ppermute | solution.py:485
  22.3 1.3 %collective-permute-start.4 = (bf16[2,2,256,256]{3,2,1,0:T(8,128)(2,1)}, bf16[2,2,256,256]{3,2,1,0:T(8,128)(2,1)}, u32[]{:S(2)}, u32[]{:S(2)}) collective-permute-start(bf16[2,2,256,256]{3,2,1,0:T(8,128)(2,1)} %get-tuple-element.29), channel_id=1, source_target_pairs={{8,0},{16,8},{24,16},{9,1},{17,9},{25,17},{10,2},{18,10},{26,18},{... | collective-permute-start | bytes 1572872 | tf_op jit(solution)/shard_map/ppermute | solution.py:496
  23.6 4.8 %local_seconds.1.row_in = f32[8,128]{1,0:T(8,128)S(1)} custom-call(s32[5,13]{1,0:T(8,128)S(1)} %get-tuple-element.19.lists, bf16[12,2,256,256]{3,2,1,0:T(8,128)(2,1)S(1)} %get-tuple-element.20.left_a.env, bf16[12,2,256,256]{3,2,1,0:T(8,128)(2,1)S(1)} %get-tuple-element.21.right_a, bf16[12,2,256,256]{3,2,1,0:T(8,128)(2,1)S(1)} %get-tuple-element.22.left_b, ...), custom_call_target="tpu_custom_call" | custom-call | flops 1610612736 | bytes 3145728 | tf_op jit(solution)/shard_map/local_seconds/pallas_call | solution.py:569
  28.4 0.0 copy-start.3
  28.4 0.0 collective-permute-done.3.shifted
  28.4 0.0 collective-permute-done.2.swapped
  28.4 0.0 copy-done
  28.4 0.0 copy-done.1
  28.4 3.4 %halo_seconds.1.after = f32[32,128]{1,0:T(8,128)} custom-call(s32[5,13]{1,0:T(8,128)S(1)} %get-tuple-element.19.lists, bf16[12,2,256,256]{3,2,1,0:T(8,128)(2,1)S(1)} %get-tuple-element.20.left_a.env, bf16[12,2,256,256]{3,2,1,0:T(8,128)(2,1)S(1)} %get-tuple-element.21.right_a, bf16[12,2,256,256]{3,2,1,0:T(8,128)(2,1)S(1)} %get-tuple-element.22.left_b, ...), custom_call_target="tpu_custom_call" | custom-call | flops 1610612736 | bytes 3145728 | tf_op jit(solution)/shard_map/halo_seconds/pallas_call | solution.py:578
  31.9 6.8 %all-to-all-start = ((f32[32,1,128]{2,1,0:T(1,128)}), f32[32,1,128]{2,1,0:T(1,128)S(1)}, u32[]{:S(2)}, u32[]{:S(2)}) async-start(f32[32,1,128]{2,1,0:T(1,128)} %bitcast.8), calls=%async_computation | async-start | bytes 32768 | tf_op jit(solution)/shard_map/all_to_all | solution.py:587
  38.6 0.0 copy-done.3
  38.7 2.6 %mixing.1.mixed_held = bf16[12,2,256,256]{3,2,1,0:T(8,128)(2,1)S(1)} custom-call(f32[12,12]{1,0:T(8,128)S(1)} %copy-done.3, bf16[12,2,256,256]{3,2,1,0:T(8,128)(2,1)S(1)} %get-tuple-element.20.left_a.env, f32[32,128]{1,0:T(8,128)} %halo_seconds.1.after), custom_call_target="tpu_custom_call" | custom-call | flops 1207959552 | bytes 6291456 | tf_op jit(solution)/shard_map/mixing/pallas_call | solution.py:588
  41.3 0.0 copy-start.2
  41.3 1.6 %copy-done.2 = bf16[12,2,256,256]{3,2,1,0:T(8,128)(2,1)} copy-done((bf16[12,2,256,256]{3,2,1,0:T(8,128)(2,1)}, bf16[12,2,256,256]{3,2,1,0:T(8,128)(2,1)S(1)}, u32[]{:S(2)}) %copy-start.2) | copy-done | bytes 3145752
  42.9 0.0 collective-permute-done.4.along_held
  42.9 2.8 %all-to-all-done = f32[32,1,128]{2,1,0:T(1,128)S(1)} async-done(((f32[32,1,128]{2,1,0:T(1,128)}), f32[32,1,128]{2,1,0:T(1,128)S(1)}, u32[]{:S(2)}, u32[]{:S(2)}) %all-to-all-start) | async-done | bytes 16416 | tf_op jit(solution)/shard_map/all_to_all | solution.py:587
  45.7 7.3 %finish.1 = (f32[2,256,256]{2,1,0:T(8,128)}, f32[2,256,256]{2,1,0:T(8,128)}, f32[1,2]{1,0:T(1,128)}, bf16[12,2,256,256]{3,2,1,0:T(8,128)(2,1)}) custom-call(f32[32,128]{1,0:T(8,128)S(1)} %bitcast.17, bf16[2,2,256,256]{3,2,1,0:T(8,128)(2,1)} %copy-done, f32[2,2,256,256]{3,2,1,0:T(8,128)} %copy-done.1, ...), custom_call_target="tpu_custom_call" | custom-call | flops 1610612736 | bytes 6291456 | tf_op jit(solution)/shard_map/finish/pallas_call | solution.py:598
Async XLA Ops:
  2.5 25.9 %copy-start = (bf16[2,2,256,256]{3,2,1,0:T(8,128)(2,1)}, bf16[2,2,256,256]{3,2,1,0:T(8,128)(2,1)S(1)}, u32[]{:S(2)}) copy-start(bf16[2,2,256,256]{3,2,1,0:T(8,128)(2,1)S(1)} %masked_starts.1.starts.starts_held) | copy-start | bytes 1572868
  2.5 11.3 %collective-permute-start.1 = (bf16[2,2,256,256]{3,2,1,0:T(8,128)(2,1)S(1)}, bf16[2,2,256,256]{3,2,1,0:T(8,128)(2,1)S(1)}, u32[]{:S(2)}, u32[]{:S(2)}) collective-permute-start(bf16[2,2,256,256]{3,2,1,0:T(8,128)(2,1)S(1)} %masked_starts.1.starts.starts_held), channel_id=1, source_target_pairs={{1,2},{3,4},{5,6},{2,1},{4,3},{6,5},{9,10},{11,12},{13,14},{10,9},... | collective-permute-start | bytes 1572872 | tf_op jit(solution)/shard_map/ppermute | solution.py:491
  3.2 10.6 %collective-permute-start = (bf16[2,2,256,256]{3,2,1,0:T(8,128)(2,1)S(1)}, bf16[2,2,256,256]{3,2,1,0:T(8,128)(2,1)S(1)}, u32[]{:S(2)}, u32[]{:S(2)}) collective-permute-start(bf16[2,2,256,256]{3,2,1,0:T(8,128)(2,1)S(1)} %masked_starts.1.starts.starts_held), channel_id=1, source_target_pairs={{0,1},{1,0},{2,3},{3,2},{4,5},{5,4},{6,7},{7,6},{8,9},{9,8},{10,11... | collective-permute-start | bytes 1572872 | tf_op jit(solution)/shard_map/ppermute | solution.py:485
  18.0 10.4 %copy-start.1 = (f32[2,2,256,256]{3,2,1,0:T(8,128)}, f32[2,2,256,256]{3,2,1,0:T(8,128)S(1)}, u32[]{:S(2)}) copy-start(f32[2,2,256,256]{3,2,1,0:T(8,128)S(1)} %get-tuple-element.26.rest.rest_held) | copy-start | bytes 3145732
  18.0 10.4 %collective-permute-start.3 = (bf16[2,2,256,256]{3,2,1,0:T(8,128)(2,1)S(1)}, bf16[2,2,256,256]{3,2,1,0:T(8,128)(2,1)S(1)}, u32[]{:S(2)}, u32[]{:S(2)}) collective-permute-start(bf16[2,2,256,256]{3,2,1,0:T(8,128)(2,1)S(1)} %get-tuple-element.25.sent), channel_id=1, source_target_pairs={{1,2},{3,4},{5,6},{2,1},{4,3},{6,5},{9,10},{11,12},{13,14},{10,9},... | collective-permute-start | bytes 1572872 | tf_op jit(solution)/shard_map/ppermute | solution.py:491
  18.7 9.7 %collective-permute-start.2 = (bf16[2,2,256,256]{3,2,1,0:T(8,128)(2,1)S(1)}, bf16[2,2,256,256]{3,2,1,0:T(8,128)(2,1)S(1)}, u32[]{:S(2)}, u32[]{:S(2)}) collective-permute-start(bf16[2,2,256,256]{3,2,1,0:T(8,128)(2,1)S(1)} %get-tuple-element.25.sent), channel_id=1, source_target_pairs={{0,1},{1,0},{2,3},{3,2},{4,5},{5,4},{6,7},{7,6},{8,9},{9,8},{10,11... | collective-permute-start | bytes 1572872 | tf_op jit(solution)/shard_map/ppermute | solution.py:485
  22.3 20.6 %collective-permute-start.4 = (bf16[2,2,256,256]{3,2,1,0:T(8,128)(2,1)}, bf16[2,2,256,256]{3,2,1,0:T(8,128)(2,1)}, u32[]{:S(2)}, u32[]{:S(2)}) collective-permute-start(bf16[2,2,256,256]{3,2,1,0:T(8,128)(2,1)} %get-tuple-element.29), channel_id=1, source_target_pairs={{8,0},{16,8},{24,16},{9,1},{17,9},{25,17},{10,2},{18,10},{26,18},{... | collective-permute-start | bytes 1572872 | tf_op jit(solution)/shard_map/ppermute | solution.py:496
  28.4 10.3 %copy-start.3 = (f32[12,12]{1,0:T(8,128)S(1)}, f32[12,12]{1,0:T(8,128)}, u32[]{:S(2)}) copy-start(f32[12,12]{1,0:T(8,128)} %mix.1) | copy-start | bytes 1732
  31.9 13.9 %all-to-all-start = ((f32[32,1,128]{2,1,0:T(1,128)}), f32[32,1,128]{2,1,0:T(1,128)S(1)}, u32[]{:S(2)}, u32[]{:S(2)}) async-start(f32[32,1,128]{2,1,0:T(1,128)} %bitcast.8), calls=%async_computation | async-start | bytes 32768 | tf_op jit(solution)/shard_map/all_to_all | solution.py:587
  41.3 1.6 %copy-start.2 = (bf16[12,2,256,256]{3,2,1,0:T(8,128)(2,1)}, bf16[12,2,256,256]{3,2,1,0:T(8,128)(2,1)S(1)}, u32[]{:S(2)}) copy-start(bf16[12,2,256,256]{3,2,1,0:T(8,128)(2,1)S(1)} %mixing.1.mixed_held) | copy-start | bytes 9437188

commit v3 on v2

--- a/solution.py
+++ b/solution.py
@@ -17,6 +17,7 @@
 BATCH = 3
 BONDS = 2
 CODES = 5
+HALO_CHANNELS, HALO_KINDS = CODES, CODES + 1
 
 (
     SIZE,
@@ -85,21 +86,26 @@
     return row
 
 
-def masked_starts(sizes, guess_a, guess_b, starts, sems):
+def masked_starts(sizes_held, guess_a, guess_b, starts, sizes, size_sem, sems):
+    sizes_copy = pltpu.make_async_copy(sizes_held, sizes, size_sem)
+    sizes_copy.start()
+    downs, block = starts.shape[1], starts.shape[-1]
+    places = [(bond, down) for bond in range(BONDS) for down in range(downs)]
     copies = [
-        pltpu.make_async_copy(guess, starts.at[bond], sems.at[bond])
-        for bond, guess in enumerate((guess_a, guess_b))
+        pltpu.make_async_copy(
+            (guess_a, guess_b)[bond].at[down], starts.at[bond, down], sems.at[bond, down]
+        )
+        for bond, down in places
     ]
     for copy in copies:
         copy.start()
-    downs, block = starts.shape[1], starts.shape[-1]
-    for bond in range(BONDS):
-        copies[bond].wait()
-        for down in range(downs):
-            start = starts[bond, down]
-            starts[bond, down] = jnp.where(
-                live_of(sizes, bond, down, block), start, jnp.zeros_like(start)
-            )
+    sizes_copy.wait()
+    for copy, (bond, down) in zip(copies, places):
+        copy.wait()
+        start = starts[bond, down]
+        starts[bond, down] = jnp.where(
+            live_of(sizes, bond, down, block), start, jnp.zeros_like(start)
+        )
 
 
 def list_channels(shift, lists):
@@ -110,6 +116,13 @@
             lists[code, count] = jnp.int32(channel)
             count = count + (shift[channel] == code).astype(jnp.int32)
         lists[code, channels] = count
+    count = jnp.int32(0)
+    for channel in range(channels):
+        code = shift[channel]
+        lists[HALO_CHANNELS, count] = jnp.int32(channel)
+        lists[HALO_KINDS, count] = (code == 2).astype(jnp.int32)
+        count = count + ((code == 1) | (code == 2)).astype(jnp.int32)
+    lists[HALO_CHANNELS, channels] = count
 
 
 def add_images(lists, code, lefts, rights, sources, sums, arrived=None):
@@ -151,16 +164,45 @@
     add_images(lists, 4, lefts, rights, above, sums, arrived)
 
 
-def add_halo_images(lists, lefts, rights, swapped, shifted, halo, sums_low, sums_high):
+def add_halo_images(lists, lefts, rights, swapped, shifted, halo, sums, parted, lists_copy):
     even = lax.rem(lax.axis_index("blk"), 2) == 0
+    channels = lefts[0].shape[0]
     downs = swapped.shape[1]
-    for bond in range(BONDS):
-        for down in range(downs):
-            one, other = swapped[bond, down], shifted[bond, down]
-            halo[0, bond, down] = jnp.where(even, other, one)
-            halo[1, bond, down] = jnp.where(even, one, other)
-    add_images(lists, 1, lefts, rights, lambda bond, down: halo.at[0, bond, down], sums_low)
-    add_images(lists, 2, lefts, rights, lambda bond, down: halo.at[1, bond, down], sums_high)
+    units = [(bond, down) for bond in range(BONDS) for down in range(downs)]
+    for bond, down in units:
+        one, other = swapped[bond, down], shifted[bond, down]
+        halo[0, bond, down] = jnp.where(even, other, one)
+        halo[1, bond, down] = jnp.where(even, one, other)
+    lists_copy.wait()
+
+    def images(indices):
+        halves = []
+        for index in indices:
+            channel, kind = lists[HALO_CHANNELS, index], lists[HALO_KINDS, index]
+            halves.append(
+                [
+                    dot(lefts[bond][channel, down], halo[kind, bond, down]).astype(BF16)
+                    for bond, down in units
+                ]
+            )
+        for index, half_steps in zip(indices, halves):
+            channel, kind = lists[HALO_CHANNELS, index], lists[HALO_KINDS, index]
+            target = sums.at[kind] if parted else sums
+            for (bond, down), half in zip(units, half_steps):
+                target[bond, down] += dot_by_rows(half, rights[bond][channel, down])
+
+    def two(index, carry):
+        images([2 * index, 2 * index + 1])
+        return carry
+
+    def one_left(index, carry):
+        images([index])
+        return carry
+
+    count = lists[HALO_CHANNELS, channels]
+    odd = lax.rem(count, 2)
+    lax.fori_loop(0, lax.div(count, 2), two, 0)
+    lax.fori_loop(count - odd, count, one_left, 0)
 
 
 def opening(shift, starts, *refs):
@@ -225,8 +267,8 @@
 
 
 def first_images(
-    lists,
-    sizes,
+    lists_held,
+    sizes_held,
     left_a,
     right_a,
     left_b,
@@ -237,11 +279,17 @@
     own_images,
     rest,
     sent,
-    along,
     halo_images,
     row,
     halo,
+    lists,
+    sizes,
+    sems,
 ):
+    lists_copy = pltpu.make_async_copy(lists_held, lists, sems.at[0])
+    lists_copy.start()
+    sizes_copy = pltpu.make_async_copy(sizes_held, sizes, sems.at[1])
+    sizes_copy.start()
     downs, block = left_a.shape[1], left_a.shape[-1]
     halo_images[...] = jnp.zeros_like(halo_images)
     add_halo_images(
@@ -251,9 +299,11 @@
         swapped,
         shifted,
         halo,
-        halo_images.at[0],
-        halo_images.at[1],
-    )
+        halo_images,
+        True,
+        lists_copy,
+    )
+    sizes_copy.wait()
     found = []
     for bond in range(BONDS):
         size = jnp.zeros((1, 1), F32)
@@ -272,8 +322,6 @@
             sent[bond, down] = left_over.astype(BF16)
         offset = bond * BOND_LANES
         found += [(offset + SIZE, size), (offset + QUOTIENT, quotient)]
-    along[0] = starts[BONDS - 1]
-    along[1] = sent[BONDS - 1]
     row[...] = jnp.broadcast_to(in_lanes(row.shape[1], found), row.shape)
 
 
@@ -290,9 +338,17 @@
     halo_images,
     row_in,
     row,
+    along,
     sums,
+    sems,
 ):
     downs = left_a.shape[1]
+    copies = [
+        pltpu.make_async_copy(source.at[BONDS - 1], along.at[index], sems.at[index])
+        for index, source in enumerate((starts, sent))
+    ]
+    for copy in copies:
+        copy.start()
     sums[...] = jnp.zeros_like(sums)
     add_local_images(lists, (left_a, left_b), (right_a, right_b), sent, sums)
     found = []
@@ -311,10 +367,12 @@
         offset = bond * BOND_LANES
         found += [(offset + place, numbers[place]) for place in sorted(numbers)]
     row[...] = row_in[...] + jnp.broadcast_to(in_lanes(row.shape[1], found), row.shape)
+    for copy in copies:
+        copy.wait()
 
 
 def halo_seconds(
-    lists,
+    lists_held,
     left_a,
     right_a,
     left_b,
@@ -327,11 +385,23 @@
     row,
     halo,
     sums,
+    lists,
+    lists_sem,
 ):
+    lists_copy = pltpu.make_async_copy(lists_held, lists, lists_sem)
+    lists_copy.start()
     downs = left_a.shape[1]
     sums[...] = jnp.zeros_like(sums)
     add_halo_images(
-        lists, (left_a, left_b), (right_a, right_b), swapped, shifted, halo, sums, sums
+        lists,
+        (left_a, left_b),
+        (right_a, right_b),
+        swapped,
+        shifted,
+        halo,
+        sums,
+        False,
+        lists_copy,
     )
     found = []
     for bond in range(BONDS):
@@ -388,8 +458,9 @@
     mixed_held,
     ground_a,
     ground_b,
+    energies_out,
+    boundary,
     energies,
-    boundary,
     starts,
     rest,
     along,
@@ -402,16 +473,29 @@
     out_sems,
 ):
     channels, downs = mixed.shape[0], mixed.shape[1]
-    held = ((starts_held, starts), (rest_held, rest), (along_held, along), (edge_held, edge))
+
+    def arrival(index, source, target):
+        copy = pltpu.make_async_copy(source, target, in_sems.at[index])
+        copy.start()
+        return copy
+
+    first = [
+        arrival(0, starts_held.at[0], starts.at[0]),
+        arrival(1, rest_held.at[0], rest.at[0]),
+        arrival(2, along_held, along),
+        arrival(3, edge_held, edge),
+    ]
     arrivals = [
-        pltpu.make_async_copy(source, target, in_sems.at[index])
-        for index, (source, target) in enumerate(held)
-    ]
-    arrivals += [
         pltpu.make_async_copy(mixed_held.at[index], mixed.at[index], mixed_sems.at[index])
         for index in range(channels)
     ]
-    for copy in arrivals:
+    for copy in arrivals[: 2 * BATCH]:
+        copy.start()
+    second = [
+        arrival(4, starts_held.at[1], starts.at[1]),
+        arrival(5, rest_held.at[1], rest.at[1]),
+    ]
+    for copy in arrivals[2 * BATCH :]:
         copy.start()
     segments = numbers.shape[0] // ups
     seg, blk = lax.axis_index("seg"), lax.axis_index("blk")
@@ -433,26 +517,32 @@
     lane = lax.broadcasted_iota(jnp.int32, energies.shape, 1)
     energies[...] = jnp.where(lane == 0, energy[0], energy[1])
     last = seg == segments - 1
-    for copy in arrivals[:2]:
-        copy.wait()
-    for bond in range(BONDS):
+    out_copies = [pltpu.make_async_copy(energies, energies_out, in_sems.at[6])]
+    out_copies[0].start()
+
+    def leave(index, source, target):
+        copy = pltpu.make_async_copy(source, target, out_sems.at[index])
+        copy.start()
+        out_copies.append(copy)
+
+    def ground_of(bond, target):
         for down in range(downs):
             start = starts[bond, down].astype(F32)
             grounds[bond, down] = of_start[bond] * start + of_rest[bond] * rest[bond, down]
-    copies = [
-        pltpu.make_async_copy(grounds.at[bond], target, out_sems.at[channels + bond])
-        for bond, target in enumerate((ground_a, ground_b))
-    ]
-    for copy in copies:
-        copy.start()
-    for copy in arrivals[2:4]:
+        leave(channels + bond, grounds.at[bond], target)
+
+    for copy in first:
         copy.wait()
     products = []
     for down in range(downs):
+        start = starts[0, down].astype(F32)
+        ground = of_start[0] * start + of_rest[0] * rest[0, down]
+        grounds[0, down] = ground
         found = of_start[2] * along[0, down].astype(F32) + of_rest[2] * along[1, down].astype(F32)
         state = jnp.where(last, edge[down], found.astype(BF16))
-        product = dot(grounds[0, down].astype(BF16), state) * factor
-        products.append((product.astype(BF16), product.T.astype(BF16)))
+        product = (dot(ground.astype(BF16), state) * factor).astype(BF16)
+        products.append((product, product.T))
+    leave(channels, grounds.at[0], ground_a)
     halves = {}
 
     def last_product(group):
@@ -460,23 +550,23 @@
             for down, (_, turned) in enumerate(products):
                 made[channel, down] = dot(turned, halves[channel, down]).astype(BF16)
         for channel in group:
-            copy = pltpu.make_async_copy(
-                made.at[channel], boundary.at[channel], out_sems.at[channel]
-            )
-            copy.start()
-            copies.append(copy)
+            leave(channel, made.at[channel], boundary.at[channel])
 
     groups = [range(i, min(i + BATCH, channels)) for i in range(0, channels, BATCH)]
     for index, group in enumerate(groups):
         for channel in group:
-            arrivals[4 + channel].wait()
+            arrivals[channel].wait()
         for channel in group:
             for down, (product, _) in enumerate(products):
                 halves[channel, down] = dot(mixed[channel, down], product).astype(BF16)
         if index > 0:
             last_product(groups[index - 1])
+        if index == min(1, len(groups) - 1):
+            for copy in second:
+                copy.wait()
+            ground_of(1, ground_b)
     last_product(groups[-1])
-    for copy in copies:
+    for copy in out_copies:
         copy.wait()
 
 
@@ -526,9 +616,9 @@
     (starts,) = call(
         masked_starts,
         "masked_starts",
-        [SMEM, HBM, HBM],
+        [HBM, HBM, HBM],
         [(VMEM, pltpu.VMEM(both, BF16))],
-        [pltpu.SemaphoreType.DMA((2,))],
+        [pltpu.SMEM(sizes.shape, jnp.int32), pltpu.SemaphoreType.DMA(()), pltpu.SemaphoreType.DMA((BONDS, downs))],
         4 * downs * block * block,
         4 * bits,
     )(sizes, in_hbm(guess_a.reshape(pair)), in_hbm(guess_b.reshape(pair)))
@@ -541,7 +631,7 @@
         [(VMEM, pltpu.VMEM(env_shape, BF16))] * 4
         + [
             (VMEM, pltpu.VMEM(both, F32)),
-            (SMEM, jax.ShapeDtypeStruct((CODES, channels + 1), jnp.int32)),
+            (SMEM, jax.ShapeDtypeStruct((CODES + 2, channels + 1), jnp.int32)),
         ],
         [pltpu.SemaphoreType.DMA((channels,))],
         apply_flops,
@@ -549,38 +639,47 @@
     )(in_hbm(term_shift), starts, *held)
 
     halo = pltpu.VMEM((2,) + both, BF16)
-    rest, sent, along, halo_images, row = call(
+    rest, sent, halo_images, row = call(
         first_images,
         "first_images",
-        [SMEM, SMEM] + [VMEM] * 8,
+        [VMEM, HBM] + [VMEM] * 8,
         [
             (VMEM, pltpu.VMEM(both, F32)),
             (VMEM, pltpu.VMEM(both, BF16)),
-            (VMEM, pltpu.VMEM((2,) + pair, BF16)),
             (VMEM, pltpu.VMEM((2,) + both, F32)),
             (VMEM, tile),
         ],
-        [halo],
+        [
+            halo,
+            pltpu.SMEM(lists.shape, jnp.int32),
+            pltpu.SMEM(sizes.shape, jnp.int32),
+            pltpu.SemaphoreType.DMA((2,)),
+        ],
         apply_flops,
         env_bytes,
     )(lists, sizes, *loaded, starts, swapped, shifted, own_images)
     shifted, swapped = shifted_pairs(sent), swapped_pairs(sent)
-    from_next = from_right_segment(along)
-    (row,) = call(
+    row, along = call(
         local_seconds,
         "local_seconds",
         [SMEM] + [VMEM] * 10,
-        [(VMEM, tile)],
-        [pltpu.VMEM(both, F32)],
+        [(VMEM, tile), (HBM, jax.ShapeDtypeStruct((2,) + pair, BF16))],
+        [pltpu.VMEM(both, F32), pltpu.SemaphoreType.DMA((2,))],
         apply_flops,
         env_bytes,
     )(lists, *loaded, sent, starts, rest, own_images, halo_images, row)
+    from_next = from_right_segment(along)
     (row,) = call(
         halo_seconds,
         "halo_seconds",
-        [SMEM] + [VMEM] * 9,
-        [(VMEM, jax.ShapeDtypeStruct((devices, 128), F32))],
-        [halo, pltpu.VMEM(both, F32)],
+        [VMEM] + [VMEM] * 9,
+        [(VMEM, pltpu.VMEM((devices, 128), F32))],
+        [
+            halo,
+            pltpu.VMEM(both, F32),
+            pltpu.SMEM(lists.shape, jnp.int32),
+            pltpu.SemaphoreType.DMA(()),
+        ],
         apply_flops,
         env_bytes,
     )(lists, *loaded, swapped, shifted, starts, rest, row)
@@ -602,10 +701,11 @@
         [
             (HBM, state32),
             (HBM, state32),
-            (VMEM, jax.ShapeDtypeStruct((1, 2), F32)),
+            (HBM, jax.ShapeDtypeStruct((1, 2), F32)),
             (HBM, jax.ShapeDtypeStruct(env_shape, BF16)),
         ],
         [
+            pltpu.VMEM((1, 2), F32),
             pltpu.VMEM(both, BF16),
             pltpu.VMEM(both, F32),
             pltpu.VMEM((2,) + pair, BF16),
@@ -613,7 +713,7 @@
             pltpu.VMEM(env_shape, BF16),
             pltpu.VMEM(env_shape, BF16),
             pltpu.VMEM(both, F32),
-            pltpu.SemaphoreType.DMA((4,)),
+            pltpu.SemaphoreType.DMA((7,)),
             pltpu.SemaphoreType.DMA((channels,)),
             pltpu.SemaphoreType.DMA((channels + BONDS,)),
         ],

time: 53 us -> 51.5 us (0.972); the launches traced: 53.1 us -> 50.8 us
  Pallas kernels: 30.4 us -> 27.6 us
  starting transfers between devices: 17.4 us -> 18.1 us
    pallas_call x4, Pallas kernels: 14.2 us -> 12.5 us  [the longest x1 4.1 us: local(): call(local_seconds, 'local_seconds', [SMEM] + [VMEM] * 10, [(VMEM, tile),...]
    pallas_call x1, Pallas kernels: 7.35 us -> 6.25 us  [local(): call(functools.partial(finish, 1.0 / block, ups), 'finish', [VMEM] + [HBM...]
    all_to_all x1, starting transfers between devices: 6.78 us -> 7.43 us  [local(): numbers = lax.all_to_all(row, ('seg', 'blk'), 0, 0, tiled=True)]
  transfers between devices with their start and end apart: 6 -> 6, of which waited for: 1 -> 1; matrix products, arithmetic and copies ran while one was open for 0% -> 0% of each run, Pallas kernels for 32% -> 33%
where the time goes in v3:
time: 51.5 us; the launch traced here: 50.8 us
  Pallas kernels  27.6 us (54%)
  starting transfers between devices  18.1 us (35%)
  waiting for transfers between devices  2.61 us (5%)
  local copies, waits for them, and re-layouts  1.64 us (3%)
  between operations  0.96 us (2%)
    ppermute x2, starting transfers between devices, swapped_pairs(): lax.ppermute(block, 'blk', [(i, i ^ 1) for i in devices if i ^ 1 in devic...  7.95 us
    all_to_all x1, starting transfers between devices, local(): numbers = lax.all_to_all(row, ('seg', 'blk'), 0, 0, tiled=True)  7.43 us
    pallas_call x1, Pallas kernels, local(): call(functools.partial(finish, 1.0 / block, ups), 'finish', [VMEM] + [HBM...  6.25 us
    pallas_call x1, Pallas kernels, local(): call(opening, 'opening', [SMEM, VMEM] + [HBM] * 4, [(VMEM, pltpu.VMEM(env...  6.24 us
    pallas_call x1, Pallas kernels, local(): call(local_seconds, 'local_seconds', [SMEM] + [VMEM] * 10, [(VMEM, tile),...  4.1 us
    pallas_call x1, Pallas kernels, local(): call(halo_seconds, 'halo_seconds', [VMEM] + [VMEM] * 9, [(VMEM, pltpu.VME...  3.66 us
    pallas_call x1, Pallas kernels, local(): call(first_images, 'first_images', [VMEM, HBM] + [VMEM] * 8, [(VMEM, pltp...  3.5 us
    pallas_call x1, Pallas kernels, local(): call(mixing, 'mixing', [VMEM, VMEM, HBM], [(VMEM, jax.ShapeDtypeStruct(en...  2.64 us
  transfers between devices with their start and end apart: 6, of which 1 were waited for; matrix products, arithmetic and copies ran while one was open for 0% of the time, Pallas kernels for 33%

profile of v3, /device:TPU:0, one launch (start us, length us, event | category | flops | bytes accessed | tf_op | source)
XLA Modules:
  0.0 50.8 jit_solution(4207247243294271117)
XLA Ops:
  0.6 1.2 %masked_starts.1.starts.starts_held = bf16[2,2,256,256]{3,2,1,0:T(8,128)(2,1)S(1)} custom-call(s32[1,1,2,4]{3,2,1,0:T(2,128)} %bitcast.24, bf16[2,256,256]{2,1,0:T(8,128)(2,1)} %bitcast.22, bf16[2,256,256]{2,1,0:T(8,128)(2,1)} %bitcast.23), custom_call_target="tpu_custom_call" | custom-call | flops 524288 | bytes 1048576 | tf_op jit(solution)/shard_map/masked_starts/pallas_call | solution.py:616
  1.8 0.0 copy-start
  1.8 0.7 %collective-permute-start.1 = (bf16[2,2,256,256]{3,2,1,0:T(8,128)(2,1)S(1)}, bf16[2,2,256,256]{3,2,1,0:T(8,128)(2,1)S(1)}, u32[]{:S(2)}, u32[]{:S(2)}) collective-permute-start(bf16[2,2,256,256]{3,2,1,0:T(8,128)(2,1)S(1)} %masked_starts.1.starts.starts_held), channel_id=1, source_target_pairs={{1,2},{3,4},{5,6},{2,1},{4,3},{6,5},{9,10},{11,12},{13,14},{10,9},... | collective-permute-start | bytes 1572872 | tf_op jit(solution)/shard_map/ppermute | solution.py:581
  2.5 4.4 %collective-permute-start = (bf16[2,2,256,256]{3,2,1,0:T(8,128)(2,1)S(1)}, bf16[2,2,256,256]{3,2,1,0:T(8,128)(2,1)S(1)}, u32[]{:S(2)}, u32[]{:S(2)}) collective-permute-start(bf16[2,2,256,256]{3,2,1,0:T(8,128)(2,1)S(1)} %masked_starts.1.starts.starts_held), channel_id=1, source_target_pairs={{0,1},{1,0},{2,3},{3,2},{4,5},{5,4},{6,7},{7,6},{8,9},{9,8},{10,11... | collective-permute-start | bytes 1572872 | tf_op jit(solution)/shard_map/ppermute | solution.py:575
  7.0 6.2 %opening.1 = (bf16[12,2,256,256]{3,2,1,0:T(8,128)(2,1)S(1)}, bf16[12,2,256,256]{3,2,1,0:T(8,128)(2,1)S(1)}, bf16[12,2,256,256]{3,2,1,0:T(8,128)(2,1)S(1)}, bf16[...) custom-call(s32[12]{0:T(128)} %shift.1, ...), custom_call_target="tpu_custom_call" | custom-call | flops 1610612736 | bytes 15728640 | tf_op jit(solution)/shard_map/opening/pallas_call | solution.py:627
  13.2 0.0 collective-permute-done.1.shifted
  13.2 0.0 collective-permute-done.swapped
  13.2 3.5 %first_images.1 = (f32[2,2,256,256]{3,2,1,0:T(8,128)S(1)}, bf16[2,2,256,256]{3,2,1,0:T(8,128)(2,1)S(1)}, f32[2,2,2,256,256]{4,3,2,1,0:T(8,128)S(1)}, f32[8,128]{1,0:T(8,128)S(1)}) custom-call(s32[7,13]{1,0:T(8,128)S(1)} %get-tuple-element.20.lists_held.lists, s32[1,1,2,4]{3,2,1,0:T(2,128)} %bitcast.25, ...), custom_call_target="tpu_custom_call" | custom-call | flops 1610612736 | bytes 3145728 | tf_op jit(solution)/shard_map/first_images/pallas_call | solution.py:642
  16.7 0.0 copy-start.1
  16.8 0.7 %collective-permute-start.3 = (bf16[2,2,256,256]{3,2,1,0:T(8,128)(2,1)S(1)}, bf16[2,2,256,256]{3,2,1,0:T(8,128)(2,1)S(1)}, u32[]{:S(2)}, u32[]{:S(2)}) collective-permute-start(bf16[2,2,256,256]{3,2,1,0:T(8,128)(2,1)S(1)} %get-tuple-element.26.sent), channel_id=1, source_target_pairs={{1,2},{3,4},{5,6},{2,1},{4,3},{6,5},{9,10},{11,12},{13,14},{10,9},... | collective-permute-start | bytes 1572872 | tf_op jit(solution)/shard_map/ppermute | solution.py:581
  17.5 3.5 %collective-permute-start.2 = (bf16[2,2,256,256]{3,2,1,0:T(8,128)(2,1)S(1)}, bf16[2,2,256,256]{3,2,1,0:T(8,128)(2,1)S(1)}, u32[]{:S(2)}, u32[]{:S(2)}) collective-permute-start(bf16[2,2,256,256]{3,2,1,0:T(8,128)(2,1)S(1)} %get-tuple-element.26.sent), channel_id=1, source_target_pairs={{0,1},{1,0},{2,3},{3,2},{4,5},{5,4},{6,7},{7,6},{8,9},{9,8},{10,11... | collective-permute-start | bytes 1572872 | tf_op jit(solution)/shard_map/ppermute | solution.py:575
  21.0 4.1 %local_seconds.1 = (f32[8,128]{1,0:T(8,128)S(1)}, bf16[2,2,256,256]{3,2,1,0:T(8,128)(2,1)}) custom-call(s32[7,13]{1,0:T(8,128)S(1)} %get-tuple-element.20.lists_held.lists, bf16[12,2,256,256]{3,2,1,0:T(8,128)(2,1)S(1)} %get-tuple-element.21.left_a.env, bf16[12,2,256,256]{3,2,1,0:T(8,128)(2,1)S(1)} %get-tuple-element.22.right_a, ...), custom_call_target="tpu_custom_call" | custom-call | flops 1610612736 | bytes 3145728 | tf_op jit(solution)/shard_map/local_seconds/pallas_call | solution.py:662
  25.1 1.3 %collective-permute-start.4 = (bf16[2,2,256,256]{3,2,1,0:T(8,128)(2,1)}, bf16[2,2,256,256]{3,2,1,0:T(8,128)(2,1)}, u32[]{:S(2)}, u32[]{:S(2)}) collective-permute-start(bf16[2,2,256,256]{3,2,1,0:T(8,128)(2,1)} %get-tuple-element.31), channel_id=1, source_target_pairs={{8,0},{16,8},{24,16},{9,1},{17,9},{25,17},{10,2},{18,10},{26,18},{... | collective-permute-start | bytes 1572872 | tf_op jit(solution)/shard_map/ppermute | solution.py:586
  26.4 0.0 collective-permute-done.3.shifted
  26.4 0.0 collective-permute-done.2.swapped
  26.4 0.0 copy-done
  26.4 0.0 copy-done.1
  26.4 0.0 copy-start.3
  26.4 3.7 %halo_seconds.1.after = f32[32,128]{1,0:T(8,128)} custom-call(s32[7,13]{1,0:T(8,128)S(1)} %get-tuple-element.20.lists_held.lists, bf16[12,2,256,256]{3,2,1,0:T(8,128)(2,1)S(1)} %get-tuple-element.21.left_a.env, bf16[12,2,256,256]{3,2,1,0:T(8,128)(2,1)S(1)} %get-tuple-element.22.right_a, bf16[12,2,256,256]{3,2,1,0:T(8,128)(2,1)S(1)} %get-tuple-element.23.left_b, ...), custom_call_target="tpu_custom_call" | custom-call | flops 1610612736 | bytes 3145728 | tf_op jit(solution)/shard_map/halo_seconds/pallas_call | solution.py:672
  30.1 7.4 %all-to-all-start = ((f32[32,1,128]{2,1,0:T(1,128)}), f32[32,1,128]{2,1,0:T(1,128)S(1)}, u32[]{:S(2)}, u32[]{:S(2)}) async-start(f32[32,1,128]{2,1,0:T(1,128)} %bitcast.8), calls=%async_computation | async-start | bytes 32768 | tf_op jit(solution)/shard_map/all_to_all | solution.py:686
  37.5 0.0 copy-done.3
  37.6 2.6 %mixing.1.mixed_held = bf16[12,2,256,256]{3,2,1,0:T(8,128)(2,1)S(1)} custom-call(f32[12,12]{1,0:T(8,128)S(1)} %copy-done.3, bf16[12,2,256,256]{3,2,1,0:T(8,128)(2,1)S(1)} %get-tuple-element.21.left_a.env, f32[32,128]{1,0:T(8,128)} %halo_seconds.1.after), custom_call_target="tpu_custom_call" | custom-call | flops 1207959552 | bytes 6291456 | tf_op jit(solution)/shard_map/mixing/pallas_call | solution.py:687
  40.2 0.0 copy-start.2
  40.2 1.6 %copy-done.2 = bf16[12,2,256,256]{3,2,1,0:T(8,128)(2,1)} copy-done((bf16[12,2,256,256]{3,2,1,0:T(8,128)(2,1)}, bf16[12,2,256,256]{3,2,1,0:T(8,128)(2,1)S(1)}, u32[]{:S(2)}) %copy-start.2) | copy-done | bytes 3145752
  41.8 0.0 collective-permute-done.4.along_held
  41.8 2.6 %all-to-all-done = f32[32,1,128]{2,1,0:T(1,128)S(1)} async-done(((f32[32,1,128]{2,1,0:T(1,128)}), f32[32,1,128]{2,1,0:T(1,128)S(1)}, u32[]{:S(2)}, u32[]{:S(2)}) %all-to-all-start) | async-done | bytes 16416 | tf_op jit(solution)/shard_map/all_to_all | solution.py:686
  44.4 6.2 %finish.1 = (f32[2,256,256]{2,1,0:T(8,128)}, f32[2,256,256]{2,1,0:T(8,128)}, f32[1,2]{1,0:T(1,128)}, bf16[12,2,256,256]{3,2,1,0:T(8,128)(2,1)}) custom-call(f32[32,128]{1,0:T(8,128)S(1)} %bitcast.17, bf16[2,2,256,256]{3,2,1,0:T(8,128)(2,1)} %copy-done, f32[2,2,256,256]{3,2,1,0:T(8,128)} %copy-done.1, ...), custom_call_target="tpu_custom_call" | custom-call | flops 1610612736 | bytes 6291456 | tf_op jit(solution)/shard_map/finish/pallas_call | solution.py:697
Async XLA Ops:
  1.8 24.6 %copy-start = (bf16[2,2,256,256]{3,2,1,0:T(8,128)(2,1)}, bf16[2,2,256,256]{3,2,1,0:T(8,128)(2,1)S(1)}, u32[]{:S(2)}) copy-start(bf16[2,2,256,256]{3,2,1,0:T(8,128)(2,1)S(1)} %masked_starts.1.starts.starts_held) | copy-start | bytes 1572868
  1.8 11.4 %collective-permute-start.1 = (bf16[2,2,256,256]{3,2,1,0:T(8,128)(2,1)S(1)}, bf16[2,2,256,256]{3,2,1,0:T(8,128)(2,1)S(1)}, u32[]{:S(2)}, u32[]{:S(2)}) collective-permute-start(bf16[2,2,256,256]{3,2,1,0:T(8,128)(2,1)S(1)} %masked_starts.1.starts.starts_held), channel_id=1, source_target_pairs={{1,2},{3,4},{5,6},{2,1},{4,3},{6,5},{9,10},{11,12},{13,14},{10,9},... | collective-permute-start | bytes 1572872 | tf_op jit(solution)/shard_map/ppermute | solution.py:581
  2.5 10.7 %collective-permute-start = (bf16[2,2,256,256]{3,2,1,0:T(8,128)(2,1)S(1)}, bf16[2,2,256,256]{3,2,1,0:T(8,128)(2,1)S(1)}, u32[]{:S(2)}, u32[]{:S(2)}) collective-permute-start(bf16[2,2,256,256]{3,2,1,0:T(8,128)(2,1)S(1)} %masked_starts.1.starts.starts_held), channel_id=1, source_target_pairs={{0,1},{1,0},{2,3},{3,2},{4,5},{5,4},{6,7},{7,6},{8,9},{9,8},{10,11... | collective-permute-start | bytes 1572872 | tf_op jit(solution)/shard_map/ppermute | solution.py:575
  16.7 9.7 %copy-start.1 = (f32[2,2,256,256]{3,2,1,0:T(8,128)}, f32[2,2,256,256]{3,2,1,0:T(8,128)S(1)}, u32[]{:S(2)}) copy-start(f32[2,2,256,256]{3,2,1,0:T(8,128)S(1)} %get-tuple-element.27.rest.rest_held) | copy-start | bytes 3145732
  16.8 9.6 %collective-permute-start.3 = (bf16[2,2,256,256]{3,2,1,0:T(8,128)(2,1)S(1)}, bf16[2,2,256,256]{3,2,1,0:T(8,128)(2,1)S(1)}, u32[]{:S(2)}, u32[]{:S(2)}) collective-permute-start(bf16[2,2,256,256]{3,2,1,0:T(8,128)(2,1)S(1)} %get-tuple-element.26.sent), channel_id=1, source_target_pairs={{1,2},{3,4},{5,6},{2,1},{4,3},{6,5},{9,10},{11,12},{13,14},{10,9},... | collective-permute-start | bytes 1572872 | tf_op jit(solution)/shard_map/ppermute | solution.py:581
  17.5 9.0 %collective-permute-start.2 = (bf16[2,2,256,256]{3,2,1,0:T(8,128)(2,1)S(1)}, bf16[2,2,256,256]{3,2,1,0:T(8,128)(2,1)S(1)}, u32[]{:S(2)}, u32[]{:S(2)}) collective-permute-start(bf16[2,2,256,256]{3,2,1,0:T(8,128)(2,1)S(1)} %get-tuple-element.26.sent), channel_id=1, source_target_pairs={{0,1},{1,0},{2,3},{3,2},{4,5},{5,4},{6,7},{7,6},{8,9},{9,8},{10,11... | collective-permute-start | bytes 1572872 | tf_op jit(solution)/shard_map/ppermute | solution.py:575
  25.1 16.7 %collective-permute-start.4 = (bf16[2,2,256,256]{3,2,1,0:T(8,128)(2,1)}, bf16[2,2,256,256]{3,2,1,0:T(8,128)(2,1)}, u32[]{:S(2)}, u32[]{:S(2)}) collective-permute-start(bf16[2,2,256,256]{3,2,1,0:T(8,128)(2,1)} %get-tuple-element.31), channel_id=1, source_target_pairs={{8,0},{16,8},{24,16},{9,1},{17,9},{25,17},{10,2},{18,10},{26,18},{... | collective-permute-start | bytes 1572872 | tf_op jit(solution)/shard_map/ppermute | solution.py:586
  26.4 11.1 %copy-start.3 = (f32[12,12]{1,0:T(8,128)S(1)}, f32[12,12]{1,0:T(8,128)}, u32[]{:S(2)}) copy-start(f32[12,12]{1,0:T(8,128)} %mix.1) | copy-start | bytes 1732
  30.1 14.3 %all-to-all-start = ((f32[32,1,128]{2,1,0:T(1,128)}), f32[32,1,128]{2,1,0:T(1,128)S(1)}, u32[]{:S(2)}, u32[]{:S(2)}) async-start(f32[32,1,128]{2,1,0:T(1,128)} %bitcast.8), calls=%async_computation | async-start | bytes 32768 | tf_op jit(solution)/shard_map/all_to_all | solution.py:686
  40.2 1.6 %copy-start.2 = (bf16[12,2,256,256]{3,2,1,0:T(8,128)(2,1)}, bf16[12,2,256,256]{3,2,1,0:T(8,128)(2,1)S(1)}, u32[]{:S(2)}) copy-start(bf16[12,2,256,256]{3,2,1,0:T(8,128)(2,1)S(1)} %mixing.1.mixed_held) | copy-start | bytes 9437188

commit v4 on v3

--- a/solution.py
+++ b/solution.py
@@ -14,10 +14,13 @@
 HBM = pl.BlockSpec(memory_space=pltpu.HBM)
 MIB = 1 << 20
 GROUP = 16
-BATCH = 3
+BATCH = 4
 BONDS = 2
-CODES = 5
-HALO_CHANNELS, HALO_KINDS = CODES, CODES + 1
+
+CHANNEL, KIND, DOWN, SOURCE, OPENS = range(5)
+EARLY, LATE = 0, OPENS + 1
+LIST_ROWS = LATE + SOURCE + 1
+
 
 (
     SIZE,
@@ -26,12 +29,10 @@
     REST_IMAGE,
     START_IMAGE,
     REST_OWN,
-    REST_LOW,
-    REST_HIGH,
+    REST_SWAPPED,
     START_OWN,
-    START_LOW,
-    START_HIGH,
-) = range(11)
+    START_SWAPPED,
+) = range(9)
 BOND_LANES = 64
 
 
@@ -108,108 +109,97 @@
         )
 
 
-def list_channels(shift, lists):
+def is_late(code):
+    even = lax.rem(lax.axis_index("blk"), 2) == 0
+    return code == jnp.where(even, 1, 2)
+
+
+def list_units(shift, downs, lists):
     channels = shift.shape[0]
-    for code in range(CODES):
-        count = jnp.int32(0)
-        for channel in range(channels):
-            lists[code, count] = jnp.int32(channel)
-            count = count + (shift[channel] == code).astype(jnp.int32)
-        lists[code, channels] = count
-    count = jnp.int32(0)
+    end = channels * downs
+    early, late = jnp.int32(0), jnp.int32(0)
     for channel in range(channels):
         code = shift[channel]
-        lists[HALO_CHANNELS, count] = jnp.int32(channel)
-        lists[HALO_KINDS, count] = (code == 2).astype(jnp.int32)
-        count = count + ((code == 1) | (code == 2)).astype(jnp.int32)
-    lists[HALO_CHANNELS, channels] = count
-
-
-def add_images(lists, code, lefts, rights, sources, sums, arrived=None):
-    channels = lefts[0].shape[0]
-    downs = lefts[0].shape[1]
-    units = [
-        (bond, down)
-        for bond in range(BONDS)
-        for down in range(downs)
-        if sources(bond, down) is not None
-    ]
-
-    def step(index, carry):
-        channel = lists[code, index]
+        far = is_late(code)
+        near = jnp.logical_not(far) & ((code == 1) | (code == 2))
+        move = (code == 4).astype(jnp.int32) - (code == 3).astype(jnp.int32)
+        opens = jnp.int32(1)
+        for down in range(downs):
+            source = down + move
+            here = jnp.logical_not(far) & (source >= 0) & (source < downs)
+            lists[EARLY + CHANNEL, early] = jnp.int32(channel)
+            lists[EARLY + KIND, early] = near.astype(jnp.int32)
+            lists[EARLY + DOWN, early] = jnp.int32(down)
+            lists[EARLY + SOURCE, early] = jnp.where(near, downs + down, source)
+            lists[EARLY + OPENS, early] = opens
+            lists[LATE + CHANNEL, late] = jnp.int32(channel)
+            lists[LATE + KIND, late] = jnp.int32(0)
+            lists[LATE + DOWN, late] = jnp.int32(down)
+            lists[LATE + SOURCE, late] = jnp.int32(down)
+            opens = jnp.where(here, 0, opens)
+            early = early + here.astype(jnp.int32)
+            late = late + far.astype(jnp.int32)
+    lists[EARLY, end] = early
+    lists[LATE, end] = late
+
+
+class Unparted:
+    def __init__(self, sums):
+        self.sums = sums
+
+    def __getitem__(self, place):
+        return self.sums[place[1:]]
+
+    def __setitem__(self, place, value):
+        self.sums[place[1:]] = value
+
+
+def add_units(lists, base, lefts, rights, sources, sums, arrived=None):
+    def images(indices):
+        units = [
+            [lists[base + part, index] for part in (CHANNEL, KIND, DOWN, SOURCE)]
+            for index in indices
+        ]
         if arrived is not None:
-            arrived(channel)
+            for index, unit in zip(indices, units):
+                pl.when(lists[base + OPENS, index] == 1)(functools.partial(arrived, unit[0]))
         halves = [
-            dot(lefts[bond][channel, down], sources(bond, down)[...]).astype(BF16)
-            for bond, down in units
+            [
+                dot(lefts[bond][channel, down], sources[bond, source]).astype(BF16)
+                for bond in range(BONDS)
+            ]
+            for channel, _, down, source in units
         ]
-        for (bond, down), half in zip(units, halves):
-            sums[bond, down] += dot_by_rows(half, rights[bond][channel, down])
-        return carry
-
-    lax.fori_loop(0, lists[code, channels], step, 0)
-
-
-def add_local_images(lists, lefts, rights, states, sums, arrived=None):
-    downs = states.shape[1]
-
-    def below(bond, down):
-        return states.at[bond, down - 1] if down > 0 else None
-
-    def above(bond, down):
-        return states.at[bond, down + 1] if down + 1 < downs else None
-
-    add_images(lists, 0, lefts, rights, lambda bond, down: states.at[bond, down], sums, arrived)
-    add_images(lists, 3, lefts, rights, below, sums, arrived)
-    add_images(lists, 4, lefts, rights, above, sums, arrived)
-
-
-def add_halo_images(lists, lefts, rights, swapped, shifted, halo, sums, parted, lists_copy):
-    even = lax.rem(lax.axis_index("blk"), 2) == 0
-    channels = lefts[0].shape[0]
-    downs = swapped.shape[1]
-    units = [(bond, down) for bond in range(BONDS) for down in range(downs)]
-    for bond, down in units:
-        one, other = swapped[bond, down], shifted[bond, down]
-        halo[0, bond, down] = jnp.where(even, other, one)
-        halo[1, bond, down] = jnp.where(even, one, other)
-    lists_copy.wait()
-
-    def images(indices):
-        halves = []
-        for index in indices:
-            channel, kind = lists[HALO_CHANNELS, index], lists[HALO_KINDS, index]
-            halves.append(
-                [
-                    dot(lefts[bond][channel, down], halo[kind, bond, down]).astype(BF16)
-                    for bond, down in units
-                ]
-            )
-        for index, half_steps in zip(indices, halves):
-            channel, kind = lists[HALO_CHANNELS, index], lists[HALO_KINDS, index]
-            target = sums.at[kind] if parted else sums
-            for (bond, down), half in zip(units, half_steps):
-                target[bond, down] += dot_by_rows(half, rights[bond][channel, down])
-
-    def two(index, carry):
-        images([2 * index, 2 * index + 1])
-        return carry
-
-    def one_left(index, carry):
-        images([index])
-        return carry
-
-    count = lists[HALO_CHANNELS, channels]
-    odd = lax.rem(count, 2)
-    lax.fori_loop(0, lax.div(count, 2), two, 0)
-    lax.fori_loop(count - odd, count, one_left, 0)
-
-
-def opening(shift, starts, *refs):
-    held, loaded, (own_images, lists, sems) = refs[:4], refs[4:8], refs[8:]
+        for (channel, kind, down, _), half in zip(units, halves):
+            for bond in range(BONDS):
+                sums[kind, bond, down] += dot_by_rows(half[bond], rights[bond][channel, down])
+
+    count = lists[base, lists.shape[1] - 1]
+    done = jnp.int32(0)
+    for size in (4, 2, 1):
+        steps = lax.div(count - done, size)
+
+        def step(index, carry, size=size, done=done):
+            first = done + size * index
+            images([first + i for i in range(size)])
+            return carry
+
+        lax.fori_loop(0, steps, step, 0)
+        done = done + size * steps
+
+
+def fill_sources(own, swapped, sources):
+    downs = own.shape[1]
+    for bond in range(BONDS):
+        for down in range(downs):
+            sources[bond, down] = own[bond, down]
+            sources[bond, downs + down] = swapped[bond, down]
+
+
+def opening(shift, starts, swapped, *refs):
+    held, loaded, (images, row, lists, sources, sems) = refs[:4], refs[4:8], refs[8:]
     left_a, right_a, left_b, right_b = loaded
-    channels = left_a.shape[0]
-    list_channels(shift, lists)
+    channels, downs = left_a.shape[0], left_a.shape[1]
 
     def copies(channel):
         return [
@@ -217,25 +207,39 @@
             for source, target in zip(held, loaded)
         ]
 
-    def bring(index, carry, code):
-        for copy in copies(lists[code, index]):
+    def bring(channel):
+        for copy in copies(channel):
             copy.start()
-        return carry
 
     def await_one(channel):
         for copy in copies(channel):
             copy.wait()
 
-    def await_listed(index, carry, code):
-        await_one(lists[code, index])
-        return carry
-
-    for code in (0, 3, 4, 1, 2):
-        lax.fori_loop(0, lists[code, channels], functools.partial(bring, code=code), 0)
-    own_images[...] = jnp.zeros_like(own_images)
-    add_local_images(lists, (left_a, left_b), (right_a, right_b), starts, own_images, await_one)
-    for code in (1, 2):
-        lax.fori_loop(0, lists[code, channels], functools.partial(await_listed, code=code), 0)
+    for channel in range(channels):
+        pl.when(jnp.logical_not(is_late(shift[channel])))(functools.partial(bring, channel))
+    for channel in range(channels):
+        pl.when(is_late(shift[channel]))(functools.partial(bring, channel))
+    list_units(shift, downs, lists)
+    images[...] = jnp.zeros_like(images)
+    fill_sources(starts, swapped, sources)
+    found = []
+    for bond in range(BONDS):
+        size = jnp.zeros((1, 1), F32)
+        for down in range(downs):
+            start = starts[bond, down].astype(F32)
+            size += total(start * start)
+        found.append((bond * BOND_LANES + SIZE, size))
+    add_units(lists, EARLY, (left_a, left_b), (right_a, right_b), sources, images, await_one)
+    for bond in range(BONDS):
+        numbers = [jnp.zeros((1, 1), F32) for _ in range(2)]
+        for down in range(downs):
+            start = starts[bond, down].astype(F32)
+            for kind in range(2):
+                numbers[kind] += total(start * images[kind, bond, down])
+        found += [(bond * BOND_LANES + START_OWN + kind, numbers[kind]) for kind in range(2)]
+    row[...] = jnp.broadcast_to(in_lanes(row.shape[1], found), row.shape)
+    for channel in range(channels):
+        pl.when(is_late(shift[channel]))(functools.partial(await_one, channel))
 
 
 def mixing(mix, env, after, mixed):
@@ -274,14 +278,13 @@
     left_b,
     right_b,
     starts,
-    swapped,
     shifted,
-    own_images,
+    images,
+    row_in,
     rest,
     sent,
-    halo_images,
     row,
-    halo,
+    late,
     lists,
     sizes,
     sems,
@@ -291,57 +294,51 @@
     sizes_copy = pltpu.make_async_copy(sizes_held, sizes, sems.at[1])
     sizes_copy.start()
     downs, block = left_a.shape[1], left_a.shape[-1]
-    halo_images[...] = jnp.zeros_like(halo_images)
-    add_halo_images(
-        lists,
-        (left_a, left_b),
-        (right_a, right_b),
-        swapped,
-        shifted,
-        halo,
-        halo_images,
-        True,
-        lists_copy,
-    )
+    late[...] = jnp.zeros_like(late)
+    lists_copy.wait()
+    add_units(lists, LATE, (left_a, left_b), (right_a, right_b), shifted, late)
     sizes_copy.wait()
     found = []
     for bond in range(BONDS):
-        size = jnp.zeros((1, 1), F32)
+        at = bond * BOND_LANES + SIZE
+        size = row_in[0:1, at : at + 1]
         cross = jnp.zeros((1, 1), F32)
         for down in range(downs):
-            image = own_images[bond, down] + halo_images[0, bond, down] + halo_images[1, bond, down]
+            image = images[0, bond, down] + images[1, bond, down] + late[0, bond, down]
             rest[bond, down] = image
-            start = starts[bond, down].astype(F32)
-            size += total(start * start)
-            cross += total(start * image)
+            cross += total(starts[bond, down].astype(F32) * image)
         quotient = jnp.where(size > 0.0, cross / jnp.where(size > 0.0, size, 1.0), 0.0)
         for down in range(downs):
             image = jnp.where(live_of(sizes, bond, down, block), rest[bond, down], 0.0)
             left_over = image - quotient * starts[bond, down].astype(F32)
             rest[bond, down] = left_over
             sent[bond, down] = left_over.astype(BF16)
-        offset = bond * BOND_LANES
-        found += [(offset + SIZE, size), (offset + QUOTIENT, quotient)]
-    row[...] = jnp.broadcast_to(in_lanes(row.shape[1], found), row.shape)
-
-
-def local_seconds(
-    lists,
+        found.append((bond * BOND_LANES + QUOTIENT, quotient))
+    row[...] = row_in[...] + jnp.broadcast_to(in_lanes(row.shape[1], found), row.shape)
+
+
+def early_seconds(
+    lists_held,
     left_a,
     right_a,
     left_b,
     right_b,
     sent,
+    swapped,
     starts,
     rest,
-    own_images,
-    halo_images,
+    images,
     row_in,
     row,
+    sums,
     along,
-    sums,
+    sources,
+    lists,
+    lists_sem,
     sems,
 ):
+    lists_copy = pltpu.make_async_copy(lists_held, lists, lists_sem)
+    lists_copy.start()
     downs = left_a.shape[1]
     copies = [
         pltpu.make_async_copy(source.at[BONDS - 1], along.at[index], sems.at[index])
@@ -350,20 +347,17 @@
     for copy in copies:
         copy.start()
     sums[...] = jnp.zeros_like(sums)
-    add_local_images(lists, (left_a, left_b), (right_a, right_b), sent, sums)
+    fill_sources(sent, swapped, sources)
+    lists_copy.wait()
+    add_units(lists, EARLY, (left_a, left_b), (right_a, right_b), sources, Unparted(sums))
     found = []
     for bond in range(BONDS):
-        numbers = {place: jnp.zeros((1, 1), F32) for place in range(REST, START_HIGH + 1)}
-        for down in range(downs):
-            start = starts[bond, down].astype(F32)
+        numbers = {place: jnp.zeros((1, 1), F32) for place in (REST, REST_OWN, REST_SWAPPED)}
+        for down in range(downs):
             left_over = rest[bond, down]
             numbers[REST] += total(left_over * left_over)
-            numbers[REST_IMAGE] += total(left_over * sums[bond, down])
-            numbers[START_IMAGE] += total(start * sums[bond, down])
-            parts = (own_images[bond, down], halo_images[0, bond, down], halo_images[1, bond, down])
-            for kind, part in enumerate(parts):
-                numbers[REST_OWN + kind] += total(left_over * part)
-                numbers[START_OWN + kind] += total(start * part)
+            for kind in range(2):
+                numbers[REST_OWN + kind] += total(left_over * images[kind, bond, down])
         offset = bond * BOND_LANES
         found += [(offset + place, numbers[place]) for place in sorted(numbers)]
     row[...] = row_in[...] + jnp.broadcast_to(in_lanes(row.shape[1], found), row.shape)
@@ -371,19 +365,18 @@
         copy.wait()
 
 
-def halo_seconds(
+def late_seconds(
     lists_held,
     left_a,
     right_a,
     left_b,
     right_b,
-    swapped,
     shifted,
     starts,
     rest,
+    early_sums,
     row_in,
     row,
-    halo,
     sums,
     lists,
     lists_sem,
@@ -391,18 +384,9 @@
     lists_copy = pltpu.make_async_copy(lists_held, lists, lists_sem)
     lists_copy.start()
     downs = left_a.shape[1]
-    sums[...] = jnp.zeros_like(sums)
-    add_halo_images(
-        lists,
-        (left_a, left_b),
-        (right_a, right_b),
-        swapped,
-        shifted,
-        halo,
-        sums,
-        False,
-        lists_copy,
-    )
+    sums[...] = early_sums[...]
+    lists_copy.wait()
+    add_units(lists, LATE, (left_a, left_b), (right_a, right_b), shifted, Unparted(sums))
     found = []
     for bond in range(BONDS):
         of_rest = jnp.zeros((1, 1), F32)
@@ -415,26 +399,38 @@
     row[...] = jnp.broadcast_to(row_in[0:1, :] + in_lanes(row.shape[1], found), row.shape)
 
 
-def ritz(rows):
-    ups = rows.shape[1]
-
-    def column(array, place):
-        return array[:, :, place : place + 1]
-
-    def over_ups(array):
-        return jnp.sum(array, axis=1, keepdims=True)
-
-    size = column(rows, SIZE)
-    quotient = column(rows, QUOTIENT)
+def ritz(numbers, bond, first, ups, place):
+    lane = lax.broadcasted_iota(jnp.int32, (1, numbers.shape[1]), 1)
+    inside = (lane >= first) & (lane < first + ups)
+
+    def part(index):
+        at = bond * BOND_LANES + index
+        return numbers[at : at + 1]
+
+    def over_ups(values):
+        return jnp.sum(jnp.where(inside, values, 0.0), axis=1, keepdims=True)
+
+    size = part(SIZE)
+    quotient = part(QUOTIENT)
+    low = pltpu.roll(quotient, 1, 1)
+    high = pltpu.roll(quotient, quotient.shape[1] - 1, 1)
+    even = (lane & 1) == 0
+    none_low, none_high = lane == first, lane == first + ups - 1
     norm_sq = over_ups(size)
     alpha_zero = over_ups(size * quotient) / norm_sq
     off = quotient - alpha_zero
-    off_low = column(pltpu.roll(rows, 1, 1), QUOTIENT) - alpha_zero
-    off_high = column(pltpu.roll(rows, ups - 1, 1), QUOTIENT) - alpha_zero
-    residual_sq = over_ups(column(rows, REST) + size * off * off)
-    crossed = column(rows, REST_IMAGE) + off * column(rows, START_IMAGE)
-    for kind, factor in enumerate((off, off_low, off_high)):
-        crossed += factor * (column(rows, REST_OWN + kind) + off * column(rows, START_OWN + kind))
+    off_low = jnp.where(none_low, 0.0, low - alpha_zero)
+    off_high = jnp.where(none_high, 0.0, high - alpha_zero)
+    off_swapped = jnp.where(even, off_high, off_low)
+    off_shifted = jnp.where(even, off_low, off_high)
+    residual_sq = over_ups(part(REST) + size * off * off)
+    crossed = part(REST_IMAGE) + off * part(START_IMAGE)
+    rest_of = [part(REST_OWN), part(REST_SWAPPED)]
+    start_of = [part(START_OWN), part(START_SWAPPED)]
+    rest_of.append(part(REST) - rest_of[0] - rest_of[1])
+    start_of.append(quotient * size - start_of[0] - start_of[1])
+    for factor, of_rest, of_start in zip((off, off_swapped, off_shifted), rest_of, start_of):
+        crossed += factor * (of_rest + off * of_start)
     alpha_one = over_ups(crossed) / residual_sq
     beta_sq = residual_sq / norm_sq
     beta = jnp.sqrt(beta_sq)
@@ -443,8 +439,8 @@
     weight_one = energy - alpha_zero
     length = jnp.sqrt(beta_sq + weight_one * weight_one)
     of_rest = weight_one / (beta * length)
-    of_start = beta / length + of_rest * off
-    return energy, of_start, of_rest
+    own_off = jnp.sum(jnp.where(lane == first + place, off, 0.0), axis=1, keepdims=True)
+    return energy, beta / length + of_rest * own_off, of_rest
 
 
 def finish(
@@ -497,23 +493,16 @@
     ]
     for copy in arrivals[2 * BATCH :]:
         copy.start()
-    segments = numbers.shape[0] // ups
+    devices, width = numbers.shape
+    segments = devices // ups
     seg, blk = lax.axis_index("seg"), lax.axis_index("blk")
-    here = numbers[pl.ds(pl.multiple_of(seg * ups, ups), ups), :]
     after = jnp.minimum(seg + 1, segments - 1)
-    there = numbers[pl.ds(pl.multiple_of(after * ups, ups), ups), :]
-    width = numbers.shape[1]
-    energy, of_start, of_rest = ritz(
-        jnp.stack(
-            [
-                here,
-                pltpu.roll(here, width - BOND_LANES, 1),
-                pltpu.roll(there, width - BOND_LANES, 1),
-            ]
-        )
-    )
-    place = lax.broadcasted_iota(jnp.int32, of_start.shape, 1)
-    of_start = jnp.sum(jnp.where(place == blk, of_start, 0.0), axis=1, keepdims=True)
+    padding = [jnp.zeros((-devices % width, width), F32)] if devices % width else []
+    by_place = jnp.concatenate([numbers[...], *padding]).T
+    solves = [
+        ritz(by_place, bond, at * ups, ups, blk) for bond, at in ((0, seg), (1, seg), (1, after))
+    ]
+    energy, of_start, of_rest = zip(*solves)
     lane = lax.broadcasted_iota(jnp.int32, energies.shape, 1)
     energies[...] = jnp.where(lane == 0, energy[0], energy[1])
     last = seg == segments - 1
@@ -552,13 +541,19 @@
         for channel in group:
             leave(channel, made.at[channel], boundary.at[channel])
 
-    groups = [range(i, min(i + BATCH, channels)) for i in range(0, channels, BATCH)]
+    groups = []
+    while sum(map(len, groups)) < channels:
+        at = sum(map(len, groups))
+        groups.append(range(at, at + min(BATCH, (channels - at + 1) // 2)))
     for index, group in enumerate(groups):
         for channel in group:
             arrivals[channel].wait()
-        for channel in group:
-            for down, (product, _) in enumerate(products):
-                halves[channel, down] = dot(mixed[channel, down], product).astype(BF16)
+        for down, (product, _) in enumerate(products):
+            block = product.shape[0]
+            stacked = mixed[group.start : group.stop, down].reshape(len(group) * block, block)
+            half = dot(stacked, product).astype(BF16)
+            for place, channel in enumerate(group):
+                halves[channel, down] = half[place * block : (place + 1) * block]
         if index > 0:
             last_product(groups[index - 1])
         if index == min(1, len(groups) - 1):
@@ -622,67 +617,76 @@
         4 * downs * block * block,
         4 * bits,
     )(sizes, in_hbm(guess_a.reshape(pair)), in_hbm(guess_b.reshape(pair)))
-    shifted, swapped = shifted_pairs(starts), swapped_pairs(starts)
-
-    *loaded, own_images, lists = call(
+    swapped, shifted = swapped_pairs(starts), shifted_pairs(starts)
+
+    list_shape = (LIST_ROWS, channels * downs + 1)
+    sources = pltpu.VMEM((BONDS, 2 * downs, block, block), BF16)
+    *loaded, images, row, lists = call(
         opening,
         "opening",
-        [SMEM, VMEM] + [HBM] * 4,
+        [SMEM, VMEM, VMEM] + [HBM] * 4,
         [(VMEM, pltpu.VMEM(env_shape, BF16))] * 4
         + [
-            (VMEM, pltpu.VMEM(both, F32)),
-            (SMEM, jax.ShapeDtypeStruct((CODES + 2, channels + 1), jnp.int32)),
+            (VMEM, pltpu.VMEM((2,) + both, F32)),
+            (VMEM, tile),
+            (SMEM, jax.ShapeDtypeStruct(list_shape, jnp.int32)),
         ],
-        [pltpu.SemaphoreType.DMA((channels,))],
+        [sources, pltpu.SemaphoreType.DMA((channels,))],
         apply_flops,
         5 * env_bytes,
-    )(in_hbm(term_shift), starts, *held)
-
-    halo = pltpu.VMEM((2,) + both, BF16)
-    rest, sent, halo_images, row = call(
+    )(in_hbm(term_shift), starts, swapped, *held)
+
+    rest, sent, row = call(
         first_images,
         "first_images",
         [VMEM, HBM] + [VMEM] * 8,
         [
             (VMEM, pltpu.VMEM(both, F32)),
             (VMEM, pltpu.VMEM(both, BF16)),
-            (VMEM, pltpu.VMEM((2,) + both, F32)),
             (VMEM, tile),
         ],
         [
-            halo,
-            pltpu.SMEM(lists.shape, jnp.int32),
+            pltpu.VMEM((1,) + both, F32),
+            pltpu.SMEM(list_shape, jnp.int32),
             pltpu.SMEM(sizes.shape, jnp.int32),
             pltpu.SemaphoreType.DMA((2,)),
         ],
         apply_flops,
         env_bytes,
-    )(lists, sizes, *loaded, starts, swapped, shifted, own_images)
-    shifted, swapped = shifted_pairs(sent), swapped_pairs(sent)
-    row, along = call(
-        local_seconds,
-        "local_seconds",
-        [SMEM] + [VMEM] * 10,
-        [(VMEM, tile), (HBM, jax.ShapeDtypeStruct((2,) + pair, BF16))],
-        [pltpu.VMEM(both, F32), pltpu.SemaphoreType.DMA((2,))],
+    )(lists, sizes, *loaded, starts, shifted, images, row)
+    swapped, shifted = swapped_pairs(sent), shifted_pairs(sent)
+    row, sums, along = call(
+        early_seconds,
+        "early_seconds",
+        [VMEM] * 11,
+        [
+            (VMEM, tile),
+            (VMEM, pltpu.VMEM(both, F32)),
+            (HBM, jax.ShapeDtypeStruct((2,) + pair, BF16)),
+        ],
+        [
+            sources,
+            pltpu.SMEM(list_shape, jnp.int32),
+            pltpu.SemaphoreType.DMA(()),
+            pltpu.SemaphoreType.DMA((2,)),
+        ],
         apply_flops,
         env_bytes,
-    )(lists, *loaded, sent, starts, rest, own_images, halo_images, row)
+    )(lists, *loaded, sent, swapped, starts, rest, images, row)
     from_next = from_right_segment(along)
     (row,) = call(
-        halo_seconds,
-        "halo_seconds",
-        [VMEM] + [VMEM] * 9,
+        late_seconds,
+        "late_seconds",
+        [VMEM] * 10,
         [(VMEM, pltpu.VMEM((devices, 128), F32))],
         [
-            halo,
             pltpu.VMEM(both, F32),
-            pltpu.SMEM(lists.shape, jnp.int32),
+            pltpu.SMEM(list_shape, jnp.int32),
             pltpu.SemaphoreType.DMA(()),
         ],
         apply_flops,
         env_bytes,
-    )(lists, *loaded, swapped, shifted, starts, rest, row)
+    )(lists, *loaded, shifted, starts, rest, sums, row)
     numbers = lax.all_to_all(row, ("seg", "blk"), 0, 0, tiled=True)
     (mixed,) = call(
         mixing,

time: 51.5 us -> 49.3 us (0.957); the launches traced: 50.8 us -> 49.3 us
  Pallas kernels: 27.6 us -> 25.4 us
  waiting for transfers between devices: 2.61 us -> 4.3 us
  starting transfers between devices: 18.1 us -> 17.1 us
    ppermute x2, starting transfers between devices: 7.95 us -> 3.71 us  [swapped_pairs(): lax.ppermute(block, 'blk', [(i, i ^ 1) for i in devices if i ^ 1 in devic...]
    all_to_all x1, starting transfers between devices: 7.43 us -> 10.7 us  [local(): numbers = lax.all_to_all(row, ('seg', 'blk'), 0, 0, tiled=True)]
    ppermute x2, waiting for transfers between devices: 0.01 us -> 1.69 us  [swapped_pairs(): lax.ppermute(block, 'blk', [(i, i ^ 1) for i in devices if i ^ 1 in devic...]
    pallas_call x3, Pallas kernels: 14 us -> 12.8 us  [the longest x1 6.43 us: local(): call(opening, 'opening', [SMEM, VMEM, VMEM] + [HBM] * 4, [(VMEM, pltpu.VM...]
    pallas_call x1, Pallas kernels: 3.5 us -> 2.78 us  [local(): call(first_images, 'first_images', [VMEM, HBM] + [VMEM] * 8, [(VMEM, pltp...]
  transfers between devices with their start and end apart: 6 -> 6, of which waited for: 1 -> 3; matrix products, arithmetic and copies ran while one was open for 0% -> 0% of each run, Pallas kernels for 33% -> 31%
where the time goes in v4:
time: 49.3 us
  Pallas kernels  25.4 us (52%)
  starting transfers between devices  17.1 us (35%)
  waiting for transfers between devices  4.3 us (9%)
  local copies, waits for them, and re-layouts  1.64 us (3%)
  between operations  0.94 us (2%)
    all_to_all x1, starting transfers between devices, local(): numbers = lax.all_to_all(row, ('seg', 'blk'), 0, 0, tiled=True)  10.7 us
    pallas_call x1, Pallas kernels, local(): call(opening, 'opening', [SMEM, VMEM, VMEM] + [HBM] * 4, [(VMEM, pltpu.VM...  6.43 us
    pallas_call x1, Pallas kernels, local(): call(functools.partial(finish, 1.0 / block, ups), 'finish', [VMEM] + [HBM...  5.97 us
    ppermute x2, starting transfers between devices, swapped_pairs(): lax.ppermute(block, 'blk', [(i, i ^ 1) for i in devices if i ^ 1 in devic...  3.71 us
    pallas_call x1, Pallas kernels, local(): call(early_seconds, 'early_seconds', [VMEM] * 11, [(VMEM, tile), (VMEM, p...  3.33 us
    pallas_call x1, Pallas kernels, local(): call(late_seconds, 'late_seconds', [VMEM] * 10, [(VMEM, pltpu.VMEM((devic...  3.01 us
    pallas_call x1, Pallas kernels, local(): call(first_images, 'first_images', [VMEM, HBM] + [VMEM] * 8, [(VMEM, pltp...  2.78 us
    pallas_call x1, Pallas kernels, local(): call(mixing, 'mixing', [VMEM, VMEM, HBM], [(VMEM, jax.ShapeDtypeStruct(en...  2.64 us
  transfers between devices with their start and end apart: 6, of which 3 were waited for; matrix products, arithmetic and copies ran while one was open for 0% of the time, Pallas kernels for 31%

profile of v4, /device:TPU:0, one launch (start us, length us, event | category | flops | bytes accessed | tf_op | source)
XLA Modules:
  0.0 49.3 jit_solution(15107057893832237521)
XLA Ops:
  0.6 1.2 %masked_starts.1.starts.starts_held = bf16[2,2,256,256]{3,2,1,0:T(8,128)(2,1)S(1)} custom-call(s32[1,1,2,4]{3,2,1,0:T(2,128)} %bitcast.24, bf16[2,256,256]{2,1,0:T(8,128)(2,1)} %bitcast.22, bf16[2,256,256]{2,1,0:T(8,128)(2,1)} %bitcast.23), custom_call_target="tpu_custom_call" | custom-call | flops 524288 | bytes 1048576 | tf_op jit(solution)/shard_map/masked_starts/pallas_call | solution.py:611
  1.8 0.0 copy-start
  1.8 0.5 %collective-permute-start = (bf16[2,2,256,256]{3,2,1,0:T(8,128)(2,1)S(1)}, bf16[2,2,256,256]{3,2,1,0:T(8,128)(2,1)S(1)}, u32[]{:S(2)}, u32[]{:S(2)}) collective-permute-start(bf16[2,2,256,256]{3,2,1,0:T(8,128)(2,1)S(1)} %masked_starts.1.starts.starts_held), channel_id=1, source_target_pairs={{0,1},{1,0},{2,3},{3,2},{4,5},{5,4},{6,7},{7,6},{8,9},{9,8},{10,11... | collective-permute-start | bytes 1572872 | tf_op jit(solution)/shard_map/ppermute | solution.py:570
  2.4 0.7 %collective-permute-start.1 = (bf16[2,2,256,256]{3,2,1,0:T(8,128)(2,1)S(1)}, bf16[2,2,256,256]{3,2,1,0:T(8,128)(2,1)S(1)}, u32[]{:S(2)}, u32[]{:S(2)}) collective-permute-start(bf16[2,2,256,256]{3,2,1,0:T(8,128)(2,1)S(1)} %masked_starts.1.starts.starts_held), channel_id=1, source_target_pairs={{1,2},{3,4},{5,6},{2,1},{4,3},{6,5},{9,10},{11,12},{13,14},{10,9},... | collective-permute-start | bytes 1572872 | tf_op jit(solution)/shard_map/ppermute | solution.py:576
  3.0 0.8 %collective-permute-done.swapped = bf16[2,2,256,256]{3,2,1,0:T(8,128)(2,1)S(1)} collective-permute-done((bf16[2,2,256,256]{3,2,1,0:T(8,128)(2,1)S(1)}, bf16[2,2,256,256]{3,2,1,0:T(8,128)(2,1)S(1)}, u32[]{:S(2)}, u32[]{:S(2)}) %collective-permute-start) | collective-permute-done | bytes 524320 | tf_op jit(solution)/shard_map/ppermute | solution.py:570
  3.9 6.4 %opening.1 = (bf16[12,2,256,256]{3,2,1,0:T(8,128)(2,1)S(1)}, bf16[12,2,256,256]{3,2,1,0:T(8,128)(2,1)S(1)}, bf16[12,2,256,256]{3,2,1,0:T(8,128)(2,1)S(1)}, bf16[...) custom-call(s32[12]{0:T(128)} %shift.1, ...), custom_call_target="tpu_custom_call" | custom-call | flops 1610612736 | bytes 15728640 | tf_op jit(solution)/shard_map/opening/pallas_call | solution.py:624
  10.3 0.0 collective-permute-done.1.shifted
  10.3 2.8 %first_images.1 = (f32[2,2,256,256]{3,2,1,0:T(8,128)S(1)}, bf16[2,2,256,256]{3,2,1,0:T(8,128)(2,1)S(1)}, f32[8,128]{1,0:T(8,128)S(1)}) custom-call(s32[9,25]{1,0:T(8,128)S(1)} %get-tuple-element.21.lists_held, s32[1,1,2,4]{3,2,1,0:T(2,128)} %bitcast.25, bf16[12,2,256,256]{3,2,1,0:T(8,128)(2,1)S(1)} %get-tuple-element.22.left_a.env, ...), custom_call_target="tpu_custom_call" | custom-call | flops 1610612736 | bytes 3145728 | tf_op jit(solution)/shard_map/first_images/pallas_call | solution.py:639
  13.1 0.0 copy-start.1
  13.2 3.2 %collective-permute-start.3 = (bf16[2,2,256,256]{3,2,1,0:T(8,128)(2,1)S(1)}, bf16[2,2,256,256]{3,2,1,0:T(8,128)(2,1)S(1)}, u32[]{:S(2)}, u32[]{:S(2)}) collective-permute-start(bf16[2,2,256,256]{3,2,1,0:T(8,128)(2,1)S(1)} %get-tuple-element.28.sent), channel_id=1, source_target_pairs={{0,1},{1,0},{2,3},{3,2},{4,5},{5,4},{6,7},{7,6},{8,9},{9,8},{10,11... | collective-permute-start | bytes 1572872 | tf_op jit(solution)/shard_map/ppermute | solution.py:570
  16.3 0.7 %collective-permute-start.2 = (bf16[2,2,256,256]{3,2,1,0:T(8,128)(2,1)S(1)}, bf16[2,2,256,256]{3,2,1,0:T(8,128)(2,1)S(1)}, u32[]{:S(2)}, u32[]{:S(2)}) collective-permute-start(bf16[2,2,256,256]{3,2,1,0:T(8,128)(2,1)S(1)} %get-tuple-element.28.sent), channel_id=1, source_target_pairs={{1,2},{3,4},{5,6},{2,1},{4,3},{6,5},{9,10},{11,12},{13,14},{10,9},... | collective-permute-start | bytes 1572872 | tf_op jit(solution)/shard_map/ppermute | solution.py:576
  17.0 0.8 %collective-permute-done.3.swapped = bf16[2,2,256,256]{3,2,1,0:T(8,128)(2,1)S(1)} collective-permute-done((bf16[2,2,256,256]{3,2,1,0:T(8,128)(2,1)S(1)}, bf16[2,2,256,256]{3,2,1,0:T(8,128)(2,1)S(1)}, u32[]{:S(2)}, u32[]{:S(2)}) %collective-permute-start.3) | collective-permute-done | bytes 524320 | tf_op jit(solution)/shard_map/ppermute | solution.py:570
  17.9 3.3 %early_seconds.1 = (f32[8,128]{1,0:T(8,128)S(1)}, f32[2,2,256,256]{3,2,1,0:T(8,128)S(1)}, bf16[2,2,256,256]{3,2,1,0:T(8,128)(2,1)}) custom-call(s32[9,25]{1,0:T(8,128)S(1)} %get-tuple-element.21.lists_held, bf16[12,2,256,256]{3,2,1,0:T(8,128)(2,1)S(1)} %get-tuple-element.22.left_a.env, bf16[12,2,256,256]{3,2,1,0:T(8,128)(2,1)S(1)} %get-tuple-element.23.right_a, ...), custom_call_target="tpu_custom_call" | custom-call | flops 1610612736 | bytes 3145728 | tf_op jit(solution)/shard_map/early_seconds/pallas_call | solution.py:658
  21.2 1.3 %collective-permute-start.4 = (bf16[2,2,256,256]{3,2,1,0:T(8,128)(2,1)}, bf16[2,2,256,256]{3,2,1,0:T(8,128)(2,1)}, u32[]{:S(2)}, u32[]{:S(2)}) collective-permute-start(bf16[2,2,256,256]{3,2,1,0:T(8,128)(2,1)} %get-tuple-element.33), channel_id=1, source_target_pairs={{8,0},{16,8},{24,16},{9,1},{17,9},{25,17},{10,2},{18,10},{26,18},{... | collective-permute-start | bytes 1572872 | tf_op jit(solution)/shard_map/ppermute | solution.py:581
  22.5 0.0 collective-permute-done.2.shifted
  22.5 0.0 copy-done
  22.5 0.0 copy-done.1
  22.6 0.0 copy-start.3
  22.6 3.0 %late_seconds.1.after = f32[32,128]{1,0:T(8,128)} custom-call(s32[9,25]{1,0:T(8,128)S(1)} %get-tuple-element.21.lists_held, bf16[12,2,256,256]{3,2,1,0:T(8,128)(2,1)S(1)} %get-tuple-element.22.left_a.env, bf16[12,2,256,256]{3,2,1,0:T(8,128)(2,1)S(1)} %get-tuple-element.23.right_a, bf16[12,2,256,256]{3,2,1,0:T(8,128)(2,1)S(1)} %get-tuple-element.24.left_b, ...), custom_call_target="tpu_custom_call" | custom-call | flops 1610612736 | bytes 3145728 | tf_op jit(solution)/shard_map/late_seconds/pallas_call | solution.py:677
  25.6 10.7 %all-to-all-start = ((f32[32,1,128]{2,1,0:T(1,128)}), f32[32,1,128]{2,1,0:T(1,128)S(1)}, u32[]{:S(2)}, u32[]{:S(2)}) async-start(f32[32,1,128]{2,1,0:T(1,128)} %bitcast.8), calls=%async_computation | async-start | bytes 32768 | tf_op jit(solution)/shard_map/all_to_all | solution.py:690
  36.3 0.0 copy-done.3
  36.3 2.6 %mixing.1.mixed_held = bf16[12,2,256,256]{3,2,1,0:T(8,128)(2,1)S(1)} custom-call(f32[12,12]{1,0:T(8,128)S(1)} %copy-done.3, bf16[12,2,256,256]{3,2,1,0:T(8,128)(2,1)S(1)} %get-tuple-element.22.left_a.env, f32[32,128]{1,0:T(8,128)} %late_seconds.1.after), custom_call_target="tpu_custom_call" | custom-call | flops 1207959552 | bytes 6291456 | tf_op jit(solution)/shard_map/mixing/pallas_call | solution.py:691
  39.0 0.0 copy-start.2
  39.0 1.6 %copy-done.2 = bf16[12,2,256,256]{3,2,1,0:T(8,128)(2,1)} copy-done((bf16[12,2,256,256]{3,2,1,0:T(8,128)(2,1)}, bf16[12,2,256,256]{3,2,1,0:T(8,128)(2,1)S(1)}, u32[]{:S(2)}) %copy-start.2) | copy-done | bytes 3145752
  40.6 2.6 %all-to-all-done = f32[32,1,128]{2,1,0:T(1,128)S(1)} async-done(((f32[32,1,128]{2,1,0:T(1,128)}), f32[32,1,128]{2,1,0:T(1,128)S(1)}, u32[]{:S(2)}, u32[]{:S(2)}) %all-to-all-start) | async-done | bytes 16416 | tf_op jit(solution)/shard_map/all_to_all | solution.py:690
  43.2 0.0 collective-permute-done.4.along_held
  43.2 6.0 %finish.1 = (f32[2,256,256]{2,1,0:T(8,128)}, f32[2,256,256]{2,1,0:T(8,128)}, f32[1,2]{1,0:T(1,128)}, bf16[12,2,256,256]{3,2,1,0:T(8,128)(2,1)}) custom-call(f32[32,128]{1,0:T(8,128)S(1)} %bitcast.17, bf16[2,2,256,256]{3,2,1,0:T(8,128)(2,1)} %copy-done, f32[2,2,256,256]{3,2,1,0:T(8,128)} %copy-done.1, ...), custom_call_target="tpu_custom_call" | custom-call | flops 1610612736 | bytes 6291456 | tf_op jit(solution)/shard_map/finish/pallas_call | solution.py:701
Async XLA Ops:
  1.8 20.7 %copy-start = (bf16[2,2,256,256]{3,2,1,0:T(8,128)(2,1)}, bf16[2,2,256,256]{3,2,1,0:T(8,128)(2,1)S(1)}, u32[]{:S(2)}) copy-start(bf16[2,2,256,256]{3,2,1,0:T(8,128)(2,1)S(1)} %masked_starts.1.starts.starts_held) | copy-start | bytes 1572868
  1.8 2.1 %collective-permute-start = (bf16[2,2,256,256]{3,2,1,0:T(8,128)(2,1)S(1)}, bf16[2,2,256,256]{3,2,1,0:T(8,128)(2,1)S(1)}, u32[]{:S(2)}, u32[]{:S(2)}) collective-permute-start(bf16[2,2,256,256]{3,2,1,0:T(8,128)(2,1)S(1)} %masked_starts.1.starts.starts_held), channel_id=1, source_target_pairs={{0,1},{1,0},{2,3},{3,2},{4,5},{5,4},{6,7},{7,6},{8,9},{9,8},{10,11... | collective-permute-start | bytes 1572872 | tf_op jit(solution)/shard_map/ppermute | solution.py:570
  2.4 8.0 %collective-permute-start.1 = (bf16[2,2,256,256]{3,2,1,0:T(8,128)(2,1)S(1)}, bf16[2,2,256,256]{3,2,1,0:T(8,128)(2,1)S(1)}, u32[]{:S(2)}, u32[]{:S(2)}) collective-permute-start(bf16[2,2,256,256]{3,2,1,0:T(8,128)(2,1)S(1)} %masked_starts.1.starts.starts_held), channel_id=1, source_target_pairs={{1,2},{3,4},{5,6},{2,1},{4,3},{6,5},{9,10},{11,12},{13,14},{10,9},... | collective-permute-start | bytes 1572872 | tf_op jit(solution)/shard_map/ppermute | solution.py:576
  13.1 9.4 %copy-start.1 = (f32[2,2,256,256]{3,2,1,0:T(8,128)}, f32[2,2,256,256]{3,2,1,0:T(8,128)S(1)}, u32[]{:S(2)}) copy-start(f32[2,2,256,256]{3,2,1,0:T(8,128)S(1)} %get-tuple-element.29.rest.rest_held) | copy-start | bytes 3145732
  13.2 4.7 %collective-permute-start.3 = (bf16[2,2,256,256]{3,2,1,0:T(8,128)(2,1)S(1)}, bf16[2,2,256,256]{3,2,1,0:T(8,128)(2,1)S(1)}, u32[]{:S(2)}, u32[]{:S(2)}) collective-permute-start(bf16[2,2,256,256]{3,2,1,0:T(8,128)(2,1)S(1)} %get-tuple-element.28.sent), channel_id=1, source_target_pairs={{0,1},{1,0},{2,3},{3,2},{4,5},{5,4},{6,7},{7,6},{8,9},{9,8},{10,11... | collective-permute-start | bytes 1572872 | tf_op jit(solution)/shard_map/ppermute | solution.py:570
  16.3 6.2 %collective-permute-start.2 = (bf16[2,2,256,256]{3,2,1,0:T(8,128)(2,1)S(1)}, bf16[2,2,256,256]{3,2,1,0:T(8,128)(2,1)S(1)}, u32[]{:S(2)}, u32[]{:S(2)}) collective-permute-start(bf16[2,2,256,256]{3,2,1,0:T(8,128)(2,1)S(1)} %get-tuple-element.28.sent), channel_id=1, source_target_pairs={{1,2},{3,4},{5,6},{2,1},{4,3},{6,5},{9,10},{11,12},{13,14},{10,9},... | collective-permute-start | bytes 1572872 | tf_op jit(solution)/shard_map/ppermute | solution.py:576
  21.2 22.0 %collective-permute-start.4 = (bf16[2,2,256,256]{3,2,1,0:T(8,128)(2,1)}, bf16[2,2,256,256]{3,2,1,0:T(8,128)(2,1)}, u32[]{:S(2)}, u32[]{:S(2)}) collective-permute-start(bf16[2,2,256,256]{3,2,1,0:T(8,128)(2,1)} %get-tuple-element.33), channel_id=1, source_target_pairs={{8,0},{16,8},{24,16},{9,1},{17,9},{25,17},{10,2},{18,10},{26,18},{... | collective-permute-start | bytes 1572872 | tf_op jit(solution)/shard_map/ppermute | solution.py:581
  22.6 13.8 %copy-start.3 = (f32[12,12]{1,0:T(8,128)S(1)}, f32[12,12]{1,0:T(8,128)}, u32[]{:S(2)}) copy-start(f32[12,12]{1,0:T(8,128)} %mix.1) | copy-start | bytes 1732
  25.6 17.6 %all-to-all-start = ((f32[32,1,128]{2,1,0:T(1,128)}), f32[32,1,128]{2,1,0:T(1,128)S(1)}, u32[]{:S(2)}, u32[]{:S(2)}) async-start(f32[32,1,128]{2,1,0:T(1,128)} %bitcast.8), calls=%async_computation | async-start | bytes 32768 | tf_op jit(solution)/shard_map/all_to_all | solution.py:690
  39.0 1.6 %copy-start.2 = (bf16[12,2,256,256]{3,2,1,0:T(8,128)(2,1)}, bf16[12,2,256,256]{3,2,1,0:T(8,128)(2,1)S(1)}, u32[]{:S(2)}) copy-start(bf16[12,2,256,256]{3,2,1,0:T(8,128)(2,1)S(1)} %mixing.1.mixed_held) | copy-start | bytes 9437188

commit v5 on v4

--- a/solution.py
+++ b/solution.py
@@ -14,7 +14,7 @@
 HBM = pl.BlockSpec(memory_space=pltpu.HBM)
 MIB = 1 << 20
 GROUP = 16
-BATCH = 4
+BATCH = 6
 BONDS = 2
 
 CHANNEL, KIND, DOWN, SOURCE, OPENS = range(5)
@@ -26,13 +26,14 @@
     SIZE,
     QUOTIENT,
     REST,
+    START_REST,
     REST_IMAGE,
     START_IMAGE,
     REST_OWN,
     REST_SWAPPED,
     START_OWN,
     START_SWAPPED,
-) = range(9)
+) = range(10)
 BOND_LANES = 64
 
 
@@ -77,6 +78,18 @@
 
 def total(array):
     return jnp.sum(jnp.sum(array, axis=0, keepdims=True), axis=1, keepdims=True)
+
+
+def folded(array):
+    return jnp.sum(array.reshape(-1, 8, array.shape[-1]), axis=0)
+
+
+def totals(parts):
+    rows = parts[0].shape[0]
+    by_row = jnp.sum(jnp.concatenate(parts), axis=1, keepdims=True)
+    return [
+        jnp.sum(by_row[i * rows : (i + 1) * rows], axis=0, keepdims=True) for i in range(len(parts))
+    ]
 
 
 def in_lanes(width, pairs):
@@ -196,8 +209,14 @@
             sources[bond, downs + down] = swapped[bond, down]
 
 
-def opening(shift, starts, swapped, *refs):
-    held, loaded, (images, row, lists, sources, sems) = refs[:4], refs[4:8], refs[8:]
+def opening(shift_held, starts, swapped, *refs):
+    held, loaded, (images, near_rest, row, lists, sources, shift, shift_sem, sems) = (
+        refs[:4],
+        refs[4:8],
+        refs[8:],
+    )
+    shift_copy = pltpu.make_async_copy(shift_held, shift, shift_sem)
+    shift_copy.start()
     left_a, right_a, left_b, right_b = loaded
     channels, downs = left_a.shape[0], left_a.shape[1]
 
@@ -207,18 +226,14 @@
             for source, target in zip(held, loaded)
         ]
 
-    def bring(channel):
-        for copy in copies(channel):
-            copy.start()
-
     def await_one(channel):
         for copy in copies(channel):
             copy.wait()
 
     for channel in range(channels):
-        pl.when(jnp.logical_not(is_late(shift[channel])))(functools.partial(bring, channel))
-    for channel in range(channels):
-        pl.when(is_late(shift[channel]))(functools.partial(bring, channel))
+        for copy in copies(channel):
+            copy.start()
+    shift_copy.wait()
     list_units(shift, downs, lists)
     images[...] = jnp.zeros_like(images)
     fill_sources(starts, swapped, sources)
@@ -230,13 +245,26 @@
             size += total(start * start)
         found.append((bond * BOND_LANES + SIZE, size))
     add_units(lists, EARLY, (left_a, left_b), (right_a, right_b), sources, images, await_one)
+    pairs = [(bond, kind) for bond in range(BONDS) for kind in range(2)]
+    crosses = totals(
+        [
+            sum(
+                folded(starts[bond, down].astype(F32) * images[kind, bond, down])
+                for down in range(downs)
+            )
+            for bond, kind in pairs
+        ]
+    )
+    for (bond, kind), cross in zip(pairs, crosses):
+        found.append((bond * BOND_LANES + START_OWN + kind, cross))
     for bond in range(BONDS):
-        numbers = [jnp.zeros((1, 1), F32) for _ in range(2)]
+        size = found[bond][1]
+        cross = crosses[2 * bond] + crosses[2 * bond + 1]
+        quotient = jnp.where(size > 0.0, cross / jnp.where(size > 0.0, size, 1.0), 0.0)
+        found.append((bond * BOND_LANES + QUOTIENT, quotient))
         for down in range(downs):
-            start = starts[bond, down].astype(F32)
-            for kind in range(2):
-                numbers[kind] += total(start * images[kind, bond, down])
-        found += [(bond * BOND_LANES + START_OWN + kind, numbers[kind]) for kind in range(2)]
+            image = images[0, bond, down] + images[1, bond, down]
+            near_rest[bond, down] = image - quotient * starts[bond, down].astype(F32)
     row[...] = jnp.broadcast_to(in_lanes(row.shape[1], found), row.shape)
     for channel in range(channels):
         pl.when(is_late(shift[channel]))(functools.partial(await_one, channel))
@@ -277,14 +305,10 @@
     right_a,
     left_b,
     right_b,
-    starts,
     shifted,
-    images,
-    row_in,
+    near_rest,
     rest,
     sent,
-    row,
-    late,
     lists,
     sizes,
     sems,
@@ -294,27 +318,15 @@
     sizes_copy = pltpu.make_async_copy(sizes_held, sizes, sems.at[1])
     sizes_copy.start()
     downs, block = left_a.shape[1], left_a.shape[-1]
-    late[...] = jnp.zeros_like(late)
+    rest[...] = near_rest[...]
     lists_copy.wait()
-    add_units(lists, LATE, (left_a, left_b), (right_a, right_b), shifted, late)
+    add_units(lists, LATE, (left_a, left_b), (right_a, right_b), shifted, Unparted(rest))
     sizes_copy.wait()
-    found = []
     for bond in range(BONDS):
-        at = bond * BOND_LANES + SIZE
-        size = row_in[0:1, at : at + 1]
-        cross = jnp.zeros((1, 1), F32)
         for down in range(downs):
-            image = images[0, bond, down] + images[1, bond, down] + late[0, bond, down]
-            rest[bond, down] = image
-            cross += total(starts[bond, down].astype(F32) * image)
-        quotient = jnp.where(size > 0.0, cross / jnp.where(size > 0.0, size, 1.0), 0.0)
-        for down in range(downs):
-            image = jnp.where(live_of(sizes, bond, down, block), rest[bond, down], 0.0)
-            left_over = image - quotient * starts[bond, down].astype(F32)
+            left_over = jnp.where(live_of(sizes, bond, down, block), rest[bond, down], 0.0)
             rest[bond, down] = left_over
             sent[bond, down] = left_over.astype(BF16)
-        found.append((bond * BOND_LANES + QUOTIENT, quotient))
-    row[...] = row_in[...] + jnp.broadcast_to(in_lanes(row.shape[1], found), row.shape)
 
 
 def early_seconds(
@@ -350,16 +362,18 @@
     fill_sources(sent, swapped, sources)
     lists_copy.wait()
     add_units(lists, EARLY, (left_a, left_b), (right_a, right_b), sources, Unparted(sums))
-    found = []
+    places, parts = [], []
     for bond in range(BONDS):
-        numbers = {place: jnp.zeros((1, 1), F32) for place in (REST, REST_OWN, REST_SWAPPED)}
+        folds = {place: 0.0 for place in (REST, START_REST, REST_OWN, REST_SWAPPED)}
         for down in range(downs):
             left_over = rest[bond, down]
-            numbers[REST] += total(left_over * left_over)
+            folds[START_REST] += folded(left_over * starts[bond, down].astype(F32))
+            folds[REST] += folded(left_over * left_over)
             for kind in range(2):
-                numbers[REST_OWN + kind] += total(left_over * images[kind, bond, down])
-        offset = bond * BOND_LANES
-        found += [(offset + place, numbers[place]) for place in sorted(numbers)]
+                folds[REST_OWN + kind] += folded(left_over * images[kind, bond, down])
+        places += [bond * BOND_LANES + place for place in folds]
+        parts += folds.values()
+    found = list(zip(places, totals(parts)))
     row[...] = row_in[...] + jnp.broadcast_to(in_lanes(row.shape[1], found), row.shape)
     for copy in copies:
         copy.wait()
@@ -387,15 +401,16 @@
     sums[...] = early_sums[...]
     lists_copy.wait()
     add_units(lists, LATE, (left_a, left_b), (right_a, right_b), shifted, Unparted(sums))
-    found = []
+    places, parts = [], []
     for bond in range(BONDS):
-        of_rest = jnp.zeros((1, 1), F32)
-        of_start = jnp.zeros((1, 1), F32)
+        of_rest, of_start = 0.0, 0.0
         for down in range(downs):
-            of_rest += total(rest[bond, down] * sums[bond, down])
-            of_start += total(starts[bond, down].astype(F32) * sums[bond, down])
-        offset = bond * BOND_LANES
-        found += [(offset + REST_IMAGE, of_rest), (offset + START_IMAGE, of_start)]
+            image = sums[bond, down]
+            of_rest += folded(rest[bond, down] * image)
+            of_start += folded(starts[bond, down].astype(F32) * image)
+        places += [bond * BOND_LANES + REST_IMAGE, bond * BOND_LANES + START_IMAGE]
+        parts += [of_rest, of_start]
+    found = list(zip(places, totals(parts)))
     row[...] = jnp.broadcast_to(row_in[0:1, :] + in_lanes(row.shape[1], found), row.shape)
 
 
@@ -412,23 +427,27 @@
 
     size = part(SIZE)
     quotient = part(QUOTIENT)
+    rest_sq = part(REST)
+    start_rest = part(START_REST)
     low = pltpu.roll(quotient, 1, 1)
     high = pltpu.roll(quotient, quotient.shape[1] - 1, 1)
     even = (lane & 1) == 0
     none_low, none_high = lane == first, lane == first + ups - 1
     norm_sq = over_ups(size)
-    alpha_zero = over_ups(size * quotient) / norm_sq
+    alpha_zero = over_ups(size * quotient + start_rest) / norm_sq
     off = quotient - alpha_zero
     off_low = jnp.where(none_low, 0.0, low - alpha_zero)
     off_high = jnp.where(none_high, 0.0, high - alpha_zero)
     off_swapped = jnp.where(even, off_high, off_low)
     off_shifted = jnp.where(even, off_low, off_high)
-    residual_sq = over_ups(part(REST) + size * off * off)
+    along_start = jnp.where(size > 0.0, start_rest / jnp.where(size > 0.0, size, 1.0), 0.0)
+    across_sq = jnp.maximum(rest_sq - start_rest * along_start, 0.0)
+    residual_sq = over_ups(across_sq + size * (off + along_start) * (off + along_start))
     crossed = part(REST_IMAGE) + off * part(START_IMAGE)
     rest_of = [part(REST_OWN), part(REST_SWAPPED)]
     start_of = [part(START_OWN), part(START_SWAPPED)]
-    rest_of.append(part(REST) - rest_of[0] - rest_of[1])
-    start_of.append(quotient * size - start_of[0] - start_of[1])
+    rest_of.append(rest_sq + quotient * start_rest - rest_of[0] - rest_of[1])
+    start_of.append(start_rest + quotient * size - start_of[0] - start_of[1])
     for factor, of_rest, of_start in zip((off, off_swapped, off_shifted), rest_of, start_of):
         crossed += factor * (of_rest + off * of_start)
     alpha_one = over_ups(crossed) / residual_sq
@@ -476,22 +495,25 @@
         return copy
 
     first = [
-        arrival(0, starts_held.at[0], starts.at[0]),
-        arrival(1, rest_held.at[0], rest.at[0]),
-        arrival(2, along_held, along),
-        arrival(3, edge_held, edge),
+        [
+            arrival(0 + 4 * down, starts_held.at[0, down], starts.at[0, down]),
+            arrival(1 + 4 * down, rest_held.at[0, down], rest.at[0, down]),
+            arrival(2 + 4 * down, along_held.at[:, down], along.at[:, down]),
+            arrival(3 + 4 * down, edge_held.at[down], edge.at[down]),
+        ]
+        for down in range(downs)
     ]
     arrivals = [
         pltpu.make_async_copy(mixed_held.at[index], mixed.at[index], mixed_sems.at[index])
         for index in range(channels)
     ]
-    for copy in arrivals[: 2 * BATCH]:
+    for copy in arrivals[:BATCH]:
         copy.start()
     second = [
-        arrival(4, starts_held.at[1], starts.at[1]),
-        arrival(5, rest_held.at[1], rest.at[1]),
+        arrival(4 * downs, starts_held.at[1], starts.at[1]),
+        arrival(4 * downs + 1, rest_held.at[1], rest.at[1]),
     ]
-    for copy in arrivals[2 * BATCH :]:
+    for copy in arrivals[BATCH:]:
         copy.start()
     devices, width = numbers.shape
     segments = devices // ups
@@ -506,7 +528,7 @@
     lane = lax.broadcasted_iota(jnp.int32, energies.shape, 1)
     energies[...] = jnp.where(lane == 0, energy[0], energy[1])
     last = seg == segments - 1
-    out_copies = [pltpu.make_async_copy(energies, energies_out, in_sems.at[6])]
+    out_copies = [pltpu.make_async_copy(energies, energies_out, in_sems.at[4 * downs + 2])]
     out_copies[0].start()
 
     def leave(index, source, target):
@@ -520,10 +542,10 @@
             grounds[bond, down] = of_start[bond] * start + of_rest[bond] * rest[bond, down]
         leave(channels + bond, grounds.at[bond], target)
 
-    for copy in first:
-        copy.wait()
     products = []
     for down in range(downs):
+        for copy in first[down]:
+            copy.wait()
         start = starts[0, down].astype(F32)
         ground = of_start[0] * start + of_rest[0] * rest[0, down]
         grounds[0, down] = ground
@@ -621,39 +643,43 @@
 
     list_shape = (LIST_ROWS, channels * downs + 1)
     sources = pltpu.VMEM((BONDS, 2 * downs, block, block), BF16)
-    *loaded, images, row, lists = call(
+    *loaded, images, near_rest, row, lists = call(
         opening,
         "opening",
-        [SMEM, VMEM, VMEM] + [HBM] * 4,
+        [HBM, VMEM, VMEM] + [HBM] * 4,
         [(VMEM, pltpu.VMEM(env_shape, BF16))] * 4
         + [
             (VMEM, pltpu.VMEM((2,) + both, F32)),
+            (VMEM, pltpu.VMEM(both, F32)),
             (VMEM, tile),
             (SMEM, jax.ShapeDtypeStruct(list_shape, jnp.int32)),
         ],
-        [sources, pltpu.SemaphoreType.DMA((channels,))],
+        [
+            sources,
+            pltpu.SMEM((channels,), jnp.int32),
+            pltpu.SemaphoreType.DMA(()),
+            pltpu.SemaphoreType.DMA((channels,)),
+        ],
         apply_flops,
         5 * env_bytes,
     )(in_hbm(term_shift), starts, swapped, *held)
 
-    rest, sent, row = call(
+    rest, sent = call(
         first_images,
         "first_images",
-        [VMEM, HBM] + [VMEM] * 8,
+        [VMEM, HBM] + [VMEM] * 6,
         [
             (VMEM, pltpu.VMEM(both, F32)),
             (VMEM, pltpu.VMEM(both, BF16)),
-            (VMEM, tile),
-        ],
-        [
-            pltpu.VMEM((1,) + both, F32),
+        ],
+        [
             pltpu.SMEM(list_shape, jnp.int32),
             pltpu.SMEM(sizes.shape, jnp.int32),
             pltpu.SemaphoreType.DMA((2,)),
         ],
         apply_flops,
         env_bytes,
-    )(lists, sizes, *loaded, starts, shifted, images, row)
+    )(lists, sizes, *loaded, shifted, near_rest)
     swapped, shifted = swapped_pairs(sent), shifted_pairs(sent)
     row, sums, along = call(
         early_seconds,
@@ -717,7 +743,7 @@
             pltpu.VMEM(env_shape, BF16),
             pltpu.VMEM(env_shape, BF16),
             pltpu.VMEM(both, F32),
-            pltpu.SemaphoreType.DMA((7,)),
+            pltpu.SemaphoreType.DMA((4 * downs + 3,)),
             pltpu.SemaphoreType.DMA((channels,)),
             pltpu.SemaphoreType.DMA((channels + BONDS,)),
         ],

time: 49.3 us -> 47.5 us (0.963)
  starting transfers between devices: 17.1 us -> 15.6 us
  Pallas kernels: 25.4 us -> 24.8 us
    all_to_all x1, starting transfers between devices: 10.7 us -> 9.54 us  [local(): numbers = lax.all_to_all(row, ('seg', 'blk'), 0, 0, tiled=True)]
    pallas_call x1, Pallas kernels: 3.33 us -> 4.17 us  [local(): call(early_seconds, 'early_seconds', [VMEM] * 11, [(VMEM, tile), (VMEM, p...]
    pallas_call x1, Pallas kernels: 3.01 us -> 2.27 us  [local(): call(late_seconds, 'late_seconds', [VMEM] * 10, [(VMEM, pltpu.VMEM((devic...]
    pallas_call x2, Pallas kernels: 9.22 us -> 8.57 us  [the longest x1 7.04 us: local(): call(opening, 'opening', [HBM, VMEM, VMEM] + [HBM] * 4, [(VMEM, pltpu.VME...]
  transfers between devices with their start and end apart: 6 -> 6, of which waited for: 3 -> 3; matrix products, arithmetic and copies ran while one was open for 0% -> 0% of each run, Pallas kernels for 31% -> 34%
where the time goes in v5:
time: 47.5 us; the launch traced here: 47.3 us
  Pallas kernels  24.8 us (52%)
  starting transfers between devices  15.6 us (33%)
  waiting for transfers between devices  4.3 us (9%)
  local copies, waits for them, and re-layouts  1.64 us (3%)
  between operations  0.94 us (2%)
    all_to_all x1, starting transfers between devices, local(): numbers = lax.all_to_all(row, ('seg', 'blk'), 0, 0, tiled=True)  9.54 us
    pallas_call x1, Pallas kernels, local(): call(opening, 'opening', [HBM, VMEM, VMEM] + [HBM] * 4, [(VMEM, pltpu.VME...  7.04 us
    pallas_call x1, Pallas kernels, local(): call(functools.partial(finish, 1.0 / block, ups), 'finish', [VMEM] + [HBM...  5.92 us
    pallas_call x1, Pallas kernels, local(): call(early_seconds, 'early_seconds', [VMEM] * 11, [(VMEM, tile), (VMEM, p...  4.17 us
    ppermute x2, starting transfers between devices, swapped_pairs(): lax.ppermute(block, 'blk', [(i, i ^ 1) for i in devices if i ^ 1 in devic...  3.45 us
    pallas_call x1, Pallas kernels, local(): call(mixing, 'mixing', [VMEM, VMEM, HBM], [(VMEM, jax.ShapeDtypeStruct(en...  2.64 us
    all_to_all x1, waiting for transfers between devices, local(): numbers = lax.all_to_all(row, ('seg', 'blk'), 0, 0, tiled=True)  2.6 us
    pallas_call x1, Pallas kernels, local(): call(late_seconds, 'late_seconds', [VMEM] * 10, [(VMEM, pltpu.VMEM((devic...  2.27 us
  transfers between devices with their start and end apart: 6, of which 3 were waited for; matrix products, arithmetic and copies ran while one was open for 0% of the time, Pallas kernels for 34%

profile of v5, /device:TPU:0, one launch (start us, length us, event | category | flops | bytes accessed | tf_op | source)
XLA Modules:
  0.0 47.3 jit_solution(4598349158547080467)
XLA Ops:
  0.6 1.2 %masked_starts.1.starts.starts_held = bf16[2,2,256,256]{3,2,1,0:T(8,128)(2,1)S(1)} custom-call(s32[1,1,2,4]{3,2,1,0:T(2,128)} %bitcast.24, bf16[2,256,256]{2,1,0:T(8,128)(2,1)} %bitcast.22, bf16[2,256,256]{2,1,0:T(8,128)(2,1)} %bitcast.23), custom_call_target="tpu_custom_call" | custom-call | flops 524288 | bytes 1048576 | tf_op jit(solution)/shard_map/masked_starts/pallas_call | solution.py:633
  1.8 0.0 copy-start
  1.8 0.5 %collective-permute-start = (bf16[2,2,256,256]{3,2,1,0:T(8,128)(2,1)S(1)}, bf16[2,2,256,256]{3,2,1,0:T(8,128)(2,1)S(1)}, u32[]{:S(2)}, u32[]{:S(2)}) collective-permute-start(bf16[2,2,256,256]{3,2,1,0:T(8,128)(2,1)S(1)} %masked_starts.1.starts.starts_held), channel_id=1, source_target_pairs={{0,1},{1,0},{2,3},{3,2},{4,5},{5,4},{6,7},{7,6},{8,9},{9,8},{10,11... | collective-permute-start | bytes 1572872 | tf_op jit(solution)/shard_map/ppermute | solution.py:592
  2.4 0.7 %collective-permute-start.1 = (bf16[2,2,256,256]{3,2,1,0:T(8,128)(2,1)S(1)}, bf16[2,2,256,256]{3,2,1,0:T(8,128)(2,1)S(1)}, u32[]{:S(2)}, u32[]{:S(2)}) collective-permute-start(bf16[2,2,256,256]{3,2,1,0:T(8,128)(2,1)S(1)} %masked_starts.1.starts.starts_held), channel_id=1, source_target_pairs={{1,2},{3,4},{5,6},{2,1},{4,3},{6,5},{9,10},{11,12},{13,14},{10,9},... | collective-permute-start | bytes 1572872 | tf_op jit(solution)/shard_map/ppermute | solution.py:598
  3.0 0.8 %collective-permute-done.swapped = bf16[2,2,256,256]{3,2,1,0:T(8,128)(2,1)S(1)} collective-permute-done((bf16[2,2,256,256]{3,2,1,0:T(8,128)(2,1)S(1)}, bf16[2,2,256,256]{3,2,1,0:T(8,128)(2,1)S(1)}, u32[]{:S(2)}, u32[]{:S(2)}) %collective-permute-start) | collective-permute-done | bytes 524320 | tf_op jit(solution)/shard_map/ppermute | solution.py:592
  3.9 7.0 %opening.1 = (bf16[12,2,256,256]{3,2,1,0:T(8,128)(2,1)S(1)}, bf16[12,2,256,256]{3,2,1,0:T(8,128)(2,1)S(1)}, bf16[12,2,256,256]{3,2,1,0:T(8,128)(2,1)S(1)}, bf16[...) custom-call(s32[12]{0:T(128)} %shift_held.1, ...), custom_call_target="tpu_custom_call" | custom-call | flops 1610612736 | bytes 15728640 | tf_op jit(solution)/shard_map/opening/pallas_call | solution.py:646
  10.9 0.0 collective-permute-done.1.shifted
  11.0 1.5 %first_images.1 = (f32[2,2,256,256]{3,2,1,0:T(8,128)S(1)}, bf16[2,2,256,256]{3,2,1,0:T(8,128)(2,1)S(1)}) custom-call(s32[9,25]{1,0:T(8,128)S(1)} %get-tuple-element.21.lists_held, s32[1,1,2,4]{3,2,1,0:T(2,128)} %bitcast.25, bf16[12,2,256,256]{3,2,1,0:T(8,128)(2,1)S(1)} %get-tuple-element.22.left_a.env, ...), custom_call_target="tpu_custom_call" | custom-call | flops 1610612736 | bytes 3145728 | tf_op jit(solution)/shard_map/first_images/pallas_call | solution.py:667
  12.5 0.0 copy-start.1
  12.5 2.9 %collective-permute-start.3 = (bf16[2,2,256,256]{3,2,1,0:T(8,128)(2,1)S(1)}, bf16[2,2,256,256]{3,2,1,0:T(8,128)(2,1)S(1)}, u32[]{:S(2)}, u32[]{:S(2)}) collective-permute-start(bf16[2,2,256,256]{3,2,1,0:T(8,128)(2,1)S(1)} %get-tuple-element.27.sent), channel_id=1, source_target_pairs={{0,1},{1,0},{2,3},{3,2},{4,5},{5,4},{6,7},{7,6},{8,9},{9,8},{10,11... | collective-permute-start | bytes 1572872 | tf_op jit(solution)/shard_map/ppermute | solution.py:592
  15.4 0.7 %collective-permute-start.2 = (bf16[2,2,256,256]{3,2,1,0:T(8,128)(2,1)S(1)}, bf16[2,2,256,256]{3,2,1,0:T(8,128)(2,1)S(1)}, u32[]{:S(2)}, u32[]{:S(2)}) collective-permute-start(bf16[2,2,256,256]{3,2,1,0:T(8,128)(2,1)S(1)} %get-tuple-element.27.sent), channel_id=1, source_target_pairs={{1,2},{3,4},{5,6},{2,1},{4,3},{6,5},{9,10},{11,12},{13,14},{10,9},... | collective-permute-start | bytes 1572872 | tf_op jit(solution)/shard_map/ppermute | solution.py:598
  16.1 0.8 %collective-permute-done.3.swapped = bf16[2,2,256,256]{3,2,1,0:T(8,128)(2,1)S(1)} collective-permute-done((bf16[2,2,256,256]{3,2,1,0:T(8,128)(2,1)S(1)}, bf16[2,2,256,256]{3,2,1,0:T(8,128)(2,1)S(1)}, u32[]{:S(2)}, u32[]{:S(2)}) %collective-permute-start.3) | collective-permute-done | bytes 524320 | tf_op jit(solution)/shard_map/ppermute | solution.py:592
  17.0 4.2 %early_seconds.1 = (f32[8,128]{1,0:T(8,128)S(1)}, f32[2,2,256,256]{3,2,1,0:T(8,128)S(1)}, bf16[2,2,256,256]{3,2,1,0:T(8,128)(2,1)}) custom-call(s32[9,25]{1,0:T(8,128)S(1)} %get-tuple-element.21.lists_held, bf16[12,2,256,256]{3,2,1,0:T(8,128)(2,1)S(1)} %get-tuple-element.22.left_a.env, bf16[12,2,256,256]{3,2,1,0:T(8,128)(2,1)S(1)} %get-tuple-element.23.right_a, ...), custom_call_target="tpu_custom_call" | custom-call | flops 1610612736 | bytes 3145728 | tf_op jit(solution)/shard_map/early_seconds/pallas_call | solution.py:684
  21.2 1.3 %collective-permute-start.4 = (bf16[2,2,256,256]{3,2,1,0:T(8,128)(2,1)}, bf16[2,2,256,256]{3,2,1,0:T(8,128)(2,1)}, u32[]{:S(2)}, u32[]{:S(2)}) collective-permute-start(bf16[2,2,256,256]{3,2,1,0:T(8,128)(2,1)} %get-tuple-element.33), channel_id=1, source_target_pairs={{8,0},{16,8},{24,16},{9,1},{17,9},{25,17},{10,2},{18,10},{26,18},{... | collective-permute-start | bytes 1572872 | tf_op jit(solution)/shard_map/ppermute | solution.py:603
  22.5 0.0 collective-permute-done.2.shifted
  22.5 0.0 copy-done
  22.5 0.0 copy-done.1
  22.5 0.0 copy-start.3
  22.5 2.3 %late_seconds.1.after = f32[32,128]{1,0:T(8,128)} custom-call(s32[9,25]{1,0:T(8,128)S(1)} %get-tuple-element.21.lists_held, bf16[12,2,256,256]{3,2,1,0:T(8,128)(2,1)S(1)} %get-tuple-element.22.left_a.env, bf16[12,2,256,256]{3,2,1,0:T(8,128)(2,1)S(1)} %get-tuple-element.23.right_a, bf16[12,2,256,256]{3,2,1,0:T(8,128)(2,1)S(1)} %get-tuple-element.24.left_b, ...), custom_call_target="tpu_custom_call" | custom-call | flops 1610612736 | bytes 3145728 | tf_op jit(solution)/shard_map/late_seconds/pallas_call | solution.py:703
  24.8 9.5 %all-to-all-start = ((f32[32,1,128]{2,1,0:T(1,128)}), f32[32,1,128]{2,1,0:T(1,128)S(1)}, u32[]{:S(2)}, u32[]{:S(2)}) async-start(f32[32,1,128]{2,1,0:T(1,128)} %bitcast.8), calls=%async_computation | async-start | bytes 32768 | tf_op jit(solution)/shard_map/all_to_all | solution.py:716
  34.3 0.0 copy-done.3
  34.3 2.6 %mixing.1.mixed_held = bf16[12,2,256,256]{3,2,1,0:T(8,128)(2,1)S(1)} custom-call(f32[12,12]{1,0:T(8,128)S(1)} %copy-done.3, bf16[12,2,256,256]{3,2,1,0:T(8,128)(2,1)S(1)} %get-tuple-element.22.left_a.env, f32[32,128]{1,0:T(8,128)} %late_seconds.1.after), custom_call_target="tpu_custom_call" | custom-call | flops 1207959552 | bytes 6291456 | tf_op jit(solution)/shard_map/mixing/pallas_call | solution.py:717
  37.0 0.0 copy-start.2
  37.0 1.6 %copy-done.2 = bf16[12,2,256,256]{3,2,1,0:T(8,128)(2,1)} copy-done((bf16[12,2,256,256]{3,2,1,0:T(8,128)(2,1)}, bf16[12,2,256,256]{3,2,1,0:T(8,128)(2,1)S(1)}, u32[]{:S(2)}) %copy-start.2) | copy-done | bytes 3145752
  38.6 2.6 %all-to-all-done = f32[32,1,128]{2,1,0:T(1,128)S(1)} async-done(((f32[32,1,128]{2,1,0:T(1,128)}), f32[32,1,128]{2,1,0:T(1,128)S(1)}, u32[]{:S(2)}, u32[]{:S(2)}) %all-to-all-start) | async-done | bytes 16416 | tf_op jit(solution)/shard_map/all_to_all | solution.py:716
  41.2 0.0 collective-permute-done.4.along_held
  41.2 5.9 %finish.1 = (f32[2,256,256]{2,1,0:T(8,128)}, f32[2,256,256]{2,1,0:T(8,128)}, f32[1,2]{1,0:T(1,128)}, bf16[12,2,256,256]{3,2,1,0:T(8,128)(2,1)}) custom-call(f32[32,128]{1,0:T(8,128)S(1)} %bitcast.17, bf16[2,2,256,256]{3,2,1,0:T(8,128)(2,1)} %copy-done, f32[2,2,256,256]{3,2,1,0:T(8,128)} %copy-done.1, ...), custom_call_target="tpu_custom_call" | custom-call | flops 1610612736 | bytes 6291456 | tf_op jit(solution)/shard_map/finish/pallas_call | solution.py:727
Async XLA Ops:
  1.8 20.6 %copy-start = (bf16[2,2,256,256]{3,2,1,0:T(8,128)(2,1)}, bf16[2,2,256,256]{3,2,1,0:T(8,128)(2,1)S(1)}, u32[]{:S(2)}) copy-start(bf16[2,2,256,256]{3,2,1,0:T(8,128)(2,1)S(1)} %masked_starts.1.starts.starts_held) | copy-start | bytes 1572868
  1.8 2.1 %collective-permute-start = (bf16[2,2,256,256]{3,2,1,0:T(8,128)(2,1)S(1)}, bf16[2,2,256,256]{3,2,1,0:T(8,128)(2,1)S(1)}, u32[]{:S(2)}, u32[]{:S(2)}) collective-permute-start(bf16[2,2,256,256]{3,2,1,0:T(8,128)(2,1)S(1)} %masked_starts.1.starts.starts_held), channel_id=1, source_target_pairs={{0,1},{1,0},{2,3},{3,2},{4,5},{5,4},{6,7},{7,6},{8,9},{9,8},{10,11... | collective-permute-start | bytes 1572872 | tf_op jit(solution)/shard_map/ppermute | solution.py:592
  2.4 8.6 %collective-permute-start.1 = (bf16[2,2,256,256]{3,2,1,0:T(8,128)(2,1)S(1)}, bf16[2,2,256,256]{3,2,1,0:T(8,128)(2,1)S(1)}, u32[]{:S(2)}, u32[]{:S(2)}) collective-permute-start(bf16[2,2,256,256]{3,2,1,0:T(8,128)(2,1)S(1)} %masked_starts.1.starts.starts_held), channel_id=1, source_target_pairs={{1,2},{3,4},{5,6},{2,1},{4,3},{6,5},{9,10},{11,12},{13,14},{10,9},... | collective-permute-start | bytes 1572872 | tf_op jit(solution)/shard_map/ppermute | solution.py:598
  12.5 10.0 %copy-start.1 = (f32[2,2,256,256]{3,2,1,0:T(8,128)}, f32[2,2,256,256]{3,2,1,0:T(8,128)S(1)}, u32[]{:S(2)}) copy-start(f32[2,2,256,256]{3,2,1,0:T(8,128)S(1)} %get-tuple-element.28.rest.rest_held) | copy-start | bytes 3145732
  12.5 4.5 %collective-permute-start.3 = (bf16[2,2,256,256]{3,2,1,0:T(8,128)(2,1)S(1)}, bf16[2,2,256,256]{3,2,1,0:T(8,128)(2,1)S(1)}, u32[]{:S(2)}, u32[]{:S(2)}) collective-permute-start(bf16[2,2,256,256]{3,2,1,0:T(8,128)(2,1)S(1)} %get-tuple-element.27.sent), channel_id=1, source_target_pairs={{0,1},{1,0},{2,3},{3,2},{4,5},{5,4},{6,7},{7,6},{8,9},{9,8},{10,11... | collective-permute-start | bytes 1572872 | tf_op jit(solution)/shard_map/ppermute | solution.py:592
  15.4 7.0 %collective-permute-start.2 = (bf16[2,2,256,256]{3,2,1,0:T(8,128)(2,1)S(1)}, bf16[2,2,256,256]{3,2,1,0:T(8,128)(2,1)S(1)}, u32[]{:S(2)}, u32[]{:S(2)}) collective-permute-start(bf16[2,2,256,256]{3,2,1,0:T(8,128)(2,1)S(1)} %get-tuple-element.27.sent), channel_id=1, source_target_pairs={{1,2},{3,4},{5,6},{2,1},{4,3},{6,5},{9,10},{11,12},{13,14},{10,9},... | collective-permute-start | bytes 1572872 | tf_op jit(solution)/shard_map/ppermute | solution.py:598
  21.2 20.1 %collective-permute-start.4 = (bf16[2,2,256,256]{3,2,1,0:T(8,128)(2,1)}, bf16[2,2,256,256]{3,2,1,0:T(8,128)(2,1)}, u32[]{:S(2)}, u32[]{:S(2)}) collective-permute-start(bf16[2,2,256,256]{3,2,1,0:T(8,128)(2,1)} %get-tuple-element.33), channel_id=1, source_target_pairs={{8,0},{16,8},{24,16},{9,1},{17,9},{25,17},{10,2},{18,10},{26,18},{... | collective-permute-start | bytes 1572872 | tf_op jit(solution)/shard_map/ppermute | solution.py:603
  22.5 11.8 %copy-start.3 = (f32[12,12]{1,0:T(8,128)S(1)}, f32[12,12]{1,0:T(8,128)}, u32[]{:S(2)}) copy-start(f32[12,12]{1,0:T(8,128)} %mix.1) | copy-start | bytes 1732
  24.8 16.4 %all-to-all-start = ((f32[32,1,128]{2,1,0:T(1,128)}), f32[32,1,128]{2,1,0:T(1,128)S(1)}, u32[]{:S(2)}, u32[]{:S(2)}) async-start(f32[32,1,128]{2,1,0:T(1,128)} %bitcast.8), calls=%async_computation | async-start | bytes 32768 | tf_op jit(solution)/shard_map/all_to_all | solution.py:716
  37.0 1.6 %copy-start.2 = (bf16[12,2,256,256]{3,2,1,0:T(8,128)(2,1)}, bf16[12,2,256,256]{3,2,1,0:T(8,128)(2,1)S(1)}, u32[]{:S(2)}) copy-start(bf16[12,2,256,256]{3,2,1,0:T(8,128)(2,1)S(1)} %mixing.1.mixed_held) | copy-start | bytes 9437188

commit v6 on v5

--- a/solution.py
+++ b/solution.py
@@ -104,18 +104,16 @@
     sizes_copy = pltpu.make_async_copy(sizes_held, sizes, size_sem)
     sizes_copy.start()
     downs, block = starts.shape[1], starts.shape[-1]
-    places = [(bond, down) for bond in range(BONDS) for down in range(downs)]
     copies = [
-        pltpu.make_async_copy(
-            (guess_a, guess_b)[bond].at[down], starts.at[bond, down], sems.at[bond, down]
-        )
-        for bond, down in places
+        pltpu.make_async_copy(guess, starts.at[bond], sems.at[bond])
+        for bond, guess in enumerate((guess_a, guess_b))
     ]
     for copy in copies:
         copy.start()
     sizes_copy.wait()
-    for copy, (bond, down) in zip(copies, places):
-        copy.wait()
+    for bond, down in [(bond, down) for bond in range(BONDS) for down in range(downs)]:
+        if down == 0:
+            copies[bond].wait()
         start = starts[bond, down]
         starts[bond, down] = jnp.where(
             live_of(sizes, bond, down, block), start, jnp.zeros_like(start)
@@ -495,25 +493,26 @@
         return copy
 
     first = [
-        [
-            arrival(0 + 4 * down, starts_held.at[0, down], starts.at[0, down]),
-            arrival(1 + 4 * down, rest_held.at[0, down], rest.at[0, down]),
-            arrival(2 + 4 * down, along_held.at[:, down], along.at[:, down]),
-            arrival(3 + 4 * down, edge_held.at[down], edge.at[down]),
-        ]
-        for down in range(downs)
+        arrival(0, starts_held.at[0], starts.at[0]),
+        arrival(1, rest_held.at[0], rest.at[0]),
+        arrival(2, along_held, along),
+        arrival(3, edge_held, edge),
     ]
+    groups = []
+    while sum(map(len, groups)) < channels:
+        at = sum(map(len, groups))
+        groups.append(range(at, at + min(BATCH, (channels - at + 1) // 2)))
+
+    def part(array, group):
+        return array.at[group.start : group.stop]
+
     arrivals = [
-        pltpu.make_async_copy(mixed_held.at[index], mixed.at[index], mixed_sems.at[index])
-        for index in range(channels)
+        pltpu.make_async_copy(part(mixed_held, group), part(mixed, group), mixed_sems.at[index])
+        for index, group in enumerate(groups)
     ]
-    for copy in arrivals[:BATCH]:
-        copy.start()
-    second = [
-        arrival(4 * downs, starts_held.at[1], starts.at[1]),
-        arrival(4 * downs + 1, rest_held.at[1], rest.at[1]),
-    ]
-    for copy in arrivals[BATCH:]:
+    arrivals[0].start()
+    second = [arrival(4, starts_held.at[1], starts.at[1]), arrival(5, rest_held.at[1], rest.at[1])]
+    for copy in arrivals[1:]:
         copy.start()
     devices, width = numbers.shape
     segments = devices // ups
@@ -528,7 +527,7 @@
     lane = lax.broadcasted_iota(jnp.int32, energies.shape, 1)
     energies[...] = jnp.where(lane == 0, energy[0], energy[1])
     last = seg == segments - 1
-    out_copies = [pltpu.make_async_copy(energies, energies_out, in_sems.at[4 * downs + 2])]
+    out_copies = [pltpu.make_async_copy(energies, energies_out, in_sems.at[6])]
     out_copies[0].start()
 
     def leave(index, source, target):
@@ -542,10 +541,10 @@
             grounds[bond, down] = of_start[bond] * start + of_rest[bond] * rest[bond, down]
         leave(channels + bond, grounds.at[bond], target)
 
+    for copy in first:
+        copy.wait()
     products = []
     for down in range(downs):
-        for copy in first[down]:
-            copy.wait()
         start = starts[0, down].astype(F32)
         ground = of_start[0] * start + of_rest[0] * rest[0, down]
         grounds[0, down] = ground
@@ -556,20 +555,14 @@
     leave(channels, grounds.at[0], ground_a)
     halves = {}
 
-    def last_product(group):
-        for channel in group:
+    def last_product(index):
+        for channel in groups[index]:
             for down, (_, turned) in enumerate(products):
                 made[channel, down] = dot(turned, halves[channel, down]).astype(BF16)
-        for channel in group:
-            leave(channel, made.at[channel], boundary.at[channel])
-
-    groups = []
-    while sum(map(len, groups)) < channels:
-        at = sum(map(len, groups))
-        groups.append(range(at, at + min(BATCH, (channels - at + 1) // 2)))
+        leave(index, part(made, groups[index]), part(boundary, groups[index]))
+
     for index, group in enumerate(groups):
-        for channel in group:
-            arrivals[channel].wait()
+        arrivals[index].wait()
         for down, (product, _) in enumerate(products):
             block = product.shape[0]
             stacked = mixed[group.start : group.stop, down].reshape(len(group) * block, block)
@@ -577,12 +570,12 @@
             for place, channel in enumerate(group):
                 halves[channel, down] = half[place * block : (place + 1) * block]
         if index > 0:
-            last_product(groups[index - 1])
+            last_product(index - 1)
         if index == min(1, len(groups) - 1):
             for copy in second:
                 copy.wait()
             ground_of(1, ground_b)
-    last_product(groups[-1])
+    last_product(len(groups) - 1)
     for copy in out_copies:
         copy.wait()
 
@@ -635,7 +628,7 @@
         "masked_starts",
         [HBM, HBM, HBM],
         [(VMEM, pltpu.VMEM(both, BF16))],
-        [pltpu.SMEM(sizes.shape, jnp.int32), pltpu.SemaphoreType.DMA(()), pltpu.SemaphoreType.DMA((BONDS, downs))],
+        [pltpu.SMEM(sizes.shape, jnp.int32), pltpu.SemaphoreType.DMA(()), pltpu.SemaphoreType.DMA((BONDS,))],
         4 * downs * block * block,
         4 * bits,
     )(sizes, in_hbm(guess_a.reshape(pair)), in_hbm(guess_b.reshape(pair)))
@@ -743,7 +736,7 @@
             pltpu.VMEM(env_shape, BF16),
             pltpu.VMEM(env_shape, BF16),
             pltpu.VMEM(both, F32),
-            pltpu.SemaphoreType.DMA((4 * downs + 3,)),
+            pltpu.SemaphoreType.DMA((7,)),
             pltpu.SemaphoreType.DMA((channels,)),
             pltpu.SemaphoreType.DMA((channels + BONDS,)),
         ],

time: 47.5 us -> 48.6 us (1.023); the launches traced: 47.3 us -> 49.2 us
  starting transfers between devices: 15.6 us -> 17 us
  Pallas kernels: 24.8 us -> 25.3 us
    all_to_all x1, starting transfers between devices: 9.54 us -> 11.8 us  [local(): numbers = lax.all_to_all(row, ('seg', 'blk'), 0, 0, tiled=True)]
    pallas_call x1, Pallas kernels: 1.53 us -> 2.71 us  [local(): call(first_images, 'first_images', [VMEM, HBM] + [VMEM] * 6, [(VMEM, pltp...]
    pallas_call x1, Pallas kernels: 2.27 us -> 3.45 us  [local(): call(late_seconds, 'late_seconds', [VMEM] * 10, [(VMEM, pltpu.VMEM((devic...]
    pallas_call x1, Pallas kernels: 4.17 us -> 3.06 us  [local(): call(early_seconds, 'early_seconds', [VMEM] * 11, [(VMEM, tile), (VMEM, p...]
    ppermute x2, starting transfers between devices: 3.45 us -> 2.49 us  [swapped_pairs(): lax.ppermute(block, 'blk', [(i, i ^ 1) for i in devices if i ^ 1 in devic...]
  transfers between devices with their start and end apart: 6 -> 6, of which waited for: 3 -> 3; matrix products, arithmetic and copies ran while one was open for 0% -> 0% of each run, Pallas kernels for 34% -> 32%
where the time goes in v6:
time: 48.6 us; the launch traced here: 49.2 us
  Pallas kernels  25.3 us (52%)
  starting transfers between devices  17 us (35%)
  waiting for transfers between devices  4.3 us (9%)
  local copies, waits for them, and re-layouts  1.64 us (3%)
  between operations  0.94 us (2%)
    all_to_all x1, starting transfers between devices, local(): numbers = lax.all_to_all(row, ('seg', 'blk'), 0, 0, tiled=True)  11.8 us
    pallas_call x1, Pallas kernels, local(): call(opening, 'opening', [HBM, VMEM, VMEM] + [HBM] * 4, [(VMEM, pltpu.VME...  6.82 us
    pallas_call x1, Pallas kernels, local(): call(functools.partial(finish, 1.0 / block, ups), 'finish', [VMEM] + [HBM...  5.48 us
    pallas_call x1, Pallas kernels, local(): call(late_seconds, 'late_seconds', [VMEM] * 10, [(VMEM, pltpu.VMEM((devic...  3.45 us
    pallas_call x1, Pallas kernels, local(): call(early_seconds, 'early_seconds', [VMEM] * 11, [(VMEM, tile), (VMEM, p...  3.06 us
    pallas_call x1, Pallas kernels, local(): call(first_images, 'first_images', [VMEM, HBM] + [VMEM] * 6, [(VMEM, pltp...  2.71 us
    pallas_call x1, Pallas kernels, local(): call(mixing, 'mixing', [VMEM, VMEM, HBM], [(VMEM, jax.ShapeDtypeStruct(en...  2.64 us
    all_to_all x1, waiting for transfers between devices, local(): numbers = lax.all_to_all(row, ('seg', 'blk'), 0, 0, tiled=True)  2.6 us
  transfers between devices with their start and end apart: 6, of which 3 were waited for; matrix products, arithmetic and copies ran while one was open for 0% of the time, Pallas kernels for 32%

profile of v6, /device:TPU:0, one launch (start us, length us, event | category | flops | bytes accessed | tf_op | source)
XLA Modules:
  0.0 49.2 jit_solution(9480136440201153877)
XLA Ops:
  0.6 1.2 %masked_starts.1.starts.starts_held = bf16[2,2,256,256]{3,2,1,0:T(8,128)(2,1)S(1)} custom-call(s32[1,1,2,4]{3,2,1,0:T(2,128)} %bitcast.24, bf16[2,256,256]{2,1,0:T(8,128)(2,1)} %bitcast.22, bf16[2,256,256]{2,1,0:T(8,128)(2,1)} %bitcast.23), custom_call_target="tpu_custom_call" | custom-call | flops 524288 | bytes 1048576 | tf_op jit(solution)/shard_map/masked_starts/pallas_call | solution.py:626
  1.8 0.0 copy-start
  1.8 0.5 %collective-permute-start = (bf16[2,2,256,256]{3,2,1,0:T(8,128)(2,1)S(1)}, bf16[2,2,256,256]{3,2,1,0:T(8,128)(2,1)S(1)}, u32[]{:S(2)}, u32[]{:S(2)}) collective-permute-start(bf16[2,2,256,256]{3,2,1,0:T(8,128)(2,1)S(1)} %masked_starts.1.starts.starts_held), channel_id=1, source_target_pairs={{0,1},{1,0},{2,3},{3,2},{4,5},{5,4},{6,7},{7,6},{8,9},{9,8},{10,11... | collective-permute-start | bytes 1572872 | tf_op jit(solution)/shard_map/ppermute | solution.py:585
  2.4 0.7 %collective-permute-start.1 = (bf16[2,2,256,256]{3,2,1,0:T(8,128)(2,1)S(1)}, bf16[2,2,256,256]{3,2,1,0:T(8,128)(2,1)S(1)}, u32[]{:S(2)}, u32[]{:S(2)}) collective-permute-start(bf16[2,2,256,256]{3,2,1,0:T(8,128)(2,1)S(1)} %masked_starts.1.starts.starts_held), channel_id=1, source_target_pairs={{1,2},{3,4},{5,6},{2,1},{4,3},{6,5},{9,10},{11,12},{13,14},{10,9},... | collective-permute-start | bytes 1572872 | tf_op jit(solution)/shard_map/ppermute | solution.py:591
  3.0 0.8 %collective-permute-done.swapped = bf16[2,2,256,256]{3,2,1,0:T(8,128)(2,1)S(1)} collective-permute-done((bf16[2,2,256,256]{3,2,1,0:T(8,128)(2,1)S(1)}, bf16[2,2,256,256]{3,2,1,0:T(8,128)(2,1)S(1)}, u32[]{:S(2)}, u32[]{:S(2)}) %collective-permute-start) | collective-permute-done | bytes 524320 | tf_op jit(solution)/shard_map/ppermute | solution.py:585
  3.9 6.8 %opening.1 = (bf16[12,2,256,256]{3,2,1,0:T(8,128)(2,1)S(1)}, bf16[12,2,256,256]{3,2,1,0:T(8,128)(2,1)S(1)}, bf16[12,2,256,256]{3,2,1,0:T(8,128)(2,1)S(1)}, bf16[...) custom-call(s32[12]{0:T(128)} %shift_held.1, ...), custom_call_target="tpu_custom_call" | custom-call | flops 1610612736 | bytes 15728640 | tf_op jit(solution)/shard_map/opening/pallas_call | solution.py:639
  10.7 0.0 collective-permute-done.1.shifted
  10.7 2.7 %first_images.1 = (f32[2,2,256,256]{3,2,1,0:T(8,128)S(1)}, bf16[2,2,256,256]{3,2,1,0:T(8,128)(2,1)S(1)}) custom-call(s32[9,25]{1,0:T(8,128)S(1)} %get-tuple-element.21.lists_held, s32[1,1,2,4]{3,2,1,0:T(2,128)} %bitcast.25, bf16[12,2,256,256]{3,2,1,0:T(8,128)(2,1)S(1)} %get-tuple-element.22.left_a.env, ...), custom_call_target="tpu_custom_call" | custom-call | flops 1610612736 | bytes 3145728 | tf_op jit(solution)/shard_map/first_images/pallas_call | solution.py:660
  13.4 0.0 copy-start.1
  13.5 2.0 %collective-permute-start.3 = (bf16[2,2,256,256]{3,2,1,0:T(8,128)(2,1)S(1)}, bf16[2,2,256,256]{3,2,1,0:T(8,128)(2,1)S(1)}, u32[]{:S(2)}, u32[]{:S(2)}) collective-permute-start(bf16[2,2,256,256]{3,2,1,0:T(8,128)(2,1)S(1)} %get-tuple-element.27.sent), channel_id=1, source_target_pairs={{0,1},{1,0},{2,3},{3,2},{4,5},{5,4},{6,7},{7,6},{8,9},{9,8},{10,11... | collective-permute-start | bytes 1572872 | tf_op jit(solution)/shard_map/ppermute | solution.py:585
  15.4 0.7 %collective-permute-start.2 = (bf16[2,2,256,256]{3,2,1,0:T(8,128)(2,1)S(1)}, bf16[2,2,256,256]{3,2,1,0:T(8,128)(2,1)S(1)}, u32[]{:S(2)}, u32[]{:S(2)}) collective-permute-start(bf16[2,2,256,256]{3,2,1,0:T(8,128)(2,1)S(1)} %get-tuple-element.27.sent), channel_id=1, source_target_pairs={{1,2},{3,4},{5,6},{2,1},{4,3},{6,5},{9,10},{11,12},{13,14},{10,9},... | collective-permute-start | bytes 1572872 | tf_op jit(solution)/shard_map/ppermute | solution.py:591
  16.1 0.8 %collective-permute-done.3.swapped = bf16[2,2,256,256]{3,2,1,0:T(8,128)(2,1)S(1)} collective-permute-done((bf16[2,2,256,256]{3,2,1,0:T(8,128)(2,1)S(1)}, bf16[2,2,256,256]{3,2,1,0:T(8,128)(2,1)S(1)}, u32[]{:S(2)}, u32[]{:S(2)}) %collective-permute-start.3) | collective-permute-done | bytes 524320 | tf_op jit(solution)/shard_map/ppermute | solution.py:585
  17.0 3.1 %early_seconds.1 = (f32[8,128]{1,0:T(8,128)S(1)}, f32[2,2,256,256]{3,2,1,0:T(8,128)S(1)}, bf16[2,2,256,256]{3,2,1,0:T(8,128)(2,1)}) custom-call(s32[9,25]{1,0:T(8,128)S(1)} %get-tuple-element.21.lists_held, bf16[12,2,256,256]{3,2,1,0:T(8,128)(2,1)S(1)} %get-tuple-element.22.left_a.env, bf16[12,2,256,256]{3,2,1,0:T(8,128)(2,1)S(1)} %get-tuple-element.23.right_a, ...), custom_call_target="tpu_custom_call" | custom-call | flops 1610612736 | bytes 3145728 | tf_op jit(solution)/shard_map/early_seconds/pallas_call | solution.py:677
  20.0 1.3 %collective-permute-start.4 = (bf16[2,2,256,256]{3,2,1,0:T(8,128)(2,1)}, bf16[2,2,256,256]{3,2,1,0:T(8,128)(2,1)}, u32[]{:S(2)}, u32[]{:S(2)}) collective-permute-start(bf16[2,2,256,256]{3,2,1,0:T(8,128)(2,1)} %get-tuple-element.33), channel_id=1, source_target_pairs={{8,0},{16,8},{24,16},{9,1},{17,9},{25,17},{10,2},{18,10},{26,18},{... | collective-permute-start | bytes 1572872 | tf_op jit(solution)/shard_map/ppermute | solution.py:596
  21.3 0.0 collective-permute-done.2.shifted
  21.4 0.0 copy-done
  21.4 0.0 copy-done.1
  21.4 0.0 copy-start.3
  21.4 3.4 %late_seconds.1.after = f32[32,128]{1,0:T(8,128)} custom-call(s32[9,25]{1,0:T(8,128)S(1)} %get-tuple-element.21.lists_held, bf16[12,2,256,256]{3,2,1,0:T(8,128)(2,1)S(1)} %get-tuple-element.22.left_a.env, bf16[12,2,256,256]{3,2,1,0:T(8,128)(2,1)S(1)} %get-tuple-element.23.right_a, bf16[12,2,256,256]{3,2,1,0:T(8,128)(2,1)S(1)} %get-tuple-element.24.left_b, ...), custom_call_target="tpu_custom_call" | custom-call | flops 1610612736 | bytes 3145728 | tf_op jit(solution)/shard_map/late_seconds/pallas_call | solution.py:696
  24.8 11.8 %all-to-all-start = ((f32[32,1,128]{2,1,0:T(1,128)}), f32[32,1,128]{2,1,0:T(1,128)S(1)}, u32[]{:S(2)}, u32[]{:S(2)}) async-start(f32[32,1,128]{2,1,0:T(1,128)} %bitcast.8), calls=%async_computation | async-start | bytes 32768 | tf_op jit(solution)/shard_map/all_to_all | solution.py:709
  36.7 0.0 copy-done.3
  36.7 2.6 %mixing.1.mixed_held = bf16[12,2,256,256]{3,2,1,0:T(8,128)(2,1)S(1)} custom-call(f32[12,12]{1,0:T(8,128)S(1)} %copy-done.3, bf16[12,2,256,256]{3,2,1,0:T(8,128)(2,1)S(1)} %get-tuple-element.22.left_a.env, f32[32,128]{1,0:T(8,128)} %late_seconds.1.after), custom_call_target="tpu_custom_call" | custom-call | flops 1207959552 | bytes 6291456 | tf_op jit(solution)/shard_map/mixing/pallas_call | solution.py:710
  39.3 0.0 copy-start.2
  39.3 1.6 %copy-done.2 = bf16[12,2,256,256]{3,2,1,0:T(8,128)(2,1)} copy-done((bf16[12,2,256,256]{3,2,1,0:T(8,128)(2,1)}, bf16[12,2,256,256]{3,2,1,0:T(8,128)(2,1)S(1)}, u32[]{:S(2)}) %copy-start.2) | copy-done | bytes 3145752
  41.0 2.6 %all-to-all-done = f32[32,1,128]{2,1,0:T(1,128)S(1)} async-done(((f32[32,1,128]{2,1,0:T(1,128)}), f32[32,1,128]{2,1,0:T(1,128)S(1)}, u32[]{:S(2)}, u32[]{:S(2)}) %all-to-all-start) | async-done | bytes 16416 | tf_op jit(solution)/shard_map/all_to_all | solution.py:709
  43.6 0.0 collective-permute-done.4.along_held
  43.6 5.5 %finish.1 = (f32[2,256,256]{2,1,0:T(8,128)}, f32[2,256,256]{2,1,0:T(8,128)}, f32[1,2]{1,0:T(1,128)}, bf16[12,2,256,256]{3,2,1,0:T(8,128)(2,1)}) custom-call(f32[32,128]{1,0:T(8,128)S(1)} %bitcast.17, bf16[2,2,256,256]{3,2,1,0:T(8,128)(2,1)} %copy-done, f32[2,2,256,256]{3,2,1,0:T(8,128)} %copy-done.1, ...), custom_call_target="tpu_custom_call" | custom-call | flops 1610612736 | bytes 6291456 | tf_op jit(solution)/shard_map/finish/pallas_call | solution.py:720
Async XLA Ops:
  1.8 19.5 %copy-start = (bf16[2,2,256,256]{3,2,1,0:T(8,128)(2,1)}, bf16[2,2,256,256]{3,2,1,0:T(8,128)(2,1)S(1)}, u32[]{:S(2)}) copy-start(bf16[2,2,256,256]{3,2,1,0:T(8,128)(2,1)S(1)} %masked_starts.1.starts.starts_held) | copy-start | bytes 1572868
  1.8 2.1 %collective-permute-start = (bf16[2,2,256,256]{3,2,1,0:T(8,128)(2,1)S(1)}, bf16[2,2,256,256]{3,2,1,0:T(8,128)(2,1)S(1)}, u32[]{:S(2)}, u32[]{:S(2)}) collective-permute-start(bf16[2,2,256,256]{3,2,1,0:T(8,128)(2,1)S(1)} %masked_starts.1.starts.starts_held), channel_id=1, source_target_pairs={{0,1},{1,0},{2,3},{3,2},{4,5},{5,4},{6,7},{7,6},{8,9},{9,8},{10,11... | collective-permute-start | bytes 1572872 | tf_op jit(solution)/shard_map/ppermute | solution.py:585
  2.4 8.4 %collective-permute-start.1 = (bf16[2,2,256,256]{3,2,1,0:T(8,128)(2,1)S(1)}, bf16[2,2,256,256]{3,2,1,0:T(8,128)(2,1)S(1)}, u32[]{:S(2)}, u32[]{:S(2)}) collective-permute-start(bf16[2,2,256,256]{3,2,1,0:T(8,128)(2,1)S(1)} %masked_starts.1.starts.starts_held), channel_id=1, source_target_pairs={{1,2},{3,4},{5,6},{2,1},{4,3},{6,5},{9,10},{11,12},{13,14},{10,9},... | collective-permute-start | bytes 1572872 | tf_op jit(solution)/shard_map/ppermute | solution.py:591
  13.4 7.9 %copy-start.1 = (f32[2,2,256,256]{3,2,1,0:T(8,128)}, f32[2,2,256,256]{3,2,1,0:T(8,128)S(1)}, u32[]{:S(2)}) copy-start(f32[2,2,256,256]{3,2,1,0:T(8,128)S(1)} %get-tuple-element.28.rest.rest_held) | copy-start | bytes 3145732
  13.5 3.5 %collective-permute-start.3 = (bf16[2,2,256,256]{3,2,1,0:T(8,128)(2,1)S(1)}, bf16[2,2,256,256]{3,2,1,0:T(8,128)(2,1)S(1)}, u32[]{:S(2)}, u32[]{:S(2)}) collective-permute-start(bf16[2,2,256,256]{3,2,1,0:T(8,128)(2,1)S(1)} %get-tuple-element.27.sent), channel_id=1, source_target_pairs={{0,1},{1,0},{2,3},{3,2},{4,5},{5,4},{6,7},{7,6},{8,9},{9,8},{10,11... | collective-permute-start | bytes 1572872 | tf_op jit(solution)/shard_map/ppermute | solution.py:585
  15.4 5.9 %collective-permute-start.2 = (bf16[2,2,256,256]{3,2,1,0:T(8,128)(2,1)S(1)}, bf16[2,2,256,256]{3,2,1,0:T(8,128)(2,1)S(1)}, u32[]{:S(2)}, u32[]{:S(2)}) collective-permute-start(bf16[2,2,256,256]{3,2,1,0:T(8,128)(2,1)S(1)} %get-tuple-element.27.sent), channel_id=1, source_target_pairs={{1,2},{3,4},{5,6},{2,1},{4,3},{6,5},{9,10},{11,12},{13,14},{10,9},... | collective-permute-start | bytes 1572872 | tf_op jit(solution)/shard_map/ppermute | solution.py:591
  20.0 23.5 %collective-permute-start.4 = (bf16[2,2,256,256]{3,2,1,0:T(8,128)(2,1)}, bf16[2,2,256,256]{3,2,1,0:T(8,128)(2,1)}, u32[]{:S(2)}, u32[]{:S(2)}) collective-permute-start(bf16[2,2,256,256]{3,2,1,0:T(8,128)(2,1)} %get-tuple-element.33), channel_id=1, source_target_pairs={{8,0},{16,8},{24,16},{9,1},{17,9},{25,17},{10,2},{18,10},{26,18},{... | collective-permute-start | bytes 1572872 | tf_op jit(solution)/shard_map/ppermute | solution.py:596
  21.4 15.3 %copy-start.3 = (f32[12,12]{1,0:T(8,128)S(1)}, f32[12,12]{1,0:T(8,128)}, u32[]{:S(2)}) copy-start(f32[12,12]{1,0:T(8,128)} %mix.1) | copy-start | bytes 1732
  24.8 18.7 %all-to-all-start = ((f32[32,1,128]{2,1,0:T(1,128)}), f32[32,1,128]{2,1,0:T(1,128)S(1)}, u32[]{:S(2)}, u32[]{:S(2)}) async-start(f32[32,1,128]{2,1,0:T(1,128)} %bitcast.8), calls=%async_computation | async-start | bytes 32768 | tf_op jit(solution)/shard_map/all_to_all | solution.py:709
  39.3 1.6 %copy-start.2 = (bf16[12,2,256,256]{3,2,1,0:T(8,128)(2,1)}, bf16[12,2,256,256]{3,2,1,0:T(8,128)(2,1)S(1)}, u32[]{:S(2)}) copy-start(bf16[12,2,256,256]{3,2,1,0:T(8,128)(2,1)S(1)} %mixing.1.mixed_held) | copy-start | bytes 9437188

commit v7 on v6

--- a/solution.py
+++ b/solution.py
@@ -389,26 +389,57 @@
     early_sums,
     row_in,
     row,
-    sums,
     lists,
     lists_sem,
 ):
     lists_copy = pltpu.make_async_copy(lists_held, lists, lists_sem)
     lists_copy.start()
+    lefts, rights = (left_a, left_b), (right_a, right_b)
     downs = left_a.shape[1]
-    sums[...] = early_sums[...]
+    places = [
+        bond * BOND_LANES + place for bond in range(BONDS) for place in (REST_IMAGE, START_IMAGE)
+    ]
+
+    def with_image(parts, bond, down, image):
+        parts[2 * bond] += folded(rest[bond, down] * image)
+        parts[2 * bond + 1] += folded(starts[bond, down].astype(F32) * image)
+
+    def with_units(indices, parts):
+        parts = list(parts)
+        units = [
+            [lists[LATE + part, index] for part in (CHANNEL, DOWN, SOURCE)] for index in indices
+        ]
+        halves = [
+            [
+                dot(lefts[bond][channel, down], shifted[bond, source]).astype(BF16)
+                for bond in range(BONDS)
+            ]
+            for channel, down, source in units
+        ]
+        for (channel, down, _), half in zip(units, halves):
+            for bond in range(BONDS):
+                image = dot_by_rows(half[bond], rights[bond][channel, down])
+                with_image(parts, bond, down, image)
+        return tuple(parts)
+
+    parts = [jnp.zeros((8, rest.shape[-1]), F32) for _ in places]
+    for bond in range(BONDS):
+        for down in range(downs):
+            with_image(parts, bond, down, early_sums[bond, down])
+    parts = tuple(parts)
     lists_copy.wait()
-    add_units(lists, LATE, (left_a, left_b), (right_a, right_b), shifted, Unparted(sums))
-    places, parts = [], []
-    for bond in range(BONDS):
-        of_rest, of_start = 0.0, 0.0
-        for down in range(downs):
-            image = sums[bond, down]
-            of_rest += folded(rest[bond, down] * image)
-            of_start += folded(starts[bond, down].astype(F32) * image)
-        places += [bond * BOND_LANES + REST_IMAGE, bond * BOND_LANES + START_IMAGE]
-        parts += [of_rest, of_start]
-    found = list(zip(places, totals(parts)))
+    count = lists[LATE, lists.shape[1] - 1]
+    done = jnp.int32(0)
+    for size in (4, 2, 1):
+        steps = lax.div(count - done, size)
+
+        def step(index, parts, size=size, done=done):
+            first = done + size * index
+            return with_units([first + i for i in range(size)], parts)
+
+        parts = lax.fori_loop(0, steps, step, parts)
+        done = done + size * steps
+    found = list(zip(places, totals(list(parts))))
     row[...] = jnp.broadcast_to(row_in[0:1, :] + in_lanes(row.shape[1], found), row.shape)
 
 
@@ -571,7 +602,7 @@
                 halves[channel, down] = half[place * block : (place + 1) * block]
         if index > 0:
             last_product(index - 1)
-        if index == min(1, len(groups) - 1):
+        if index == 0:
             for copy in second:
                 copy.wait()
             ground_of(1, ground_b)
@@ -698,11 +729,7 @@
         "late_seconds",
         [VMEM] * 10,
         [(VMEM, pltpu.VMEM((devices, 128), F32))],
-        [
-            pltpu.VMEM(both, F32),
-            pltpu.SMEM(list_shape, jnp.int32),
-            pltpu.SemaphoreType.DMA(()),
-        ],
+        [pltpu.SMEM(list_shape, jnp.int32), pltpu.SemaphoreType.DMA(())],
         apply_flops,
         env_bytes,
     )(lists, *loaded, shifted, starts, rest, sums, row)

time: 48.6 us -> 46.7 us (0.961)
  Pallas kernels: 25.3 us -> 23.6 us
  starting transfers between devices: 17 us -> 16.3 us
    all_to_all x1, starting transfers between devices: 11.8 us -> 9.24 us  [local(): numbers = lax.all_to_all(row, ('seg', 'blk'), 0, 0, tiled=True)]
    ppermute x2, starting transfers between devices: 2.49 us -> 4.44 us  [swapped_pairs(): lax.ppermute(block, 'blk', [(i, i ^ 1) for i in devices if i ^ 1 in devic...]
    pallas_call x1, Pallas kernels: 3.45 us -> 2.15 us  [local(): call(late_seconds, 'late_seconds', [VMEM] * 10, [(VMEM, pltpu.VMEM((devic...]
    pallas_call x1, Pallas kernels: 2.71 us -> 1.53 us  [local(): call(first_images, 'first_images', [VMEM, HBM] + [VMEM] * 6, [(VMEM, pltp...]
    pallas_call x1, Pallas kernels: 3.06 us -> 4.12 us  [local(): call(early_seconds, 'early_seconds', [VMEM] * 11, [(VMEM, tile), (VMEM, p...]
  transfers between devices with their start and end apart: 6 -> 6, of which waited for: 3 -> 3; matrix products, arithmetic and copies ran while one was open for 0% -> 0% of each run, Pallas kernels for 32% -> 33%
where the time goes in v7:
time: 46.7 us; the launch traced here: 46.8 us
  Pallas kernels  23.6 us (51%)
  starting transfers between devices  16.3 us (35%)
  waiting for transfers between devices  4.3 us (9%)
  local copies, waits for them, and re-layouts  1.64 us (4%)
  between operations  0.94 us (2%)
    all_to_all x1, starting transfers between devices, local(): numbers = lax.all_to_all(row, ('seg', 'blk'), 0, 0, tiled=True)  9.24 us
    pallas_call x1, Pallas kernels, local(): call(opening, 'opening', [HBM, VMEM, VMEM] + [HBM] * 4, [(VMEM, pltpu.VME...  6.52 us
    pallas_call x1, Pallas kernels, local(): call(functools.partial(finish, 1.0 / block, ups), 'finish', [VMEM] + [HBM...  5.48 us
    ppermute x2, starting transfers between devices, swapped_pairs(): lax.ppermute(block, 'blk', [(i, i ^ 1) for i in devices if i ^ 1 in devic...  4.44 us
    pallas_call x1, Pallas kernels, local(): call(early_seconds, 'early_seconds', [VMEM] * 11, [(VMEM, tile), (VMEM, p...  4.12 us
    pallas_call x1, Pallas kernels, local(): call(mixing, 'mixing', [VMEM, VMEM, HBM], [(VMEM, jax.ShapeDtypeStruct(en...  2.64 us
    all_to_all x1, waiting for transfers between devices, local(): numbers = lax.all_to_all(row, ('seg', 'blk'), 0, 0, tiled=True)  2.6 us
    pallas_call x1, Pallas kernels, local(): call(late_seconds, 'late_seconds', [VMEM] * 10, [(VMEM, pltpu.VMEM((devic...  2.15 us
  transfers between devices with their start and end apart: 6, of which 3 were waited for; matrix products, arithmetic and copies ran while one was open for 0% of the time, Pallas kernels for 33%

profile of v7, /device:TPU:0, one launch (start us, length us, event | category | flops | bytes accessed | tf_op | source)
XLA Modules:
  0.0 46.8 jit_solution(12453149194575947607)
XLA Ops:
  0.6 1.2 %masked_starts.1.starts.starts_held = bf16[2,2,256,256]{3,2,1,0:T(8,128)(2,1)S(1)} custom-call(s32[1,1,2,4]{3,2,1,0:T(2,128)} %bitcast.24, bf16[2,256,256]{2,1,0:T(8,128)(2,1)} %bitcast.22, bf16[2,256,256]{2,1,0:T(8,128)(2,1)} %bitcast.23), custom_call_target="tpu_custom_call" | custom-call | flops 524288 | bytes 1048576 | tf_op jit(solution)/shard_map/masked_starts/pallas_call | solution.py:657
  1.8 0.0 copy-start
  1.8 0.5 %collective-permute-start = (bf16[2,2,256,256]{3,2,1,0:T(8,128)(2,1)S(1)}, bf16[2,2,256,256]{3,2,1,0:T(8,128)(2,1)S(1)}, u32[]{:S(2)}, u32[]{:S(2)}) collective-permute-start(bf16[2,2,256,256]{3,2,1,0:T(8,128)(2,1)S(1)} %masked_starts.1.starts.starts_held), channel_id=1, source_target_pairs={{0,1},{1,0},{2,3},{3,2},{4,5},{5,4},{6,7},{7,6},{8,9},{9,8},{10,11... | collective-permute-start | bytes 1572872 | tf_op jit(solution)/shard_map/ppermute | solution.py:616
  2.4 0.7 %collective-permute-start.1 = (bf16[2,2,256,256]{3,2,1,0:T(8,128)(2,1)S(1)}, bf16[2,2,256,256]{3,2,1,0:T(8,128)(2,1)S(1)}, u32[]{:S(2)}, u32[]{:S(2)}) collective-permute-start(bf16[2,2,256,256]{3,2,1,0:T(8,128)(2,1)S(1)} %masked_starts.1.starts.starts_held), channel_id=1, source_target_pairs={{1,2},{3,4},{5,6},{2,1},{4,3},{6,5},{9,10},{11,12},{13,14},{10,9},... | collective-permute-start | bytes 1572872 | tf_op jit(solution)/shard_map/ppermute | solution.py:622
  3.0 0.8 %collective-permute-done.swapped = bf16[2,2,256,256]{3,2,1,0:T(8,128)(2,1)S(1)} collective-permute-done((bf16[2,2,256,256]{3,2,1,0:T(8,128)(2,1)S(1)}, bf16[2,2,256,256]{3,2,1,0:T(8,128)(2,1)S(1)}, u32[]{:S(2)}, u32[]{:S(2)}) %collective-permute-start) | collective-permute-done | bytes 524320 | tf_op jit(solution)/shard_map/ppermute | solution.py:616
  3.9 6.5 %opening.1 = (bf16[12,2,256,256]{3,2,1,0:T(8,128)(2,1)S(1)}, bf16[12,2,256,256]{3,2,1,0:T(8,128)(2,1)S(1)}, bf16[12,2,256,256]{3,2,1,0:T(8,128)(2,1)S(1)}, bf16[...) custom-call(s32[12]{0:T(128)} %shift_held.1, ...), custom_call_target="tpu_custom_call" | custom-call | flops 1610612736 | bytes 15728640 | tf_op jit(solution)/shard_map/opening/pallas_call | solution.py:670
  10.4 0.0 collective-permute-done.1.shifted
  10.4 1.5 %first_images.1 = (f32[2,2,256,256]{3,2,1,0:T(8,128)S(1)}, bf16[2,2,256,256]{3,2,1,0:T(8,128)(2,1)S(1)}) custom-call(s32[9,25]{1,0:T(8,128)S(1)} %get-tuple-element.21.lists_held, s32[1,1,2,4]{3,2,1,0:T(2,128)} %bitcast.25, bf16[12,2,256,256]{3,2,1,0:T(8,128)(2,1)S(1)} %get-tuple-element.22.left_a.env, ...), custom_call_target="tpu_custom_call" | custom-call | flops 1610612736 | bytes 3145728 | tf_op jit(solution)/shard_map/first_images/pallas_call | solution.py:691
  12.0 0.0 copy-start.1
  12.0 3.9 %collective-permute-start.3 = (bf16[2,2,256,256]{3,2,1,0:T(8,128)(2,1)S(1)}, bf16[2,2,256,256]{3,2,1,0:T(8,128)(2,1)S(1)}, u32[]{:S(2)}, u32[]{:S(2)}) collective-permute-start(bf16[2,2,256,256]{3,2,1,0:T(8,128)(2,1)S(1)} %get-tuple-element.27.sent), channel_id=1, source_target_pairs={{0,1},{1,0},{2,3},{3,2},{4,5},{5,4},{6,7},{7,6},{8,9},{9,8},{10,11... | collective-permute-start | bytes 1572872 | tf_op jit(solution)/shard_map/ppermute | solution.py:616
  15.9 0.7 %collective-permute-start.2 = (bf16[2,2,256,256]{3,2,1,0:T(8,128)(2,1)S(1)}, bf16[2,2,256,256]{3,2,1,0:T(8,128)(2,1)S(1)}, u32[]{:S(2)}, u32[]{:S(2)}) collective-permute-start(bf16[2,2,256,256]{3,2,1,0:T(8,128)(2,1)S(1)} %get-tuple-element.27.sent), channel_id=1, source_target_pairs={{1,2},{3,4},{5,6},{2,1},{4,3},{6,5},{9,10},{11,12},{13,14},{10,9},... | collective-permute-start | bytes 1572872 | tf_op jit(solution)/shard_map/ppermute | solution.py:622
  16.6 0.8 %collective-permute-done.3.swapped = bf16[2,2,256,256]{3,2,1,0:T(8,128)(2,1)S(1)} collective-permute-done((bf16[2,2,256,256]{3,2,1,0:T(8,128)(2,1)S(1)}, bf16[2,2,256,256]{3,2,1,0:T(8,128)(2,1)S(1)}, u32[]{:S(2)}, u32[]{:S(2)}) %collective-permute-start.3) | collective-permute-done | bytes 524320 | tf_op jit(solution)/shard_map/ppermute | solution.py:616
  17.4 4.1 %early_seconds.1 = (f32[8,128]{1,0:T(8,128)S(1)}, f32[2,2,256,256]{3,2,1,0:T(8,128)S(1)}, bf16[2,2,256,256]{3,2,1,0:T(8,128)(2,1)}) custom-call(s32[9,25]{1,0:T(8,128)S(1)} %get-tuple-element.21.lists_held, bf16[12,2,256,256]{3,2,1,0:T(8,128)(2,1)S(1)} %get-tuple-element.22.left_a.env, bf16[12,2,256,256]{3,2,1,0:T(8,128)(2,1)S(1)} %get-tuple-element.23.right_a, ...), custom_call_target="tpu_custom_call" | custom-call | flops 1610612736 | bytes 3145728 | tf_op jit(solution)/shard_map/early_seconds/pallas_call | solution.py:708
  21.6 1.3 %collective-permute-start.4 = (bf16[2,2,256,256]{3,2,1,0:T(8,128)(2,1)}, bf16[2,2,256,256]{3,2,1,0:T(8,128)(2,1)}, u32[]{:S(2)}, u32[]{:S(2)}) collective-permute-start(bf16[2,2,256,256]{3,2,1,0:T(8,128)(2,1)} %get-tuple-element.33), channel_id=1, source_target_pairs={{8,0},{16,8},{24,16},{9,1},{17,9},{25,17},{10,2},{18,10},{26,18},{... | collective-permute-start | bytes 1572872 | tf_op jit(solution)/shard_map/ppermute | solution.py:627
  22.9 0.0 collective-permute-done.2.shifted
  22.9 0.0 copy-done
  22.9 0.0 copy-done.1
  22.9 0.0 copy-start.3
  22.9 2.2 %late_seconds.1.after = f32[32,128]{1,0:T(8,128)} custom-call(s32[9,25]{1,0:T(8,128)S(1)} %get-tuple-element.21.lists_held, bf16[12,2,256,256]{3,2,1,0:T(8,128)(2,1)S(1)} %get-tuple-element.22.left_a.env, bf16[12,2,256,256]{3,2,1,0:T(8,128)(2,1)S(1)} %get-tuple-element.23.right_a, bf16[12,2,256,256]{3,2,1,0:T(8,128)(2,1)S(1)} %get-tuple-element.24.left_b, ...), custom_call_target="tpu_custom_call" | custom-call | flops 1610612736 | bytes 3145728 | tf_op jit(solution)/shard_map/late_seconds/pallas_call | solution.py:727
  25.1 9.2 %all-to-all-start = ((f32[32,1,128]{2,1,0:T(1,128)}), f32[32,1,128]{2,1,0:T(1,128)S(1)}, u32[]{:S(2)}, u32[]{:S(2)}) async-start(f32[32,1,128]{2,1,0:T(1,128)} %bitcast.8), calls=%async_computation | async-start | bytes 32768 | tf_op jit(solution)/shard_map/all_to_all | solution.py:736
  34.3 0.0 copy-done.3
  34.3 2.6 %mixing.1.mixed_held = bf16[12,2,256,256]{3,2,1,0:T(8,128)(2,1)S(1)} custom-call(f32[12,12]{1,0:T(8,128)S(1)} %copy-done.3, bf16[12,2,256,256]{3,2,1,0:T(8,128)(2,1)S(1)} %get-tuple-element.22.left_a.env, f32[32,128]{1,0:T(8,128)} %late_seconds.1.after), custom_call_target="tpu_custom_call" | custom-call | flops 1207959552 | bytes 6291456 | tf_op jit(solution)/shard_map/mixing/pallas_call | solution.py:737
  37.0 0.0 copy-start.2
  37.0 1.6 %copy-done.2 = bf16[12,2,256,256]{3,2,1,0:T(8,128)(2,1)} copy-done((bf16[12,2,256,256]{3,2,1,0:T(8,128)(2,1)}, bf16[12,2,256,256]{3,2,1,0:T(8,128)(2,1)S(1)}, u32[]{:S(2)}) %copy-start.2) | copy-done | bytes 3145752
  38.6 2.6 %all-to-all-done = f32[32,1,128]{2,1,0:T(1,128)S(1)} async-done(((f32[32,1,128]{2,1,0:T(1,128)}), f32[32,1,128]{2,1,0:T(1,128)S(1)}, u32[]{:S(2)}, u32[]{:S(2)}) %all-to-all-start) | async-done | bytes 16416 | tf_op jit(solution)/shard_map/all_to_all | solution.py:736
  41.2 0.0 collective-permute-done.4.along_held
  41.2 5.5 %finish.1 = (f32[2,256,256]{2,1,0:T(8,128)}, f32[2,256,256]{2,1,0:T(8,128)}, f32[1,2]{1,0:T(1,128)}, bf16[12,2,256,256]{3,2,1,0:T(8,128)(2,1)}) custom-call(f32[32,128]{1,0:T(8,128)S(1)} %bitcast.17, bf16[2,2,256,256]{3,2,1,0:T(8,128)(2,1)} %copy-done, f32[2,2,256,256]{3,2,1,0:T(8,128)} %copy-done.1, ...), custom_call_target="tpu_custom_call" | custom-call | flops 1610612736 | bytes 6291456 | tf_op jit(solution)/shard_map/finish/pallas_call | solution.py:747
Async XLA Ops:
  1.8 21.0 %copy-start = (bf16[2,2,256,256]{3,2,1,0:T(8,128)(2,1)}, bf16[2,2,256,256]{3,2,1,0:T(8,128)(2,1)S(1)}, u32[]{:S(2)}) copy-start(bf16[2,2,256,256]{3,2,1,0:T(8,128)(2,1)S(1)} %masked_starts.1.starts.starts_held) | copy-start | bytes 1572868
  1.8 2.1 %collective-permute-start = (bf16[2,2,256,256]{3,2,1,0:T(8,128)(2,1)S(1)}, bf16[2,2,256,256]{3,2,1,0:T(8,128)(2,1)S(1)}, u32[]{:S(2)}, u32[]{:S(2)}) collective-permute-start(bf16[2,2,256,256]{3,2,1,0:T(8,128)(2,1)S(1)} %masked_starts.1.starts.starts_held), channel_id=1, source_target_pairs={{0,1},{1,0},{2,3},{3,2},{4,5},{5,4},{6,7},{7,6},{8,9},{9,8},{10,11... | collective-permute-start | bytes 1572872 | tf_op jit(solution)/shard_map/ppermute | solution.py:616
  2.4 8.1 %collective-permute-start.1 = (bf16[2,2,256,256]{3,2,1,0:T(8,128)(2,1)S(1)}, bf16[2,2,256,256]{3,2,1,0:T(8,128)(2,1)S(1)}, u32[]{:S(2)}, u32[]{:S(2)}) collective-permute-start(bf16[2,2,256,256]{3,2,1,0:T(8,128)(2,1)S(1)} %masked_starts.1.starts.starts_held), channel_id=1, source_target_pairs={{1,2},{3,4},{5,6},{2,1},{4,3},{6,5},{9,10},{11,12},{13,14},{10,9},... | collective-permute-start | bytes 1572872 | tf_op jit(solution)/shard_map/ppermute | solution.py:622
  12.0 10.9 %copy-start.1 = (f32[2,2,256,256]{3,2,1,0:T(8,128)}, f32[2,2,256,256]{3,2,1,0:T(8,128)S(1)}, u32[]{:S(2)}) copy-start(f32[2,2,256,256]{3,2,1,0:T(8,128)S(1)} %get-tuple-element.28.rest.rest_held) | copy-start | bytes 3145732
  12.0 5.5 %collective-permute-start.3 = (bf16[2,2,256,256]{3,2,1,0:T(8,128)(2,1)S(1)}, bf16[2,2,256,256]{3,2,1,0:T(8,128)(2,1)S(1)}, u32[]{:S(2)}, u32[]{:S(2)}) collective-permute-start(bf16[2,2,256,256]{3,2,1,0:T(8,128)(2,1)S(1)} %get-tuple-element.27.sent), channel_id=1, source_target_pairs={{0,1},{1,0},{2,3},{3,2},{4,5},{5,4},{6,7},{7,6},{8,9},{9,8},{10,11... | collective-permute-start | bytes 1572872 | tf_op jit(solution)/shard_map/ppermute | solution.py:616
  15.9 7.0 %collective-permute-start.2 = (bf16[2,2,256,256]{3,2,1,0:T(8,128)(2,1)S(1)}, bf16[2,2,256,256]{3,2,1,0:T(8,128)(2,1)S(1)}, u32[]{:S(2)}, u32[]{:S(2)}) collective-permute-start(bf16[2,2,256,256]{3,2,1,0:T(8,128)(2,1)S(1)} %get-tuple-element.27.sent), channel_id=1, source_target_pairs={{1,2},{3,4},{5,6},{2,1},{4,3},{6,5},{9,10},{11,12},{13,14},{10,9},... | collective-permute-start | bytes 1572872 | tf_op jit(solution)/shard_map/ppermute | solution.py:622
  21.6 19.6 %collective-permute-start.4 = (bf16[2,2,256,256]{3,2,1,0:T(8,128)(2,1)}, bf16[2,2,256,256]{3,2,1,0:T(8,128)(2,1)}, u32[]{:S(2)}, u32[]{:S(2)}) collective-permute-start(bf16[2,2,256,256]{3,2,1,0:T(8,128)(2,1)} %get-tuple-element.33), channel_id=1, source_target_pairs={{8,0},{16,8},{24,16},{9,1},{17,9},{25,17},{10,2},{18,10},{26,18},{... | collective-permute-start | bytes 1572872 | tf_op jit(solution)/shard_map/ppermute | solution.py:627
  22.9 11.4 %copy-start.3 = (f32[12,12]{1,0:T(8,128)S(1)}, f32[12,12]{1,0:T(8,128)}, u32[]{:S(2)}) copy-start(f32[12,12]{1,0:T(8,128)} %mix.1) | copy-start | bytes 1732
  25.1 16.1 %all-to-all-start = ((f32[32,1,128]{2,1,0:T(1,128)}), f32[32,1,128]{2,1,0:T(1,128)S(1)}, u32[]{:S(2)}, u32[]{:S(2)}) async-start(f32[32,1,128]{2,1,0:T(1,128)} %bitcast.8), calls=%async_computation | async-start | bytes 32768 | tf_op jit(solution)/shard_map/all_to_all | solution.py:736
  37.0 1.6 %copy-start.2 = (bf16[12,2,256,256]{3,2,1,0:T(8,128)(2,1)}, bf16[12,2,256,256]{3,2,1,0:T(8,128)(2,1)S(1)}, u32[]{:S(2)}) copy-start(bf16[12,2,256,256]{3,2,1,0:T(8,128)(2,1)S(1)} %mixing.1.mixed_held) | copy-start | bytes 9437188
